TPU v7x, 32 devices: a whole 2x2x4 slice. The times are simulated.
32 devices in a mesh: wide: 8 (over z, y), narrow: 4 (over x, core).
Axes of the slice: x: 2, y: 2, z: 4, core: 2. Of those that a mesh axis runs over, the one named last changes fastest.
Arguments:
- tokens: bfloat16 [16384, 768], P(('wide', 'narrow')), may hold values from -6 to 6
- skip_tokens: bfloat16 [16384, 768], P(('wide', 'narrow')), may hold values from -6 to 6
- cot_first: bfloat16 [16384, 768], P(('wide', 'narrow')), may hold values from -6 to 6
- cot_second: bfloat16 [16384, 768], P(('wide', 'narrow')), may hold values from -6 to 6
- w_qkv: bfloat16 [2, 768, 2304], P(None, None, ('wide', 'narrow')), may hold values from -0.21875 to 0.21875
- w_out: bfloat16 [2, 768, 768], P(None, None, ('wide', 'narrow')), may hold values from -1.75 to 1.75
- w_up: bfloat16 [2, 768, 3072], P(None, None, ('wide', 'narrow')), may hold values from -0.21875 to 0.21875
- w_down: bfloat16 [2, 3072, 768], P(None, ('wide', 'narrow')), may hold values from -0.109375 to 0.109375
- biases: bfloat16 [2, 6, 768], P(None, None, ('wide', 'narrow')), may hold values from -0.59765625 to 0.59765625
- norm_gains: bfloat16 [2, 2, 768], P(None, None, ('wide', 'narrow')), may hold values from 0.5 to 1.5
- up_bias: bfloat16 [2, 3072], P(None, ('wide', 'narrow')), may hold values from -0.59765625 to 0.59765625
- lengths: int32 [32], P(('wide', 'narrow')), may hold values from 409 to 512
- segments: int32 [32, 512], P(('wide', 'narrow')), may hold values from 0 to 7, never falling along the last dimension, each value on 1 to 128 neighbouring positions
Outputs:
- out_first: bfloat16 [16384, 768], P(('wide', 'narrow'))
- out_second: bfloat16 [16384, 768], P(('wide', 'narrow'))
- grad_tokens: float32 [16384, 768], P(('wide', 'narrow'))
- grad_skip: float32 [16384, 768], P(('wide', 'narrow'))
- grad_w_qkv: float32 [2, 768, 2304], P(None, None, ('wide', 'narrow'))
- grad_w_out: float32 [2, 768, 768], P(None, None, ('wide', 'narrow'))
- grad_w_up: float32 [2, 768, 3072], P(None, None, ('wide', 'narrow'))
- grad_w_down: float32 [2, 3072, 768], P(None, ('wide', 'narrow'))
- grad_biases: float32 [2, 6, 768], P(None, None, ('wide', 'narrow'))
- grad_gains: float32 [2, 2, 768], P(None, None, ('wide', 'narrow'))
- grad_up_bias: float32 [2, 3072], P(None, ('wide', 'narrow'))
All inputs are finite; a program needn't handle non-finite values.
Results may differ from a plain program's by a relative error of at most 0.017.
Values may be sent and summed in bfloat16 or wider, within the bound.
No kernel may reach another device: no remote copies, remote signals or barrier semaphores. Data moves between devices by JAX's collectives and lax.ppermute only.
A program may use at most 256 MiB of HBM per device.

v0:
```python
import math

import jax
import jax.numpy as jnp
from jax import lax
from jax.sharding import PartitionSpec as P

HEADS = 12
HEAD_DIM = 64


EPSILON = 1e-12
MASKED = -1e30


def shortened(shard):
    return jax.tree.map(lambda a: a.astype(jnp.bfloat16) if a.dtype == jnp.float32 else a, shard)


def normalize(values, norm_gain, norm_shift):
    average = jnp.mean(values, -1, keepdims=True)
    centred = values - average
    inverse = lax.rsqrt(jnp.mean(centred * centred, -1, keepdims=True) + EPSILON)
    scaled = centred * inverse
    return (scaled * norm_gain + norm_shift, scaled, inverse)


def normalize_back(upstream, scaled, inverse, norm_gain):
    d_gain = jnp.sum(upstream * scaled, 0)
    d_shift = jnp.sum(upstream, 0)
    through = upstream * norm_gain
    d_values = inverse * (
        through
        - jnp.mean(through, -1, keepdims=True)
        - scaled * jnp.mean(through * scaled, -1, keepdims=True)
    )
    return (d_values, d_gain, d_shift)


def allowed(lengths, segments):
    position = lax.broadcasted_iota(jnp.int32, segments.shape, 1)
    living = position < lengths[:, None]
    same_doc = segments[:, :, None] == segments[:, None, :]
    itself = position[:, :, None] == position[:, None, :]
    return same_doc & living[:, None, :] | itself


def score_block(queries, keys_in, allow_one):
    temper = HEAD_DIM ** (-0.5)
    scores = (
        jnp.einsum("qhe,khe->hqk", queries, keys_in, preferred_element_type=jnp.float32) * temper
    )
    return jnp.where(allow_one[None], scores, MASKED)


def attend_forward(inputs_one):
    queries, keys_in, values_in, allow_one = inputs_one
    scores = score_block(queries, keys_in, allow_one)
    highest = jnp.max(scores, -1, keepdims=True)
    weights_raw = jnp.exp(scores - highest)
    totals = jnp.sum(weights_raw, -1, keepdims=True)
    probs_low = (weights_raw / totals).astype(jnp.bfloat16)
    mixed_heads = jnp.einsum(
        "hqk,khe->qhe", probs_low, values_in, preferred_element_type=jnp.float32
    )
    return (mixed_heads.astype(jnp.bfloat16), highest + jnp.log(totals))


def attend_back(inputs_one):
    queries, keys_in, values_in, allow_one, log_total, d_mixed = inputs_one
    temper = HEAD_DIM ** (-0.5)
    probs_full = jnp.exp(score_block(queries, keys_in, allow_one) - log_total)
    d_probs = jnp.einsum("qhe,khe->hqk", d_mixed, values_in, preferred_element_type=jnp.float32)
    d_values = jnp.einsum(
        "hqk,qhe->khe", probs_full.astype(jnp.bfloat16), d_mixed, preferred_element_type=jnp.float32
    )
    d_scores = (probs_full * (d_probs - jnp.sum(probs_full * d_probs, -1, keepdims=True))).astype(
        jnp.bfloat16
    )
    d_queries = (
        jnp.einsum("hqk,khe->qhe", d_scores, keys_in, preferred_element_type=jnp.float32) * temper
    )
    d_keys = (
        jnp.einsum("hqk,qhe->khe", d_scores, queries, preferred_element_type=jnp.float32) * temper
    )
    return (d_queries, d_keys, d_values)


def block_forward(hidden, weights, allowed_mask):
    w_qkv, w_out, w_up, w_down, biases, norm_gains, up_bias = weights
    bias_rows = biases.astype(jnp.float32)
    gain_rows = norm_gains.astype(jnp.float32)
    seq_count = allowed_mask.shape[0]
    length = allowed_mask.shape[1]
    model_width = w_out.shape[0]
    no_bias = jnp.zeros((model_width,), jnp.float32)
    qkv_bias = jnp.concatenate([bias_rows[0], no_bias, bias_rows[1]])
    projected = (jnp.dot(hidden, w_qkv, preferred_element_type=jnp.float32) + qkv_bias).astype(
        jnp.bfloat16
    )
    split_heads = projected.reshape(seq_count, length, 3, HEADS, HEAD_DIM)
    queries = split_heads[:, :, 0]
    keys_in = split_heads[:, :, 1]
    values_in = split_heads[:, :, 2]
    mixed_heads, log_total = lax.map(attend_forward, (queries, keys_in, values_in, allowed_mask))
    mixed_heads = mixed_heads.reshape(seq_count * length, model_width)
    branch = jnp.dot(mixed_heads, w_out, preferred_element_type=jnp.float32) + bias_rows[2]
    first_norm, scaled_one, inverse_one = normalize(
        hidden.astype(jnp.float32) + branch, gain_rows[0], bias_rows[4]
    )
    first_norm = first_norm.astype(jnp.bfloat16)
    upper_in = jnp.dot(first_norm, w_up, preferred_element_type=jnp.float32) + up_bias.astype(
        jnp.float32
    )
    active = jax.nn.gelu(upper_in, approximate=False).astype(jnp.bfloat16)
    lower_out = jnp.dot(active, w_down, preferred_element_type=jnp.float32) + bias_rows[3]
    result, scaled_two, inverse_two = normalize(
        first_norm.astype(jnp.float32) + lower_out, gain_rows[1], bias_rows[5]
    )
    stored = (
        queries,
        keys_in,
        values_in,
        log_total,
        mixed_heads,
        first_norm,
        scaled_one,
        inverse_one,
        upper_in,
        active,
        scaled_two,
        inverse_two,
    )
    return (result.astype(jnp.bfloat16), stored)


def block_backward(hidden, weights, stored, allowed_mask, upstream):
    w_qkv, w_out, w_up, w_down, biases, norm_gains, up_bias = weights
    gain_rows = norm_gains.astype(jnp.float32)
    (
        queries,
        keys_in,
        values_in,
        log_total,
        mixed_heads,
        first_norm,
        scaled_one,
        inverse_one,
        upper_in,
        active,
        scaled_two,
        inverse_two,
    ) = stored
    seq_count = allowed_mask.shape[0]
    length = allowed_mask.shape[1]
    model_width = w_out.shape[0]
    d_second, d_gain_two, d_shift_two = normalize_back(
        upstream, scaled_two, inverse_two, gain_rows[1]
    )
    d_lower = d_second.astype(jnp.bfloat16)
    d_active = jnp.einsum("rd,fd->rf", d_lower, w_down, preferred_element_type=jnp.float32)
    density = jnp.exp(-0.5 * upper_in * upper_in) * (1.0 / math.sqrt(2.0 * math.pi))
    cumulative = 0.5 * (1.0 + lax.erf(upper_in * (1.0 / math.sqrt(2.0))))
    d_upper = (d_active * (cumulative + upper_in * density)).astype(jnp.bfloat16)
    d_first = d_second + jnp.einsum("rf,df->rd", d_upper, w_up, preferred_element_type=jnp.float32)
    d_pre, d_gain_one, d_shift_one = normalize_back(d_first, scaled_one, inverse_one, gain_rows[0])
    d_branch = d_pre.astype(jnp.bfloat16)
    d_mixed = jnp.einsum("re,de->rd", d_branch, w_out, preferred_element_type=jnp.float32).astype(
        jnp.bfloat16
    )
    d_mixed = d_mixed.reshape(seq_count, length, HEADS, HEAD_DIM)
    d_queries, d_keys, d_values = lax.map(
        attend_back, (queries, keys_in, values_in, allowed_mask, log_total, d_mixed)
    )
    d_project = (
        jnp.stack([d_queries, d_keys, d_values], 2)
        .reshape(seq_count * length, 3 * model_width)
        .astype(jnp.bfloat16)
    )
    d_hidden = d_pre + jnp.einsum("rc,dc->rd", d_project, w_qkv, preferred_element_type=jnp.float32)
    column_sums = jnp.sum(d_project, 0, dtype=jnp.float32)
    g_biases = jnp.stack(
        [
            column_sums[:model_width],
            column_sums[2 * model_width :],
            jnp.sum(d_branch, 0, dtype=jnp.float32),
            jnp.sum(d_lower, 0, dtype=jnp.float32),
            d_shift_one,
            d_shift_two,
        ]
    )
    g_gains = jnp.stack([d_gain_one, d_gain_two])
    g_upbias = jnp.sum(d_upper, 0, dtype=jnp.float32)
    left_rows = (hidden, mixed_heads, first_norm, d_lower)
    right_rows = (d_project, d_branch, d_upper, active)
    return (d_hidden, left_rows, right_rows, (g_biases, g_gains, g_upbias))


def group_terms(left_rows, right_rows):
    wide_count = lax.axis_size("wide")
    narrow_count = lax.axis_size("narrow")
    gathered = (
        lax.all_gather(left_rows[0], "narrow", axis=0, tiled=True),
        lax.all_gather(left_rows[1], "narrow", axis=0, tiled=True),
        lax.all_gather(left_rows[2], "narrow", axis=0, tiled=True),
        lax.all_gather(left_rows[3], "narrow", axis=0, tiled=True),
    )

    def owned_columns(matrix):
        return matrix.reshape(
            matrix.shape[0],
            wide_count,
            narrow_count,
            matrix.shape[1] // (wide_count * narrow_count),
        )

    exchanged = lax.all_to_all(
        shortened(tuple((owned_columns(matrix) for matrix in right_rows))),
        "narrow",
        split_axis=2,
        concat_axis=0,
        tiled=True,
    )
    hidden_all, mixed_all, norm_all, lower_all = gathered
    project_mine, branch_mine, upper_mine, active_mine = (piece[:, :, 0] for piece in exchanged)
    g_qkv = jnp.einsum("ra,rwc->awc", hidden_all, project_mine, preferred_element_type=jnp.float32)
    g_out = jnp.einsum("ra,rwc->awc", mixed_all, branch_mine, preferred_element_type=jnp.float32)
    g_up = jnp.einsum("ra,rwc->awc", norm_all, upper_mine, preferred_element_type=jnp.float32)
    g_down = jnp.einsum("rwc,ra->wca", active_mine, lower_all, preferred_element_type=jnp.float32)
    return (g_qkv, g_out, g_up, g_down)


def finish_terms(summed, lead):
    g_qkv, g_out, g_up, g_down = summed
    rows_model = g_qkv.shape[lead]
    cols_model = g_down.shape[-1]
    return (
        g_qkv.reshape(rows_model, -1),
        g_out.reshape(rows_model, -1),
        g_up.reshape(rows_model, -1),
        g_down.reshape(-1, cols_model),
    )


def reduce_block(terms, small):
    summed = (
        lax.psum_scatter(
            terms[0].astype(jnp.bfloat16), "wide", scatter_dimension=1, tiled=True
        ).astype(jnp.float32),
        lax.psum_scatter(
            terms[1].astype(jnp.bfloat16), "wide", scatter_dimension=1, tiled=True
        ).astype(jnp.float32),
        lax.psum_scatter(
            terms[2].astype(jnp.bfloat16), "wide", scatter_dimension=1, tiled=True
        ).astype(jnp.float32),
        lax.psum_scatter(
            terms[3].astype(jnp.bfloat16), "wide", scatter_dimension=0, tiled=True
        ).astype(jnp.float32),
    )
    small_summed = (
        lax.psum_scatter(small[0], ("wide", "narrow"), scatter_dimension=1, tiled=True),
        lax.psum_scatter(small[1], ("wide", "narrow"), scatter_dimension=1, tiled=True),
        lax.psum_scatter(small[2], ("wide", "narrow"), scatter_dimension=0, tiled=True),
    )
    return finish_terms(summed, 0) + small_summed


def fetch_forward(shards, index):
    qkv_part, out_part, up_part, down_part, bias_part, gain_part, upb_part = shards
    return (
        lax.all_gather(qkv_part[index], ("wide", "narrow"), axis=1, tiled=True),
        lax.all_gather(out_part[index], ("wide", "narrow"), axis=1, tiled=True),
        lax.all_gather(up_part[index], ("wide", "narrow"), axis=1, tiled=True),
        lax.all_gather(down_part[index], ("wide", "narrow"), axis=0, tiled=True),
        lax.all_gather(bias_part[index], ("wide", "narrow"), axis=1, tiled=True),
        lax.all_gather(gain_part[index], ("wide", "narrow"), axis=1, tiled=True),
        lax.all_gather(upb_part[index], ("wide", "narrow"), axis=0, tiled=True),
    )


def fetch_backward(shards, index):
    qkv_part, out_part, up_part, down_part, bias_part, gain_part, upb_part = shards
    return (
        lax.all_gather(qkv_part[index], ("wide", "narrow"), axis=1, tiled=True),
        lax.all_gather(out_part[index], ("wide", "narrow"), axis=1, tiled=True),
        lax.all_gather(up_part[index], ("wide", "narrow"), axis=1, tiled=True),
        lax.all_gather(down_part[index], ("wide", "narrow"), axis=0, tiled=True),
        lax.all_gather(bias_part[index], ("wide", "narrow"), axis=1, tiled=True),
        lax.all_gather(gain_part[index], ("wide", "narrow"), axis=1, tiled=True),
        lax.all_gather(upb_part[index], ("wide", "narrow"), axis=0, tiled=True),
    )


def body(
    tokens,
    skip_tokens,
    cot_first,
    cot_second,
    w_qkv,
    w_out,
    w_up,
    w_down,
    biases,
    norm_gains,
    up_bias,
    lengths,
    segments,
):
    shards = (w_qkv, w_out, w_up, w_down, biases, norm_gains, up_bias)
    allowed_mask = allowed(lengths, segments)
    seq_count = segments.shape[0]
    length = segments.shape[1]
    is_first = (lax.broadcasted_iota(jnp.int32, (seq_count, length, 1), 1) == 0).reshape(
        seq_count * length, 1
    )
    weights_one = fetch_forward(shards, 0)
    out_first, stored_one = block_forward(tokens, weights_one, allowed_mask)
    second_in = jnp.where(is_first, out_first, skip_tokens)
    weights_two = fetch_forward(shards, 1)
    out_second, stored_two = block_forward(second_in, weights_two, allowed_mask)
    back_two = fetch_backward(shards, 1)
    ignored_two, stored_two = block_forward(second_in, back_two, allowed_mask)
    d_second_in, left_two, right_two, small_two = block_backward(
        second_in, back_two, stored_two, allowed_mask, cot_second.astype(jnp.float32)
    )
    terms_two = group_terms(left_two, right_two)
    summed_two = reduce_block(terms_two, small_two)
    grad_skip = jnp.where(is_first, 0.0, d_second_in)
    upstream_one = cot_first.astype(jnp.float32) + jnp.where(is_first, d_second_in, 0.0)
    back_one = fetch_backward(shards, 0)
    ignored_one, stored_one = block_forward(tokens, back_one, allowed_mask)
    grad_tokens, left_one, right_one, small_one = block_backward(
        tokens, back_one, stored_one, allowed_mask, upstream_one
    )
    terms_one = group_terms(left_one, right_one)
    summed_one = reduce_block(terms_one, small_one)
    stacked = tuple(
        (
            jnp.stack([first_part, second_part])
            for first_part, second_part in zip(summed_one, summed_two)
        )
    )
    return (
        out_first,
        out_second,
        grad_tokens,
        grad_skip,
        stacked[0],
        stacked[1],
        stacked[2],
        stacked[3],
        stacked[4],
        stacked[5],
        stacked[6],
    )


def solution(mesh):
    placed = (
        P(("wide", "narrow"), None),
        P(("wide", "narrow"), None),
        P(("wide", "narrow"), None),
        P(("wide", "narrow"), None),
        P(None, None, ("wide", "narrow")),
        P(None, None, ("wide", "narrow")),
        P(None, None, ("wide", "narrow")),
        P(None, ("wide", "narrow"), None),
        P(None, None, ("wide", "narrow")),
        P(None, None, ("wide", "narrow")),
        P(None, ("wide", "narrow")),
        P(("wide", "narrow")),
        P(("wide", "narrow"), None),
    )
    return jax.shard_map(
        body,
        mesh=mesh,
        in_specs=placed,
        out_specs=(
            P(("wide", "narrow"), None),
            P(("wide", "narrow"), None),
            P(("wide", "narrow"), None),
            P(("wide", "narrow"), None),
            P(None, None, ("wide", "narrow")),
            P(None, None, ("wide", "narrow")),
            P(None, None, ("wide", "narrow")),
            P(None, ("wide", "narrow"), None),
            P(None, None, ("wide", "narrow")),
            P(None, None, ("wide", "narrow")),
            P(None, ("wide", "narrow")),
        ),
        check_vma=False,
    )
```

profile of v0, /device:TPU:0, one launch (start us, length us, event | category | flops | bytes accessed | tf_op | source)
XLA Modules:
  0.0 1479.1 jit_solution(1161685598918951939)
XLA Ops:
  17.6 44.8 %all-gather.1 = bf16[1,6,768]{1,0,2:T(2,128)(2,1)S(1)} all-gather(bf16[1,6,24]{1,0,2:T(2,128)(2,1)S(1)} %copy.179), channel_id=3, replica_groups=mesh['wide'=8,'narrow'=4] {'wide','narrow'}, dimensions={2}, use_global_device_ids=true | all-gather | bytes 9504 | tf_op jit(solution)/shard_map/all_gather | solution.py:275
  63.4 37.7 %all-gather.3 = bf16[1,2,768]{1,0,2:T(2,128)(2,1)S(1)} all-gather(bf16[1,2,24]{1,0,2:T(2,128)(2,1)S(1)} %copy.180), channel_id=5, replica_groups=mesh['wide'=8,'narrow'=4] {'wide','narrow'}, dimensions={2}, use_global_device_ids=true | all-gather | bytes 3168 | tf_op jit(solution)/shard_map/all_gather | solution.py:276
  102.1 37.3 %all-reduce.9 = (bf16[3072]{0:T(1024)(128)(2,1)S(1)}, bf16[3072]{0:T(1024)(128)(2,1)}) all-reduce(bf16[3072]{0:T(1024)(128)(2,1)S(1)} %dynamic-update-slice, bf16[3072]{0:T(1024)(128)(2,1)S(1)} %dynamic-update-slice.1), channel_id=7, replica_groups=mesh['wide'=8,'narrow'=4] {'wide','narrow'}, use_global_device_ids=true, to_apply=%add | all-reduce | flops 6144 | bytes 24576
  140.1 43.7 %all-gather.8 = bf16[1,6,768]{1,0,2:T(2,128)(2,1)S(1)} all-gather(bf16[1,6,24]{1,0,2:T(2,128)(2,1)S(1)} %copy.181), channel_id=10, replica_groups=mesh['wide'=8,'narrow'=4] {'wide','narrow'}, dimensions={2}, use_global_device_ids=true | all-gather | bytes 9504 | tf_op jit(solution)/shard_map/all_gather | solution.py:275
  184.3 12.8 slice_reduce_fusion.8
  197.1 13.8 slice_reduce_fusion
  215.8 5.5 fusion.58
  233.7 4.9 fusion.113
  242.7 18.7 %fusion.6 = (bf16[512,3072]{1,0:T(8,128)(2,1)}, f32[512,3072]{1,0:T(8,128)}) fusion(f32[3072]{0:T(1024)S(1)} %convert_element_type.322, bf16[512,768]{1,0:T(8,128)(2,1)S(1)} %add_convert_fusion.3, bf16[1,768,3072]{1,2,0:T(8,128)(2,1)} %all-gather.51.cloned.1.call-done), kind=kOutput, calls=%fused_computation.22 | convolution fusion | flops 2519728128 | bytes 14954496 | tf_op jit(solution)/shard_map/dot_general | solution.py:112
  264.6 6.0 fusion.149
  273.9 52.9 %all-gather.55.cloned.1.call-done = bf16[1,768,2304]{1,2,0:T(8,128)(2,1)} async-done(((bf16[1,768,72]{1,2,0:T(8,128)(2,1)}), bf16[1,768,2304]{1,2,0:T(8,128)(2,1)}) %all-gather.55.cloned.1.call-update) | async-done | bytes 3538960 | tf_op jit(solution)/shard_map/all_gather | solution.py:271
  326.8 5.5 fusion.59
  344.7 4.7 fusion.112
  352.8 40.5 %all-gather.10 = bf16[1,2,768]{1,0,2:T(2,128)(2,1)S(1)} all-gather(bf16[1,2,24]{1,0,2:T(2,128)(2,1)S(1)} %copy.182), channel_id=12, replica_groups=mesh['wide'=8,'narrow'=4] {'wide','narrow'}, dimensions={2}, use_global_device_ids=true | all-gather | bytes 3168 | tf_op jit(solution)/shard_map/all_gather | solution.py:276
  402.3 46.5 %all-gather.59.cloned.1.call-done = bf16[1,768,3072]{1,2,0:T(8,128)(2,1)} async-done(((bf16[1,768,96]{1,2,0:T(8,128)(2,1)}), bf16[1,768,3072]{1,2,0:T(8,128)(2,1)}) %all-gather.59.cloned.1.call-update) | async-done | bytes 4718608 | tf_op jit(solution)/shard_map/all_gather | solution.py:273
  448.9 18.4 %fusion.9 = (bf16[512,3072]{1,0:T(8,128)(2,1)}, f32[512,3072]{1,0:T(8,128)}) fusion(f32[3072]{0:T(1024)S(1)} %copy-done.43, bf16[512,768]{1,0:T(8,128)(2,1)S(1)} %add_convert_fusion.1, bf16[1,768,3072]{1,2,0:T(8,128)(2,1)} %all-gather.59.cloned.1.call-done), kind=kOutput, calls=%fused_computation.25 | convolution fusion | flops 2519728128 | bytes 14954496 | tf_op jit(solution)/shard_map/dot_general | solution.py:112
  467.2 47.6 %all-gather.61.cloned.1.call-done = bf16[1,3072,768]{2,1,0:T(8,128)(2,1)} async-done(((bf16[1,96,768]{2,1,0:T(8,128)(2,1)}), bf16[1,3072,768]{2,1,0:T(8,128)(2,1)}) %all-gather.61.cloned.1.call-update) | async-done | bytes 4718608 | tf_op jit(solution)/shard_map/all_gather | solution.py:274
  514.8 6.2 fusion.151
  524.0 8.1 convert_reduce_fusion
  532.2 7.8 multiply_reduce_fusion.2
  547.4 11.2 multiply_reduce_fusion.1
  560.8 7.1 multiply_convert_fusion.1
  582.7 7.3 multiply_reduce_fusion.3
  591.8 8.4 convert_reduce_fusion.1
  600.2 6.6 multiply_reduce_fusion.4
  615.6 11.7 multiply_reduce_fusion
  628.5 9.8 multiply_convert_fusion
  646.9 5.7 multiply_bitcast_fusion
  662.8 14.3 all-to-all-done.2
  691.0 36.1 %all-to-all-done = bf16[512,8,4,72]{0,3,1,2:T(8,128)(2,1)} async-done(((bf16[512,8,4,72]{0,3,1,2:T(8,128)(2,1)}), bf16[512,8,4,72]{0,3,1,2:T(8,128)(2,1)}, u32[]{:S(2)}, u32[]{:S(2)}) %all-to-all-start) | async-done | bytes 2359328 | tf_op jit(solution)/shard_map/all_to_all | solution.py:217
  740.4 4.9 copy.139
  745.3 5.9 squeeze.203
  751.2 5.6 fusion.114
  756.8 4.7 copy.150
  765.3 11.7 all-to-all-done.1
  777.0 4.6 all-to-all-start.4
  787.5 4.6 fusion.152
  793.2 4.7 copy.153
  801.8 33.7 %all-to-all-done.4 = bf16[512,8,4,96]{0,3,1,2:T(8,128)(2,1)} async-done(((bf16[512,8,4,96]{0,3,1,2:T(8,128)(2,1)}), bf16[512,8,4,96]{0,3,1,2:T(8,128)(2,1)}, u32[]{:S(2)}, u32[]{:S(2)}) %all-to-all-start.4) | async-done | bytes 3145760 | tf_op jit(solution)/shard_map/all_to_all | solution.py:217
  835.5 4.6 all-to-all-start.5
  847.2 5.5 fusion.155
  853.9 4.7 copy.159
  862.5 14.9 %all-to-all-done.5 = bf16[512,8,4,96]{0,3,1,2:T(8,128)(2,1)} async-done(((bf16[512,8,4,96]{0,3,1,2:T(8,128)(2,1)}), bf16[512,8,4,96]{0,3,1,2:T(8,128)(2,1)}, u32[]{:S(2)}, u32[]{:S(2)}) %all-to-all-start.5) | async-done | bytes 3145760 | tf_op jit(solution)/shard_map/all_to_all | solution.py:217
  877.4 4.7 all-to-all-start.7
  889.3 5.5 fusion.156
  895.9 4.7 copy.156
  904.5 14.8 all-to-all-done.7
  919.2 4.6 all-to-all-start.6
  923.9 6.0 copy.161
  930.0 6.1 squeeze.210
  936.1 6.5 fusion.84
  942.9 18.9 %all-to-all-done.6 = bf16[512,8,4,96]{0,3,1,2:T(8,128)(2,1)} async-done(((bf16[512,8,4,96]{0,3,1,2:T(8,128)(2,1)}), bf16[512,8,4,96]{0,3,1,2:T(8,128)(2,1)}, u32[]{:S(2)}, u32[]{:S(2)}) %all-to-all-start.6) | async-done | bytes 3145760 | tf_op jit(solution)/shard_map/all_to_all | solution.py:217
  961.8 6.0 copy.158
  967.8 6.1 squeeze.209
  973.9 6.6 fusion.81
  980.5 5.7 fusion.96
  992.5 23.3 %reduce-scatter.17.cloned.1.call-done = bf16[768,1,24]{0,2,1:T(8,128)(2,1)} async-done(((bf16[768,8,24]{0,2,1:T(8,128)(2,1)}), bf16[768,1,24]{0,2,1:T(8,128)(2,1)}) %reduce-scatter.17.cloned.1.call-update) | async-done | bytes 36880 | tf_op jit(solution)/shard_map/reduce_scatter | solution.py:250
  1015.8 61.6 %reduce-scatter.19.cloned.1.call-done = bf16[768,1,24]{0,2,1:T(8,128)(2,1)} async-done(((bf16[768,8,24]{0,2,1:T(8,128)(2,1)}), bf16[768,1,24]{0,2,1:T(8,128)(2,1)}) %reduce-scatter.19.cloned.1.call-update) | async-done | bytes 36880 | tf_op jit(solution)/shard_map/reduce_scatter | solution.py:250
  1078.9 62.2 %reduce-scatter.13.cloned.1.call-done = bf16[768,1,72]{0,2,1:T(8,128)(2,1)} async-done(((bf16[768,8,72]{0,2,1:T(8,128)(2,1)}), bf16[768,1,72]{0,2,1:T(8,128)(2,1)}) %reduce-scatter.13.cloned.1.call-update) | async-done | bytes 110608 | tf_op jit(solution)/shard_map/reduce_scatter | solution.py:247
  1141.1 63.7 %reduce-scatter.15.cloned.1.call-done = bf16[768,1,72]{0,2,1:T(8,128)(2,1)} async-done(((bf16[768,8,72]{0,2,1:T(8,128)(2,1)}), bf16[768,1,72]{0,2,1:T(8,128)(2,1)}) %reduce-scatter.15.cloned.1.call-update) | async-done | bytes 110608 | tf_op jit(solution)/shard_map/reduce_scatter | solution.py:247
  1206.5 64.7 %reduce-scatter.21.cloned.1.call-done = bf16[768,1,96]{0,2,1:T(8,128)(2,1)} async-done(((bf16[768,8,96]{0,2,1:T(8,128)(2,1)}), bf16[768,1,96]{0,2,1:T(8,128)(2,1)}) %reduce-scatter.21.cloned.1.call-update) | async-done | bytes 147472 | tf_op jit(solution)/shard_map/reduce_scatter | solution.py:253
  1271.1 66.4 %reduce-scatter.23.cloned.1.call-done = bf16[768,1,96]{0,2,1:T(8,128)(2,1)} async-done(((bf16[768,8,96]{0,2,1:T(8,128)(2,1)}), bf16[768,1,96]{0,2,1:T(8,128)(2,1)}) %reduce-scatter.23.cloned.1.call-update) | async-done | bytes 147472 | tf_op jit(solution)/shard_map/reduce_scatter | solution.py:253
  1339.4 64.5 %reduce-scatter.27.cloned.1.call-done = bf16[1,96,768]{2,1,0:T(8,128)(2,1)} async-done(((bf16[8,96,768]{2,1,0:T(8,128)(2,1)}), bf16[1,96,768]{2,1,0:T(8,128)(2,1)}) %reduce-scatter.27.cloned.1.call-update) | async-done | bytes 147472 | tf_op jit(solution)/shard_map/reduce_scatter | solution.py:256
  1403.9 66.4 %reduce-scatter.25.cloned.1.call-done = bf16[1,96,768]{2,1,0:T(8,128)(2,1)} async-done(((bf16[8,96,768]{2,1,0:T(8,128)(2,1)}), bf16[1,96,768]{2,1,0:T(8,128)(2,1)}) %reduce-scatter.25.cloned.1.call-update) | async-done | bytes 147472 | tf_op jit(solution)/shard_map/reduce_scatter | solution.py:256
  (326 shorter events, 202.0 us)
Async XLA Ops:
  7.2 55.6 %copy-start.49 = (bf16[2,2,24]{2,1,0:T(2,128)(2,1)S(1)}, bf16[2,2,24]{2,1,0:T(2,128)(2,1)}, u32[]{:S(2)}) copy-start(bf16[2,2,24]{2,1,0:T(2,128)(2,1)} %param.22) | copy-start | bytes 580
  7.2 94.4 %copy-start.47 = (bf16[2,96]{1,0:T(2,128)(2,1)S(1)}, bf16[2,96]{1,0:T(2,128)(2,1)}, u32[]{:S(2)}) copy-start(bf16[2,96]{1,0:T(2,128)(2,1)} %param.23) | copy-start | bytes 1156
  7.2 208.6 %all-gather.47.cloned.1.call-start = ((), (), s32[]{:S(2)}) async-start(), calls=%async_computation.32 | async-start | bytes 3649536 | tf_op jit(solution)/shard_map/all_gather | solution.py:271
  8.9 230.8 %all-gather.49.cloned.1.call-start = ((), (), s32[]{:S(2)}) async-start(), calls=%async_computation.33 | async-start | bytes 1216512 | tf_op jit(solution)/shard_map/all_gather | solution.py:272
  10.4 232.3 %all-gather.51.cloned.1.call-start = ((), (), s32[]{:S(2)}) async-start(), calls=%async_computation.34 | async-start | bytes 4866048 | tf_op jit(solution)/shard_map/all_gather | solution.py:273
  12.2 252.4 %all-gather.53.cloned.1.call-start = ((), (), s32[]{:S(2)}) async-start(), calls=%async_computation.35 | async-start | bytes 4866048 | tf_op jit(solution)/shard_map/all_gather | solution.py:274
  14.0 312.8 %all-gather.55.cloned.1.call-start = ((), (), s32[]{:S(2)}) async-start(), calls=%async_computation.36 | async-start | bytes 3649536 | tf_op jit(solution)/shard_map/all_gather | solution.py:271
  14.6 384.9 %all-gather.57.cloned.1.call-start = ((), (), s32[]{:S(2)}) async-start(), calls=%async_computation.37 | async-start | bytes 1216512 | tf_op jit(solution)/shard_map/all_gather | solution.py:272
  15.2 433.7 %all-gather.59.cloned.1.call-start = ((), (), s32[]{:S(2)}) async-start(), calls=%async_computation.38 | async-start | bytes 4866048 | tf_op jit(solution)/shard_map/all_gather | solution.py:273
  15.9 498.9 %all-gather.61.cloned.1.call-start = ((), (), s32[]{:S(2)}) async-start(), calls=%async_computation.39 | async-start | bytes 4866048 | tf_op jit(solution)/shard_map/all_gather | solution.py:274
  16.7 715.0 %all-gather.35.cloned.1.call-start = ((), (), s32[]{:S(2)}) async-start(), calls=%async_computation.20 | async-start | bytes 3932160 | tf_op jit(solution)/shard_map/all_gather | solution.py:204
  101.5 114.0 %copy-start.44 = (s32[1,512]{1,0:T(1,128)S(1)}, s32[1,512]{1,0:T(1,128)}, u32[]{:S(2)}) copy-start(s32[1,512]{1,0:T(1,128)} %param.25) | copy-start | bytes 6148
  139.4 103.4 %copy-start.41 = (f32[3072]{0:T(1024)}, f32[3072]{0:T(1024)S(1)}, u32[]{:S(2)}) copy-start(f32[3072]{0:T(1024)S(1)} %convert_element_type.322) | copy-start | bytes 36868
  140.1 75.7 %copy-start.24 = (bf16[512,768]{1,0:T(8,128)(2,1)S(1)}, bf16[512,768]{1,0:T(8,128)(2,1)}, u32[]{:S(2)}) copy-start(bf16[512,768]{1,0:T(8,128)(2,1)} %param.13) | copy-start | bytes 2359300
  184.3 86.7 %copy-start.32 = (pred[512]{0:T(512)(128)(4,1)}, pred[512]{0:T(512)(128)(4,1)S(1)}, u32[]{:S(2)}) copy-start(pred[512]{0:T(512)(128)(4,1)S(1)} %iota_compare_fusion.1) | copy-start | bytes 1540
  215.5 26.9 %copy-start.34 = (f32[768]{0:T(1024)}, f32[768]{0:T(1024)S(1)}, u32[]{:S(2)}) copy-start(f32[768]{0:T(1024)S(1)} %get-tuple-element.207) | copy-start | bytes 9220
  215.5 55.5 %copy-start.30 = (f32[768]{0:T(1024)}, f32[768]{0:T(1024)S(1)}, u32[]{:S(2)}) copy-start(f32[768]{0:T(1024)S(1)} %get-tuple-element.206) | copy-start | bytes 9220
  241.9 19.5 %copy-start.6 = (f32[512,768]{1,0:T(8,128)}, f32[512,768]{1,0:T(8,128)S(1)}, u32[]{:S(2)}) copy-start(f32[512,768]{1,0:T(8,128)S(1)} %get-tuple-element.265) | copy-start | bytes 4718596
  241.9 19.5 %copy-start.36 = (f32[512]{0:T(512)}, f32[512]{0:T(512)S(1)}, u32[]{:S(2)}) copy-start(f32[512]{0:T(512)S(1)} %broadcast_multiply_fusion.11) | copy-start | bytes 6148
  242.3 19.2 %copy-start.38 = (f32[512]{0:T(512)}, f32[512]{0:T(512)S(1)}, u32[]{:S(2)}) copy-start(f32[512]{0:T(512)S(1)} %add_rsqrt_fusion.3) | copy-start | bytes 6148
  242.3 493.9 %all-gather.37.cloned.1.call-start = ((), (), s32[]{:S(2)}) async-start(), calls=%async_computation.22 | async-start | bytes 3932160 | tf_op jit(solution)/shard_map/all_gather | solution.py:204
  242.7 21.9 %copy-start.13 = (bf16[512,768]{1,0:T(8,128)(2,1)}, bf16[512,768]{1,0:T(8,128)(2,1)S(1)}, u32[]{:S(2)}) copy-start(bf16[512,768]{1,0:T(8,128)(2,1)S(1)} %add_convert_fusion.3) | copy-start | bytes 2359300
  271.0 61.3 %copy-start.28 = (f32[512]{0:T(512)}, f32[512]{0:T(512)S(1)}, u32[]{:S(2)}) copy-start(f32[512]{0:T(512)S(1)} %add_rsqrt_fusion.2) | copy-start | bytes 6148
  273.9 58.5 %copy-start.8 = (bf16[512,768]{1,0:T(8,128)(2,1)}, bf16[512,768]{1,0:T(8,128)(2,1)S(1)}, u32[]{:S(2)}) copy-start(bf16[512,768]{1,0:T(8,128)(2,1)S(1)} %get-tuple-element.238) | copy-start | bytes 2359300
  349.5 50.0 %copy-start.9 = (bf16[512,768]{1,0:T(8,128)(2,1)S(1)}, bf16[512,768]{1,0:T(8,128)(2,1)}, u32[]{:S(2)}) copy-start(bf16[512,768]{1,0:T(8,128)(2,1)} %copy-done.8) | copy-start | bytes 2359300
  350.7 400.5 %all-gather.31.cloned.1.call-start = ((), (), s32[]{:S(2)}) async-start(), calls=%async_computation.16 | async-start | bytes 3932160 | tf_op jit(solution)/shard_map/all_gather | solution.py:203
  351.4 436.1 %all-gather.33.cloned.1.call-start = ((), (), s32[]{:S(2)}) async-start(), calls=%async_computation.18 | async-start | bytes 3932160 | tf_op jit(solution)/shard_map/all_gather | solution.py:203
  352.0 495.2 %all-gather.39.cloned.1.call-start = ((), (), s32[]{:S(2)}) async-start(), calls=%async_computation.24 | async-start | bytes 3932160 | tf_op jit(solution)/shard_map/all_gather | solution.py:205
  398.9 490.4 %all-gather.41.cloned.1.call-start = ((), (), s32[]{:S(2)}) async-start(), calls=%async_computation.26 | async-start | bytes 3932160 | tf_op jit(solution)/shard_map/all_gather | solution.py:205
  399.5 49.4 %copy-start.43 = (f32[3072]{0:T(1024)S(1)}, f32[3072]{0:T(1024)}, u32[]{:S(2)}) copy-start(f32[3072]{0:T(1024)} %convert_element_type.323) | copy-start | bytes 36868
  402.3 64.9 %copy-start.14 = (bf16[512,768]{1,0:T(8,128)(2,1)}, bf16[512,768]{1,0:T(8,128)(2,1)S(1)}, u32[]{:S(2)}) copy-start(bf16[512,768]{1,0:T(8,128)(2,1)S(1)} %add_convert_fusion.1) | copy-start | bytes 2359300
  402.3 112.5 %copy-start.46 = (f32[768]{0:T(1024)S(1)}, f32[768]{0:T(1024)}, u32[]{:S(2)}) copy-start(f32[768]{0:T(1024)} %get-tuple-element.201) | copy-start | bytes 9220
  524.0 8.2 copy-start.16
  540.1 396.0 %all-gather.45.cloned.1.call-start = ((), (), s32[]{:S(2)}) async-start(), calls=%async_computation.30 | async-start | bytes 3932160 | tf_op jit(solution)/shard_map/all_gather | solution.py:206
  547.4 11.3 slice-start.3
  547.4 12.2 slice-start.4
  547.4 13.4 slice-start.5
  591.7 8.4 copy-start.17
  591.7 8.4 copy-start.7
  591.7 8.4 copy-start.21
  591.7 8.4 copy-start.35
  591.7 8.4 copy-start.37
  591.7 8.4 copy-start.39
  611.5 41.1 %all-to-all-start.3 = ((bf16[512,8,4,24]{0,3,1,2:T(8,128)(2,1)}), bf16[512,8,4,24]{0,3,1,2:T(8,128)(2,1)S(1)}, u32[]{:S(2)}, u32[]{:S(2)}) async-start(bf16[512,8,4,24]{0,3,1,2:T(8,128)(2,1)} %copy.148), calls=%async_computation.6 | async-start | bytes 1572864 | tf_op jit(solution)/shard_map/all_to_all | solution.py:217
  615.0 358.9 %all-gather.43.cloned.1.call-start = ((), (), s32[]{:S(2)}) async-start(), calls=%async_computation.28 | async-start | bytes 3932160 | tf_op jit(solution)/shard_map/all_gather | solution.py:206
  615.6 11.7 slice-start
  615.6 11.7 slice-start.1
  615.6 12.9 slice-start.2
  652.5 24.7 %all-to-all-start.2 = ((bf16[512,8,4,24]{0,3,1,2:T(8,128)(2,1)}), bf16[512,8,4,24]{0,3,1,2:T(8,128)(2,1)}, u32[]{:S(2)}, u32[]{:S(2)}) async-start(bf16[512,8,4,24]{0,3,1,2:T(8,128)(2,1)} %copy.144), calls=%async_computation.4 | async-start | bytes 1572864 | tf_op jit(solution)/shard_map/all_to_all | solution.py:217
  677.2 49.9 %all-to-all-start = ((bf16[512,8,4,72]{0,3,1,2:T(8,128)(2,1)}), bf16[512,8,4,72]{0,3,1,2:T(8,128)(2,1)}, u32[]{:S(2)}, u32[]{:S(2)}) async-start(bf16[512,8,4,72]{0,3,1,2:T(8,128)(2,1)} %copy.138), calls=%async_computation | async-start | bytes 4718592 | tf_op jit(solution)/shard_map/all_to_all | solution.py:217
  681.7 304.5 %all-reduce.12.cloned.1.call-start = ((), (), s32[]{:S(2)}) async-start(), calls=%async_computation.40 | async-start | bytes 172032
  727.1 49.9 %all-to-all-start.1 = ((bf16[512,8,4,72]{0,3,1,2:T(8,128)(2,1)}), bf16[512,8,4,72]{0,3,1,2:T(8,128)(2,1)}, u32[]{:S(2)}, u32[]{:S(2)}) async-start(bf16[512,8,4,72]{0,3,1,2:T(8,128)(2,1)} %copy.140), calls=%async_computation.2 | async-start | bytes 4718592 | tf_op jit(solution)/shard_map/all_to_all | solution.py:217
  731.6 284.2 %reduce-scatter.17.cloned.1.call-start = ((), (), s32[]{:S(2)}) async-start(), calls=%async_computation.21 | async-start | bytes 331776 | tf_op jit(solution)/shard_map/reduce_scatter | solution.py:250
  735.4 342.0 %reduce-scatter.19.cloned.1.call-start = ((), (), s32[]{:S(2)}) async-start(), calls=%async_computation.23 | async-start | bytes 331776 | tf_op jit(solution)/shard_map/reduce_scatter | solution.py:250
  740.2 400.9 %reduce-scatter.13.cloned.1.call-start = ((), (), s32[]{:S(2)}) async-start(), calls=%async_computation.17 | async-start | bytes 995328 | tf_op jit(solution)/shard_map/reduce_scatter | solution.py:247
  777.0 58.5 %all-to-all-start.4 = ((bf16[512,8,4,96]{0,3,1,2:T(8,128)(2,1)}), bf16[512,8,4,96]{0,3,1,2:T(8,128)(2,1)}, u32[]{:S(2)}, u32[]{:S(2)}) async-start(bf16[512,8,4,96]{0,3,1,2:T(8,128)(2,1)} %copy.151), calls=%async_computation.8 | async-start | bytes 6291456 | tf_op jit(solution)/shard_map/all_to_all | solution.py:217
  781.7 423.1 %reduce-scatter.15.cloned.1.call-start = ((), (), s32[]{:S(2)}) async-start(), calls=%async_computation.19 | async-start | bytes 995328 | tf_op jit(solution)/shard_map/reduce_scatter | solution.py:247
  835.5 41.9 %all-to-all-start.5 = ((bf16[512,8,4,96]{0,3,1,2:T(8,128)(2,1)}), bf16[512,8,4,96]{0,3,1,2:T(8,128)(2,1)}, u32[]{:S(2)}, u32[]{:S(2)}) async-start(bf16[512,8,4,96]{0,3,1,2:T(8,128)(2,1)} %copy.154), calls=%async_computation.10 | async-start | bytes 6291456 | tf_op jit(solution)/shard_map/all_to_all | solution.py:217
  840.2 431.0 %reduce-scatter.21.cloned.1.call-start = ((), (), s32[]{:S(2)}) async-start(), calls=%async_computation.25 | async-start | bytes 1327104 | tf_op jit(solution)/shard_map/reduce_scatter | solution.py:253
  877.4 41.8 %all-to-all-start.7 = ((bf16[512,8,4,96]{0,3,1,2:T(8,128)(2,1)}), bf16[512,8,4,96]{0,3,1,2:T(8,128)(2,1)}, u32[]{:S(2)}, u32[]{:S(2)}) async-start(bf16[512,8,4,96]{0,3,1,2:T(8,128)(2,1)} %copy.160), calls=%async_computation.14 | async-start | bytes 6291456 | tf_op jit(solution)/shard_map/all_to_all | solution.py:217
  882.1 455.5 %reduce-scatter.23.cloned.1.call-start = ((), (), s32[]{:S(2)}) async-start(), calls=%async_computation.27 | async-start | bytes 1327104 | tf_op jit(solution)/shard_map/reduce_scatter | solution.py:253
  919.2 42.5 %all-to-all-start.6 = ((bf16[512,8,4,96]{0,3,1,2:T(8,128)(2,1)}), bf16[512,8,4,96]{0,3,1,2:T(8,128)(2,1)}, u32[]{:S(2)}, u32[]{:S(2)}) async-start(bf16[512,8,4,96]{0,3,1,2:T(8,128)(2,1)} %copy.157), calls=%async_computation.12 | async-start | bytes 6291456 | tf_op jit(solution)/shard_map/all_to_all | solution.py:217
  923.9 480.0 %reduce-scatter.27.cloned.1.call-start = ((), (), s32[]{:S(2)}) async-start(), calls=%async_computation.31 | async-start | bytes 1327104 | tf_op jit(solution)/shard_map/reduce_scatter | solution.py:256
  942.6 527.7 %reduce-scatter.25.cloned.1.call-start = ((), (), s32[]{:S(2)}) async-start(), calls=%async_computation.29 | async-start | bytes 1327104 | tf_op jit(solution)/shard_map/reduce_scatter | solution.py:256
  (26 other events, 109.6 us)
Sparse Core Ops, SparseCore 0:
  11.5 63.9 all-gather.46
  78.9 52.9 all-gather.48
  135.4 63.3 all-gather.50
  202.1 62.4 all-gather.52
  267.9 58.8 all-gather.54
  329.6 53.4 all-gather.56
  386.6 62.2 all-gather.58
  452.3 62.4 all-gather.60
  516.4 27.3 all-gather.34
  545.2 28.5 all-gather.36
  575.3 28.5 all-gather.30
  605.3 36.9 all-gather.32
  643.9 36.9 all-gather.38
  682.3 45.4 all-gather.40
  729.2 45.3 all-gather.44
  776.0 45.3 all-gather.42
  828.8 123.2 all-reduce.11
  955.8 59.9 reduce-scatter.16
  1019.7 57.6 reduce-scatter.18
  1080.6 60.3 reduce-scatter.12
  1144.5 60.2 reduce-scatter.14
  1208.1 62.9 reduce-scatter.20
  1274.5 62.9 reduce-scatter.22
  1340.8 62.9 reduce-scatter.26
  1407.3 62.9 reduce-scatter.24
where the time goes:
time: 1490 us; the launch traced here: 1480 us
  waiting for transfers between devices  772 us (52%)
  matrix products  214 us (14%)
  blocking collectives  204 us (14%)
  local copies, waits for them, and re-layouts  180 us (12%)
  other arithmetic  55.1 us (4%)
  starting transfers between devices  37.4 us (3%)
  between operations  16.3 us (1%)
    all_to_all x8, waiting for transfers between devices, group_terms(): lax.all_to_all(shortened(tuple((owned_columns(matrix) for matrix in right...  144 us
    reduce_scatter x2, waiting for transfers between devices, reduce_block(): lax.psum_scatter(terms[2].astype(jnp.bfloat16), 'wide', scatter_dimension...  131 us
    reduce_scatter x2, waiting for transfers between devices, reduce_block(): lax.psum_scatter(terms[3].astype(jnp.bfloat16), 'wide', scatter_dimension...  131 us
    reduce_scatter x2, waiting for transfers between devices, reduce_block(): lax.psum_scatter(terms[0].astype(jnp.bfloat16), 'wide', scatter_dimension...  126 us
    all_gather x2, blocking collectives, fetch_forward(): lax.all_gather(bias_part[index], ('wide', 'narrow'), axis=1, tiled=True)  88.5 us
    reduce_scatter x2, waiting for transfers between devices, reduce_block(): lax.psum_scatter(terms[1].astype(jnp.bfloat16), 'wide', scatter_dimension...  84.9 us
    all_gather x2, blocking collectives, fetch_forward(): lax.all_gather(gain_part[index], ('wide', 'narrow'), axis=1, tiled=True)  78.2 us
    all_gather x2, waiting for transfers between devices, fetch_forward(): lax.all_gather(qkv_part[index], ('wide', 'narrow'), axis=1, tiled=True)  53 us
  transfers between devices with their start and end apart: 33, of which 19 were waited for; matrix products, arithmetic and copies ran while one was open for 29% of the time, Pallas kernels for 0%

commit v1 on v0

v1 whole, which is shorter than its diff:
```python
import functools
import math

import jax
import jax.numpy as jnp
from jax import lax
from jax.experimental import pallas as pl
from jax.experimental.pallas import tpu as pltpu
from jax.sharding import Mesh, PartitionSpec as P

HEADS = 12
HEAD_DIM = 64
EPSILON = 1e-12
MASKED = -1e30
BF = jnp.bfloat16
F32 = jnp.float32
NT = (((1,), (1,)), ((), ()))
TN = (((0,), (0,)), ((), ()))
NN = (((1,), (0,)), ((), ()))
PARTS = 8
LANES = 128
VMEM = pl.BlockSpec(memory_space=pltpu.VMEM)


def mm(a, b, dims=NN):
    return lax.dot_general(a, b, dims, preferred_element_type=F32)


def call(kernel, out_shapes, scratch, flops, *args):
    n_bytes = sum(a.size * a.dtype.itemsize for a in args) + sum(
        math.prod(o.shape) * jnp.dtype(o.dtype).itemsize for o in out_shapes
    )
    return pl.pallas_call(
        kernel,
        out_shape=out_shapes,
        in_specs=[VMEM] * len(args),
        out_specs=[VMEM] * len(out_shapes),
        scratch_shapes=scratch,
        compiler_params=pltpu.CompilerParams(vmem_limit_bytes=56 * 1024 * 1024),
        cost_estimate=pl.CostEstimate(flops=flops, bytes_accessed=n_bytes, transcendentals=0),
    )(*args)


def windows(length):
    tiles = length // LANES
    return [
        (t, max(0, t - 1) * LANES, min(tiles, t + 2) * LANES) for t in range(tiles)
    ]


def attention_forward_kernel(length, width, x, wt, bias, seg_col, key_row, qkv, mix, lse_rows, mask, lse):
    for part in range(3):
        cols = slice(part * width, (part + 1) * width)
        qkv[:, cols] = (mm(x[...], wt[cols, :], NT) + bias[:, cols]).astype(BF)
    for t, low, high in windows(length):
        rows = lax.broadcasted_iota(jnp.int32, (LANES, high - low), 0) + t * LANES
        keys = lax.broadcasted_iota(jnp.int32, (LANES, high - low), 1) + low
        same = seg_col[t * LANES : (t + 1) * LANES, :] == key_row[:, low:high]
        mask[t, :, : high - low] = jnp.where(same | (rows == keys), 0.0, MASKED)
    lse[...] = jnp.zeros_like(lse)

    def pair(p, carry):
        at = pl.multiple_of(p * LANES, LANES)
        lane = lax.broadcasted_iota(jnp.int32, (LANES, LANES), 1)
        for t, low, high in windows(length):
            here = slice(t * LANES, (t + 1) * LANES)
            q = qkv[here, pl.ds(at, LANES)] * HEAD_DIM ** (-0.5)
            k = qkv[low:high, pl.ds(pl.multiple_of(at + width, LANES), LANES)]
            v = qkv[low:high, pl.ds(pl.multiple_of(at + 2 * width, LANES), LANES)]
            outs = []
            for h in range(2):
                mine = (lane < HEAD_DIM) == (h == 0)
                s = mm(jnp.where(mine, q, 0).astype(BF), k, NT) + mask[t, :, : high - low]
                top = jnp.max(s, -1, keepdims=True)
                e = jnp.exp(s - top)
                total = jnp.sum(e, -1, keepdims=True)
                outs.append(mm((e * (1.0 / total)).astype(BF), v))
                lse[here, :] = jnp.where(lane == 2 * p + h, top + jnp.log(total), lse[here, :])
            mix[here, pl.ds(at, LANES)] = jnp.where(lane < HEAD_DIM, outs[0], outs[1]).astype(BF)
        return carry

    lax.fori_loop(0, width // LANES, pair, 0)
    lse_rows[...] = lse[...].T[: lse_rows.shape[0], :]


def attention_forward(x, wt, bias, seg_col, key_row):
    length, width = x.shape
    shapes = [
        jax.ShapeDtypeStruct((length, 3 * width), BF),
        jax.ShapeDtypeStruct((length, width), BF),
        jax.ShapeDtypeStruct((16, length), F32),
    ]
    scratch = [
        pltpu.VMEM((length // LANES, LANES, 3 * LANES), F32),
        pltpu.VMEM((length, LANES), F32),
    ]
    flops = 2 * length * width * 3 * width + 4 * 4 * length * length * width
    return call(
        functools.partial(attention_forward_kernel, length, width),
        shapes, scratch, flops, x, wt, bias, seg_col, key_row,
    )


def attention_backward_kernel(length, width, qkv, dmix, mix, lse_rows, seg_row, key_col, dqkv, sums, mask, dq_sum):
    for t, low, high in windows(length):
        keys = lax.broadcasted_iota(jnp.int32, (LANES, high - low), 0) + t * LANES
        rows = lax.broadcasted_iota(jnp.int32, (LANES, high - low), 1) + low
        same = key_col[t * LANES : (t + 1) * LANES, :] == seg_row[:, low:high]
        mask[t, :, : high - low] = jnp.where(same | (rows == keys), 0.0, MASKED)

    def pair(p, carry):
        at = pl.multiple_of(p * LANES, LANES)
        at_k = pl.multiple_of(at + width, LANES)
        at_v = pl.multiple_of(at + 2 * width, LANES)
        lane = lax.broadcasted_iota(jnp.int32, (length, LANES), 1)
        q = qkv[:, pl.ds(at, LANES)] * HEAD_DIM ** (-0.5)
        dm = dmix[:, pl.ds(at, LANES)]
        product = dm.astype(F32) * mix[:, pl.ds(at, LANES)].astype(F32)
        ones_lane = lax.broadcasted_iota(jnp.int32, (8, LANES), 1)
        q_h, dm_h, lse_h, delta_h = [], [], [], []
        for h in range(2):
            mine = (lane < HEAD_DIM) == (h == 0)
            q_h.append(jnp.where(mine, q, 0).astype(BF))
            dm_h.append(jnp.where(mine, dm, 0).astype(BF))
            picks = jnp.where((ones_lane < HEAD_DIM) == (h == 0), 1.0, 0.0)
            delta_h.append(
                lax.dot_general(picks, product, NT, precision=lax.Precision.HIGHEST, preferred_element_type=F32)[:1, :]
            )
            lse_h.append(lse_rows[pl.ds(2 * p + h, 1), :])
        dq_sum[...] = jnp.zeros_like(dq_sum)
        for t, low, high in windows(length):
            here = slice(t * LANES, (t + 1) * LANES)
            k = qkv[here, pl.ds(at_k, LANES)]
            v = qkv[here, pl.ds(at_v, LANES)]
            dk = jnp.zeros((LANES, LANES), F32)
            dv = jnp.zeros((LANES, LANES), F32)
            dq = jnp.zeros((high - low, LANES), F32)
            for h in range(2):
                mine = (lane[:LANES] < HEAD_DIM) == (h == 0)
                q_one, dm_one = q_h[h][low:high], dm_h[h][low:high]
                s = mm(k, q_one, NT) + mask[t, :, : high - low]
                a = jnp.exp(s - lse_h[h][:, low:high])
                da = mm(v, dm_one, NT)
                ds = (a * (da - delta_h[h][:, low:high])).astype(BF)
                dv += mm(a.astype(BF), dm_one)
                dk += mm(ds, q_one)
                dq += mm(ds, jnp.where(mine, k, 0).astype(BF), TN)
            dqkv[here, pl.ds(at_k, LANES)] = dk.astype(BF)
            dqkv[here, pl.ds(at_v, LANES)] = dv.astype(BF)
            dq_sum[low:high, :] += dq
        dqkv[:, pl.ds(at, LANES)] = (dq_sum[...] * HEAD_DIM ** (-0.5)).astype(BF)
        return carry

    lax.fori_loop(0, width // LANES, pair, 0)
    for part in range(3):
        cols = slice(part * width, (part + 1) * width)
        sums[:, cols] = mm(jnp.ones((8, length), BF), dqkv[:, cols])


def attention_backward(qkv, dmix, mix, lse_rows, seg_row, key_col):
    length, width = mix.shape
    shapes = [
        jax.ShapeDtypeStruct((length, 3 * width), BF),
        jax.ShapeDtypeStruct((8, 3 * width), F32),
    ]
    scratch = [
        pltpu.VMEM((length // LANES, LANES, 3 * LANES), F32),
        pltpu.VMEM((length, LANES), F32),
    ]
    flops = 10 * 4 * length * length * width
    return call(
        functools.partial(attention_backward_kernel, length, width),
        shapes, scratch, flops, qkv, dmix, mix, lse_rows, seg_row, key_col,
    )


def norm(values):
    centred = values - jnp.mean(values, -1, keepdims=True)
    inverse = lax.rsqrt(jnp.mean(centred * centred, -1, keepdims=True) + EPSILON)
    return centred * inverse, inverse


def norm_back(upstream, scaled, inverse, gain):
    through = upstream * gain
    return inverse * (
        through
        - jnp.mean(through, -1, keepdims=True)
        - scaled * jnp.mean(through * scaled, -1, keepdims=True)
    )


def normal_terms(u):
    size = jnp.abs(u) * (1.0 / math.sqrt(2.0))
    bell = jnp.exp(-(size * size))
    s = 1.0 / (1.0 + 0.3275911 * size)
    tail = s * (0.5 * 0.254829592 + s * (0.5 * -0.284496736 + s * (0.5 * 1.421413741 + s * (0.5 * -1.453152027 + s * (0.5 * 1.061405429)))))
    tail = tail * bell
    return jnp.where(u > 0, 1.0 - tail, tail), bell * (1.0 / math.sqrt(2.0 * math.pi))


def feed_kernel(layout, backward, tile, *refs):
    refs = list(refs)
    take = lambda n: [refs.pop(0) for _ in range(n)]
    x, mix, w_out, vectors, up_bias = take(5)
    (cot,) = take(1) if backward else (None,)
    pieces = [take(n) for n in layout]
    if backward:
        y, n1_out, g_out, du_out, df_out, do_out, dr1_out, dm_out, small, up_small, slope = refs
        small[...] = jnp.zeros_like(small)
        up_small[...] = jnp.zeros_like(up_small)
    else:
        (y,) = refs
    count, width = x.shape

    def weights(part, lower):
        got = []
        for ref in pieces[part]:
            half = ref.shape[1] // 2
            block = ref[:, half:, :] if lower else ref[:, :half, :]
            got.append(block.reshape(ref.shape[0] * half, width))
        return got[0] if len(got) == 1 else jnp.concatenate(got, 0)

    b_out, b_down, shift_one, shift_two, gain_one, gain_two = (vectors[i : i + 1, :] for i in range(6))

    def rows_step(i, carry):
        rows = pl.ds(pl.multiple_of(i * tile, tile), tile)
        r1 = x[rows, :].astype(F32) + mm(mix[rows, :], w_out[...], NT) + b_out
        z1, q1 = norm(r1)
        n1 = (z1 * gain_one + shift_one).astype(BF)
        acc = n1.astype(F32) + b_down
        for part in range(PARTS):
            u = mm(n1, weights(part, False), NT) + up_bias[part : part + 1, :]
            size = u.shape[1]
            cols = slice(part * size, (part + 1) * size)
            big, bell = normal_terms(u)
            g = (u * big).astype(BF)
            if backward:
                g_out[rows, cols] = g
                slope[:, cols] = big + u * bell
            acc += mm(g, weights(part, True))
        z2, q2 = norm(acc)
        y[rows, :] = (z2 * gain_two + shift_two).astype(BF)
        if backward:
            e = cot[rows, :].astype(F32)
            small[3:4, :] += jnp.sum(e, 0, keepdims=True)
            small[5:6, :] += jnp.sum(e * z2, 0, keepdims=True)
            dr2 = norm_back(e, z2, q2, gain_two)
            df = dr2.astype(BF)
            small[1:2, :] += jnp.sum(df.astype(F32), 0, keepdims=True)
            dn1 = dr2
            for part in range(PARTS):
                da = mm(df, weights(part, True), NT)
                size = da.shape[1]
                cols = slice(part * size, (part + 1) * size)
                du = (da * slope[:, cols]).astype(BF)
                du_out[rows, cols] = du
                up_small[part : part + 1, :] += jnp.sum(du.astype(F32), 0, keepdims=True)
                dn1 += mm(du, weights(part, False))
            small[2:3, :] += jnp.sum(dn1, 0, keepdims=True)
            small[4:5, :] += jnp.sum(dn1 * z1, 0, keepdims=True)
            dr1 = norm_back(dn1, z1, q1, gain_one)
            do = dr1.astype(BF)
            small[0:1, :] += jnp.sum(do.astype(F32), 0, keepdims=True)
            dm_out[rows, :] = mm(do, w_out[...]).astype(BF)
            n1_out[rows, :] = n1
            df_out[rows, :] = df
            do_out[rows, :] = do
            dr1_out[rows, :] = dr1
        return carry

    lax.fori_loop(0, count // tile, rows_step, 0)


def feed(x, mix, w_out, vectors, up_bias, pieces, cot=None):
    count, width = x.shape
    hidden = PARTS * up_bias.shape[1]
    tile = min(256, count)
    backward = cot is not None
    wide = jax.ShapeDtypeStruct((count, width), BF)
    high = jax.ShapeDtypeStruct((count, hidden), BF)
    shapes, scratch = [wide], []
    args = [x, mix, w_out, vectors, up_bias]
    if backward:
        args.append(cot)
        shapes += [
            wide, high, high, wide, wide, jax.ShapeDtypeStruct((count, width), F32), wide,
            jax.ShapeDtypeStruct((8, width), F32), jax.ShapeDtypeStruct(up_bias.shape, F32),
        ]
        scratch.append(pltpu.VMEM((tile, hidden), F32))
    layout = [len(piece) for piece in pieces]
    flops = 4 * count * width * (hidden + width) * (2 if backward else 1)
    return call(
        functools.partial(feed_kernel, layout, backward, tile),
        shapes, scratch, flops, *args, *[ref for piece in pieces for ref in piece],
    )


def feed_grads_kernel(first, layout, received, n1, df, g, du, *refs):
    refs = list(refs)
    got = [refs.pop(0) for _ in range(received)]
    for index, sizes in enumerate(layout):
        outs = [refs.pop(0) for _ in sizes]
        size = g.shape[1] // PARTS
        cols = slice((first + index) * size, (first + index + 1) * size)
        for lower, (left, right) in enumerate(((du, n1), (g, df))):
            full = mm(left[:, cols], right[...], TN)
            at = 0
            for out, slabs in zip(outs, sizes):
                half = out.shape[1] // 2
                rows = slice(lower * half, (lower + 1) * half)
                value = full[at * half : (at + slabs) * half].reshape(slabs, half, out.shape[2])
                if received:
                    value += got[0][index, at : at + slabs, rows, :].astype(F32)
                out[:, rows, :] = value.astype(BF)
                at += slabs


def feed_grads(first, layout, half, n1, df, g, du, *received):
    width = n1.shape[1]
    shapes = [jax.ShapeDtypeStruct((slabs, 2 * half, width), BF) for sizes in layout for slabs in sizes]
    flops = 4 * n1.shape[0] * width * g.shape[1] // 2
    return call(
        functools.partial(feed_grads_kernel, first, layout, len(received)),
        shapes, [], flops, n1, df, g, du, *received,
    )


class Near:
    axes = ("z", "y", "x", "core")
    feed_layout = [1, 1, 1, 2] * 2

    def __init__(self):
        self.at = {name: lax.axis_index(name) for name in self.axes}
        self.z = lax.axis_size("z")

    def swap(self, array, axis):
        return lax.ppermute(array, axis, [(0, 1), (1, 0)])

    def gather(self, slab):
        half = self.z // 2
        here = lax.all_gather(slab, "z", axis=0, tiled=False)
        by_y, by_x = self.swap(here, "y"), self.swap(here, "x")
        both = [self.swap(by_y[:half], "x"), self.swap(by_x[half:], "y")]
        own = [here, by_y, by_x, *both]
        return own, [self.swap(part, "core") for part in own]

    def gather_feed(self, slab):
        own, other = self.gather(slab)
        return [[p[0]] for p in []] + [[own[0]], [own[1]], [own[2]], own[3:], [other[0]], [other[1]], [other[2]], other[3:]]

    def place(self, core, y, x):
        return (core ^ self.at["core"]) * 4 + (y ^ self.at["y"]) * 2 + (x ^ self.at["x"])

    def gather_attention(self, slab):
        own, other = self.gather(slab)
        parts = jnp.stack([p for side in (own, other) for p in (side[0], side[2], side[1], jnp.concatenate(side[3:], 0))])
        order = [
            lax.dynamic_index_in_dim(parts, self.place(core, y, x), 0, keepdims=False)
            for y in range(2) for x in range(2) for core in range(2)
        ]
        return jnp.stack(order, 1).reshape((-1,) + slab.shape)

    def relative(self, natural):
        blocks = natural.reshape((self.z, 8) + natural.shape[1:])
        out = []
        for core in range(2):
            for y, x in ((0, 0), (1, 0), (0, 1), (1, 1)):
                index = (y ^ self.at["y"]) * 4 + (x ^ self.at["x"]) * 2 + (core ^ self.at["core"])
                out.append(lax.dynamic_index_in_dim(blocks, index, 1, keepdims=False))
        return out

    def up_bias(self, natural):
        return jnp.stack(self.relative(natural)).reshape(PARTS, -1)

    def up_bias_grad(self, parts):
        blocks = parts.reshape(PARTS, self.z, -1)
        order = []
        for y in range(2):
            for x in range(2):
                for core in range(2):
                    index = (core ^ self.at["core"]) * 4 + (y ^ self.at["y"]) + (x ^ self.at["x"]) * 2
                    order.append(lax.dynamic_index_in_dim(blocks, index, 0, keepdims=False))
        return jnp.stack(order, 1).reshape(self.z * 8, -1)

    def reduce(self, here, by_y, by_x, both_a, both_b):
        half = self.z // 2
        got_a, got_b = self.swap(both_a, "x"), self.swap(both_b, "y")
        by_y = by_y.at[:half].add(got_a)
        by_x = by_x.at[half:].add(got_b)
        total = here + self.swap(by_y, "y") + self.swap(by_x, "x")
        return lax.psum_scatter(total, "z", scatter_dimension=0, tiled=False)

    def reduce_feed(self, n1, df, g, du, half):
        z = self.z
        sent = feed_grads(4, [[z]] * 4, half, n1, df, g, du)
        received = self.swap(jnp.stack(sent), "core")
        return self.reduce(*feed_grads(0, [[z], [z], [z], [z // 2, z // 2]], half, n1, df, g, du, received))

    def reduce_attention(self, slabs):
        parts = self.relative(slabs)
        received = self.swap(jnp.stack(parts[4:]), "core")
        here, by_y, by_x, both = (parts[i] + received[i] for i in range(4))
        half = self.z // 2
        return self.reduce(here, by_y, by_x, both[:half], both[half:])


class Far:
    axes = ("wide", "narrow")
    feed_layout = [1] * PARTS

    def gather_attention(self, slab):
        return lax.all_gather(slab, self.axes, axis=0, tiled=False)

    def gather_feed(self, slab):
        whole = lax.all_gather(slab, self.axes, axis=0, tiled=False)
        half, width = slab.shape[0] // 2, slab.shape[1]
        up = whole[:, :half].reshape(PARTS, -1, width)
        down = whole[:, half:].reshape(PARTS, -1, width)
        both = jnp.concatenate([up, down], 1)
        return [[both[i : i + 1]] for i in range(PARTS)]

    def up_bias(self, natural):
        return natural.reshape(PARTS, -1)

    def up_bias_grad(self, parts):
        return parts.reshape(lax.axis_size("wide") * lax.axis_size("narrow"), -1)

    def reduce_attention(self, slabs):
        return lax.psum_scatter(slabs, self.axes, scatter_dimension=0, tiled=False)

    def reduce_feed(self, n1, df, g, du, half):
        devices = lax.axis_size("wide") * lax.axis_size("narrow")
        rows = g.shape[1] // PARTS
        width = n1.shape[1]
        parts = feed_grads(0, [[1]] * 4, rows, n1, df, g, du) + feed_grads(4, [[1]] * 4, rows, n1, df, g, du)
        both = jnp.concatenate(parts, 0)
        up = both[:, :rows].reshape(devices, half, width)
        down = both[:, rows:].reshape(devices, half, width)
        return lax.psum_scatter(jnp.concatenate([up, down], 1), self.axes, scatter_dimension=0, tiled=False)


SMALL_ROWS = 8


class Block:
    def __init__(self, link, shards, index):
        w_qkv, w_out, w_up, w_down, biases, gains, up_bias = (s[index] for s in shards)
        self.link = link
        self.sizes = (w_qkv.shape[1], w_out.shape[1], up_bias.shape[0])
        width = w_qkv.shape[0]
        small = jnp.concatenate([biases.reshape(-1), gains.reshape(-1), up_bias])
        small = jnp.pad(small, (0, SMALL_ROWS * width - small.shape[0])).reshape(SMALL_ROWS, width)
        self.attention_slab = jnp.concatenate([w_qkv.T, w_out.T, small], 0)
        self.feed_slab = jnp.concatenate([w_up.T, w_down], 0)

    def fetch(self):
        n_qkv, n_out, n_up = self.sizes
        slabs = self.link.gather_attention(self.attention_slab)
        devices, _, width = slabs.shape
        self.wt_qkv = slabs[:, :n_qkv].reshape(devices * n_qkv, width)
        self.wt_out = slabs[:, n_qkv : n_qkv + n_out].reshape(devices * n_out, width)
        small = slabs[:, n_qkv + n_out :].reshape(devices, -1).astype(F32)
        own = width // devices
        biases = small[:, : 6 * own].reshape(devices, 6, own).transpose(1, 0, 2).reshape(6, width)
        gains = small[:, 6 * own : 8 * own].reshape(devices, 2, own).transpose(1, 0, 2).reshape(2, width)
        self.up_bias = self.link.up_bias(small[:, 8 * own : 8 * own + n_up])
        self.qkv_bias = jnp.concatenate([biases[0], jnp.zeros((width,), F32), biases[1]])[None]
        self.vectors = jnp.concatenate([biases[2:6], gains], 0)
        self.pieces = self.link.gather_feed(self.feed_slab)

    def attend(self, x, marks):
        self.x = x
        self.qkv, self.mix, self.lse = attention_forward(x, self.wt_qkv, self.qkv_bias, marks[0], marks[1])

    def forward(self):
        (y,) = feed(self.x, self.mix, self.wt_out, self.vectors, self.up_bias, self.pieces)
        return y

    def both(self, cot):
        (y, self.n1, self.g, self.du, self.df, self.do, self.dr1, self.dm, self.small, self.up_small) = feed(
            self.x, self.mix, self.wt_out, self.vectors, self.up_bias, self.pieces, cot
        )
        return y

    def feed_grads(self):
        n_up = self.sizes[2]
        total = self.link.reduce_feed(self.n1, self.df, self.g, self.du, n_up).astype(F32)
        return total[:n_up].T, total[n_up:]

    def backward(self, marks):
        self.dqkv, self.sums = attention_backward(self.qkv, self.dm, self.mix, self.lse, marks[2], marks[3])
        return self.dr1 + mm(self.dqkv, self.wt_qkv)

    def attention_grads(self):
        n_qkv, n_out, n_up = self.sizes
        width = self.x.shape[1]
        devices = width // n_out
        dw_qkv = mm(self.dqkv, self.x, TN).astype(BF).reshape(devices, n_qkv, width)
        dw_out = mm(self.do, self.mix, TN).astype(BF).reshape(devices, n_out, width)
        biases = jnp.stack([self.sums[0, :width], self.sums[0, 2 * width :], *(self.small[i] for i in range(4))])
        gains = self.small[4:6]
        cut = lambda rows: rows.reshape(rows.shape[0], devices, n_out).transpose(1, 0, 2).reshape(devices, -1)
        small = jnp.concatenate([cut(biases), cut(gains), self.link.up_bias_grad(self.up_small)], 1)
        small = jnp.pad(small, ((0, 0), (0, SMALL_ROWS * width - small.shape[1]))).astype(BF)
        slabs = jnp.concatenate([dw_qkv, dw_out, small.reshape(devices, SMALL_ROWS, width)], 1)
        total = self.link.reduce_attention(slabs).astype(F32)
        flat = total[n_qkv + n_out :].reshape(-1)
        return (
            total[:n_qkv].T,
            total[n_qkv : n_qkv + n_out].T,
            flat[: 6 * n_out].reshape(6, n_out),
            flat[6 * n_out : 8 * n_out].reshape(2, n_out),
            flat[8 * n_out : 8 * n_out + n_up],
        )


def body(make_link, tokens, skip_tokens, cot_first, cot_second, *rest):
    *shards, lengths, segments = rest
    link = make_link()
    length = segments.shape[1]
    place = lax.broadcasted_iota(jnp.int32, (1, length), 1)
    keys = jnp.where(place < lengths[:, None], segments, -1)
    marks = (segments.reshape(length, 1), keys, segments, keys.reshape(length, 1))
    is_first = lax.broadcasted_iota(jnp.int32, (length, 1), 0) == 0

    one, two = Block(link, shards, 0), Block(link, shards, 1)
    one.fetch()
    two.fetch()
    one.attend(tokens, marks)
    out_first = one.forward()
    two.attend(jnp.where(is_first, out_first, skip_tokens), marks)
    out_second = two.both(cot_second)
    up_two, down_two = two.feed_grads()
    d_second = two.backward(marks)
    att_two = two.attention_grads()
    grad_skip = jnp.where(is_first, 0.0, d_second)
    upstream = cot_first.astype(F32) + jnp.where(is_first, d_second, 0.0)
    one.both(upstream)
    up_one, down_one = one.feed_grads()
    grad_tokens = one.backward(marks)
    att_one = one.attention_grads()
    pair = lambda i: jnp.stack([att_one[i], att_two[i]])
    return (
        out_first, out_second, grad_tokens, grad_skip,
        pair(0), pair(1), jnp.stack([up_one, up_two]), jnp.stack([down_one, down_two]),
        pair(2), pair(3), pair(4),
    )


def solution(mesh):
    wide, narrow = mesh.shape["wide"], mesh.shape["narrow"]
    if narrow == 4 and wide % 4 == 0:
        mesh = Mesh(mesh.devices.reshape(wide // 2, 2, 2, 2), Near.axes)
        make_link, every = Near, Near.axes
    else:
        make_link, every = Far, Far.axes
    rows, last, middle = P(every, None), P(None, None, every), P(None, every, None)
    return jax.shard_map(
        functools.partial(body, make_link),
        mesh=mesh,
        in_specs=(
            rows, rows, rows, rows, last, last, last, middle, last, last, P(None, every), P(every), rows,
        ),
        out_specs=(rows, rows, rows, rows, last, last, last, middle, last, last, P(None, every)),
        check_vma=False,
    )
```

time: 1490 us -> 589 us (0.40)
  waiting for transfers between devices: 772 us -> 141 us
  matrix products: 214 us -> 16.1 us
  Pallas kernels: 0 us -> 189 us
  blocking collectives: 204 us -> 44.8 us
  local copies, waits for them, and re-layouts: 180 us -> 71.2 us
    reduce_scatter x8 -> x4, waiting for transfers between devices: 473 us -> 15 us  [reduce(): return lax.psum_scatter(total, 'z', scatter_dimension=0, tiled=False)]
    pallas_call x0 -> x11, Pallas kernels: none -> 189 us  [call(): pl.pallas_call(kernel, out_shape=out_shapes, in_specs=[VMEM] * len(args),...]
    dot_general x31 -> x6, matrix products: 193 us -> 16.1 us  [mm(): return lax.dot_general(a, b, dims, preferred_element_type=F32)]
    all_gather x16 -> x2, waiting for transfers between devices: 150 us -> 0.01 us  [gather(): here = lax.all_gather(slab, 'z', axis=0, tiled=False)]
    all_to_all x8 -> x0, waiting for transfers between devices: 144 us -> none  [group_terms(): lax.all_to_all(shortened(tuple((owned_columns(matrix) for matrix in right...]
    ppermute x0 -> x56, waiting for transfers between devices: none -> 126 us  [swap(): return lax.ppermute(array, axis, [(0, 1), (1, 0)])]
    all_gather x4 -> x2, blocking collectives: 167 us -> 44.8 us  [gather(): here = lax.all_gather(slab, 'z', axis=0, tiled=False)]
    ppermute x0 -> x56, starting transfers between devices: none -> 40 us  [swap(): return lax.ppermute(array, axis, [(0, 1), (1, 0)])]
  transfers between devices with their start and end apart: 33 -> 62, of which waited for: 19 -> 21; matrix products, arithmetic and copies ran while one was open for 29% -> 20% of each run, Pallas kernels for 0% -> 16%
where the time goes in v1:
time: 589 us; the launch traced here: 578 us
  Pallas kernels  189 us (32%)
  waiting for transfers between devices  141 us (24%)
  local copies, waits for them, and re-layouts  71.2 us (12%)
  other arithmetic  60 us (10%)
  blocking collectives  44.8 us (8%)
  starting transfers between devices  40.4 us (7%)
  between operations  16.2 us (3%)
  matrix products  16.1 us (3%)
    pallas_call x11, Pallas kernels, call(): pl.pallas_call(kernel, out_shape=out_shapes, in_specs=[VMEM] * len(args),...  189 us
    ppermute x56, waiting for transfers between devices, swap(): return lax.ppermute(array, axis, [(0, 1), (1, 0)])  126 us
    all_gather x2, blocking collectives, gather(): here = lax.all_gather(slab, 'z', axis=0, tiled=False)  44.8 us
    ppermute x56, starting transfers between devices, swap(): return lax.ppermute(array, axis, [(0, 1), (1, 0)])  40 us
    unnamed x113, local copies, waits for them, and re-layouts  30.6 us
    dot_general x6, matrix products, mm(): return lax.dot_general(a, b, dims, preferred_element_type=F32)  16.1 us
    reduce_scatter x4, waiting for transfers between devices, reduce(): return lax.psum_scatter(total, 'z', scatter_dimension=0, tiled=False)  15 us
  transfers between devices with their start and end apart: 62, of which 21 were waited for; matrix products, arithmetic and copies ran while one was open for 20% of the time, Pallas kernels for 16%

profile of v1, /device:TPU:0, one launch (start us, length us, event | category | flops | bytes accessed | tf_op | source)
XLA Modules:
  0.0 578.5 jit_solution(12003806487898271884)
XLA Ops:
  14.5 26.5 %all-gather.2 = bf16[416,768]{1,0:T(8,128)(2,1)S(1)} all-gather(bf16[104,768]{1,0:T(8,128)(2,1)S(1)} %pad_maximum_fusion.12), channel_id=4, replica_groups=mesh['z'=4,'y'=2,'x'=2,'core'=2] {'z'}, dimensions={0}, use_global_device_ids=true | all-gather | bytes 798720 | tf_op jit(solution)/shard_map/all_gather | solution.py:341
  44.3 18.3 %all-gather = bf16[416,768]{1,0:T(8,128)(2,1)S(1)} all-gather(bf16[104,768]{1,0:T(8,128)(2,1)S(1)} %pad_maximum_fusion.11), channel_id=2, replica_groups=mesh['z'=4,'y'=2,'x'=2,'core'=2] {'z'}, dimensions={0}, use_global_device_ids=true | all-gather | bytes 798720 | tf_op jit(solution)/shard_map/all_gather | solution.py:341
  71.9 7.4 %collective-permute-done.1 = bf16[4,104,768]{2,1,0:T(8,128)(2,1)S(1)} collective-permute-done((bf16[4,104,768]{2,1,0:T(8,128)(2,1)S(1)}, bf16[4,104,768]{2,1,0:T(8,128)(2,1)S(1)}, u32[]{:S(2)}, u32[]{:S(2)}) %collective-permute-start.1) | collective-permute-done | bytes 639008 | tf_op jit(solution)/shard_map/ppermute | solution.py:337
  84.5 2.1 collective-permute-done.20
  91.6 2.4 collective-permute-done.3
  107.0 2.0 bitcast_dynamic-update-slice_fusion.20
  109.0 2.0 copy.97
  111.0 2.0 bitcast_dynamic-update-slice_fusion.19
  113.0 2.0 bitcast_dynamic-update-slice_fusion.18
  115.0 2.0 bitcast_dynamic-update-slice_fusion.17
  117.0 2.0 bitcast_dynamic-update-slice_fusion.16
  119.0 2.0 bitcast_dynamic-update-slice_fusion.15
  121.0 2.0 bitcast_dynamic-update-slice_fusion.14
  123.0 2.0 bitcast_dynamic-update-slice_fusion.13
  124.9 1.9 slice_convert_fusion.1
  126.8 2.0 copy.90
  128.9 4.1 slice.570
  133.0 2.4 slice.575
  135.4 2.0 slice.583
  143.9 13.5 %collective-permute-done.27.refs_7_ = bf16[4,192,768]{2,1,0:T(8,128)(2,1)} collective-permute-done((bf16[4,192,768]{2,1,0:T(8,128)(2,1)}, bf16[4,192,768]{2,1,0:T(8,128)(2,1)}, u32[]{:S(2)}, u32[]{:S(2)}) %collective-permute-start.27) | collective-permute-done | bytes 1179680 | tf_op jit(solution)/shard_map/ppermute | solution.py:337
  162.6 9.0 %collective-permute-done.11.refs_8_.refs_9_ = bf16[2,192,768]{2,1,0:T(8,128)(2,1)} collective-permute-done((bf16[2,192,768]{2,1,0:T(8,128)(2,1)S(1)}, bf16[2,192,768]{2,1,0:T(8,128)(2,1)}, u32[]{:S(2)}, u32[]{:S(2)}) %collective-permute-start.11) | collective-permute-done | bytes 589856 | tf_op jit(solution)/shard_map/ppermute | solution.py:337
  172.1 10.9 %collective-permute-done.29.refs_9_ = bf16[2,192,768]{2,1,0:T(8,128)(2,1)S(1)} collective-permute-done((bf16[2,192,768]{2,1,0:T(8,128)(2,1)S(1)}, bf16[2,192,768]{2,1,0:T(8,128)(2,1)S(1)}, u32[]{:S(2)}, u32[]{:S(2)}) %collective-permute-start.29) | collective-permute-done | bytes 589856 | tf_op jit(solution)/shard_map/ppermute | solution.py:337
  188.8 22.1 %shard_map.212 = (bf16[512,2304]{1,0:T(8,128)(2,1)}, bf16[512,768]{1,0:T(8,128)(2,1)}, f32[16,512]{1,0:T(8,128)}) custom-call(bf16[512,768]{1,0:T(8,128)(2,1)} %refs_0_.3, bf16[2304,768]{1,0:T(8,128)(2,1)} %bitcast.368, f32[1,2304]{1,0:T(1,128)} %broadcast_in_dim.41.bias, s32[512,1]{1,0:T(8,128)} %copy.93.seg_col, s32[1,512]{1,0:T(1,128)} %compare_select_fusion.key_row), custom_call_target="tpu_custom_call" | custom-call | flops 5033164800 | bytes 7517184 | tf_op jit(solution)/shard_map/pallas_call | solution.py:33
  212.2 18.5 %shard_map.213 = bf16[512,768]{1,0:T(8,128)(2,1)} custom-call(bf16[512,768]{1,0:T(8,128)(2,1)} %refs_0_.3, bf16[512,768]{1,0:T(8,128)(2,1)} %get-tuple-element.154.refs_1_.mix, bf16[768,768]{1,0:T(8,128)(2,1)} %bitcast.400, f32[6,768]{1,0:T(8,128)} %pad_maximum_fusion.14.refs_3_, f32[8,384]{1,0:T(8,128)} %stack.377.refs_4_, bf16[4,192,768]{2,1,0:T(8,128)(2,1)} %bitcast.425, ...), custom_call_target="tpu_custom_call" | custom-call | flops 6039797760 | bytes 13006848 | tf_op jit(solution)/shard_map/pallas_call | solution.py:33
  230.7 2.2 broadcast_select_fusion.1.x.refs_0_
  232.9 21.9 %shard_map.214 = (bf16[512,2304]{1,0:T(8,128)(2,1)}, bf16[512,768]{1,0:T(8,128)(2,1)}, f32[16,512]{1,0:T(8,128)}) custom-call(bf16[512,768]{1,0:T(8,128)(2,1)} %broadcast_select_fusion.1.x.refs_0_, bf16[2304,768]{1,0:T(8,128)(2,1)} %bitcast.370, f32[1,2304]{1,0:T(1,128)} %broadcast_in_dim.44.bias, s32[512,1]{1,0:T(8,128)} %copy.93.seg_col, ...), custom_call_target="tpu_custom_call" | custom-call | flops 5033164800 | bytes 7517184 | tf_op jit(solution)/shard_map/pallas_call | solution.py:33
  257.0 32.2 %shard_map.215 = (bf16[512,768]{1,0:T(8,128)(2,1)}, bf16[512,768]{1,0:T(8,128)(2,1)}, bf16[512,3072]{1,0:T(8,128)(2,1)}, bf16[512,3072]{1,0:T(8,128)(2,1)}, bf16...) custom-call(bf16[512,768]{1,0:T(8,128)(2,1)} %broadcast_select_fusio, ...), custom_call_target="tpu_custom_call" | custom-call | flops 12079595520 | bytes 24840192 | tf_op jit(solution)/shard_map/pallas_call | solution.py:33
  289.2 15.8 %shard_map.216 = (bf16[512,2304]{1,0:T(8,128)(2,1)}, f32[8,2304]{1,0:T(8,128)}) custom-call(bf16[512,2304]{1,0:T(8,128)(2,1)} %get-tuple-element.158.qkv, bf16[512,768]{1,0:T(8,128)(2,1)} %get-tuple-element.159.dmix, bf16[512,768]{1,0:T(8,128)(2,1)} %get-tuple-element.155.refs_1_.mix, f32[16,512]{1,0:T(8,128)} %get-tuple-element.160.lse_rows, ...), custom_call_target="tpu_custom_call" | custom-call | flops 8053063680 | bytes 6402048 | tf_op jit(solution)/shard_map/pallas_call | solution.py:33
  305.0 3.8 fusion.97
  308.9 2.0 broadcast_select_fusion
  310.9 31.7 %shard_map.217 = (bf16[512,768]{1,0:T(8,128)(2,1)}, bf16[512,768]{1,0:T(8,128)(2,1)}, bf16[512,3072]{1,0:T(8,128)(2,1)}, bf16[512,3072]{1,0:T(8,128)(2,1)}, bf16...) custom-call(bf16[512,768]{1,0:T(8,128)(2,1)} %refs_0_.3, ...), custom_call_target="tpu_custom_call" | custom-call | flops 12079595520 | bytes 25626624 | tf_op jit(solution)/shard_map/pallas_call | solution.py:33
  343.4 1.9 convolution_convert_fusion.3
  345.4 15.6 %shard_map.218 = (bf16[512,2304]{1,0:T(8,128)(2,1)}, f32[8,2304]{1,0:T(8,128)}) custom-call(bf16[512,2304]{1,0:T(8,128)(2,1)} %get-tuple-element.163.qkv, bf16[512,768]{1,0:T(8,128)(2,1)} %get-tuple-element.164.dmix, bf16[512,768]{1,0:T(8,128)(2,1)} %get-tuple-element.154.refs_1_.mix, f32[16,512]{1,0:T(8,128)} %get-tuple-element.165.lse_rows, ...), custom_call_target="tpu_custom_call" | custom-call | flops 8053063680 | bytes 6402048 | tf_op jit(solution)/shard_map/pallas_call | solution.py:33
  362.9 3.7 convolution_convert_fusion.1
  367.0 2.4 copy-done
  369.6 1.8 pad_maximum_fusion.4
  372.8 7.0 %shard_map.219 = (bf16[4,192,768]{2,1,0:T(8,128)(2,1)}, bf16[4,192,768]{2,1,0:T(8,128)(2,1)}, bf16[4,192,768]{2,1,0:T(8,128)(2,1)}, bf16[4,192,768]{2,1,0:T(8,128)(2,1)}) custom-call(bf16[512,768]{1,0:T(8,128)(2,1)} %get-tuple-element.175.n1, bf16[512,768]{1,0:T(8,128)(2,1)} %get-tuple-element.176.df, bf16[512,3072]{1,0:T(8,128)(2,1)} %get-tuple-element.177.g, ...), custom_call_target="tpu_custom_call" | custom-call | flops 2415919104 | bytes 12582912 | tf_op jit(solution)/shard_map/pallas_call | solution.py:33
  379.8 4.2 pad_maximum_fusion.2
  385.9 2.1 convolution_convert_fusion
  389.0 2.1 pad_maximum_fusion.5
  391.2 7.1 %shard_map.221 = (bf16[4,192,768]{2,1,0:T(8,128)(2,1)}, bf16[4,192,768]{2,1,0:T(8,128)(2,1)}, bf16[4,192,768]{2,1,0:T(8,128)(2,1)}, bf16[4,192,768]{2,1,0:T(8,128)(2,1)}) custom-call(bf16[512,768]{1,0:T(8,128)(2,1)} %get-tuple-element.188.n1, bf16[512,768]{1,0:T(8,128)(2,1)} %get-tuple-element.189.df, bf16[512,3072]{1,0:T(8,128)(2,1)} %get-tuple-element.190.g, ...), custom_call_target="tpu_custom_call" | custom-call | flops 2415919104 | bytes 12582912 | tf_op jit(solution)/shard_map/pallas_call | solution.py:33
  398.3 4.4 pad_maximum_fusion.3
  403.4 1.7 fusion.14
  406.8 8.3 %collective-permute-done.37 = bf16[2,104,768]{2,1,0:T(8,128)(2,1)S(1)} collective-permute-done((bf16[2,104,768]{2,1,0:T(8,128)(2,1)S(1)}, bf16[2,104,768]{2,1,0:T(8,128)(2,1)S(1)}, u32[]{:S(2)}, u32[]{:S(2)}) %collective-permute-start.37) | collective-permute-done | bytes 319520 | tf_op jit(solution)/shard_map/ppermute | solution.py:337
  417.1 1.7 fusion.8
  420.0 11.1 %collective-permute-done.38 = bf16[4,104,768]{2,1,0:T(8,128)(2,1)S(1)} collective-permute-done((bf16[4,104,768]{2,1,0:T(8,128)(2,1)S(1)}, bf16[4,104,768]{2,1,0:T(8,128)(2,1)S(1)}, u32[]{:S(2)}, u32[]{:S(2)}) %collective-permute-start.38) | collective-permute-done | bytes 639008 | tf_op jit(solution)/shard_map/ppermute | solution.py:337
  433.4 2.1 fusion.17
  435.6 8.3 %shard_map.220 = (bf16[4,192,768]{2,1,0:T(8,128)(2,1)}, bf16[4,192,768]{2,1,0:T(8,128)(2,1)}, bf16[4,192,768]{2,1,0:T(8,128)(2,1)}, bf16[2,192,768]{2,1,0:T(8,128)(2,1)}, bf16[2,192,768]{2,1,0:T(8,128)(2,1)}) custom-call(bf16[512,768]{1,0:T(8,128)(2,1)} %get-tuple-element.175.n1, bf16[512,768]{1,0:T(8,128)(2,1)} %get-tuple-element.176.df, ...), custom_call_target="tpu_custom_call" | custom-call | flops 2415919104 | bytes 17301504 | tf_op jit(solution)/shard_map/pallas_call | solution.py:33
  448.3 12.1 %collective-permute-done.47 = bf16[2,192,768]{2,1,0:T(8,128)(2,1)S(1)} collective-permute-done((bf16[2,192,768]{2,1,0:T(8,128)(2,1)}, bf16[2,192,768]{2,1,0:T(8,128)(2,1)S(1)}, u32[]{:S(2)}, u32[]{:S(2)}) %collective-permute-start.47) | collective-permute-done | bytes 589856 | tf_op jit(solution)/shard_map/ppermute | solution.py:337
  460.4 2.0 add_dynamic-update-slice_fusion.3
  463.7 11.3 %collective-permute-done.49 = bf16[2,192,768]{2,1,0:T(8,128)(2,1)S(1)} collective-permute-done((bf16[2,192,768]{2,1,0:T(8,128)(2,1)}, bf16[2,192,768]{2,1,0:T(8,128)(2,1)S(1)}, u32[]{:S(2)}, u32[]{:S(2)}) %collective-permute-start.49) | collective-permute-done | bytes 589856 | tf_op jit(solution)/shard_map/ppermute | solution.py:337
  475.1 2.0 add_dynamic-update-slice_fusion.2
  478.1 2.3 fusion.11
  480.5 8.3 %shard_map.222 = (bf16[4,192,768]{2,1,0:T(8,128)(2,1)}, bf16[4,192,768]{2,1,0:T(8,128)(2,1)}, bf16[4,192,768]{2,1,0:T(8,128)(2,1)}, bf16[2,192,768]{2,1,0:T(8,128)(2,1)}, bf16[2,192,768]{2,1,0:T(8,128)(2,1)}) custom-call(bf16[512,768]{1,0:T(8,128)(2,1)} %get-tuple-element.188.n1, bf16[512,768]{1,0:T(8,128)(2,1)} %get-tuple-element.189.df, ...), custom_call_target="tpu_custom_call" | custom-call | flops 2415919104 | bytes 17301504 | tf_op jit(solution)/shard_map/pallas_call | solution.py:33
  491.3 9.1 %collective-permute-done.48 = bf16[4,192,768]{2,1,0:T(8,128)(2,1)} collective-permute-done((bf16[4,192,768]{2,1,0:T(8,128)(2,1)}, bf16[4,192,768]{2,1,0:T(8,128)(2,1)}, u32[]{:S(2)}, u32[]{:S(2)}) %collective-permute-start.48) | collective-permute-done | bytes 1179680 | tf_op jit(solution)/shard_map/ppermute | solution.py:337
  500.4 2.5 collective-permute-done.50
  503.0 2.8 add_add_fusion.1
  506.0 3.2 collective-permute-done.52
  509.2 2.0 add_dynamic-update-slice_fusion.1
  513.5 2.4 add_dynamic-update-slice_fusion
  517.1 16.8 %collective-permute-done.53 = bf16[4,192,768]{2,1,0:T(8,128)(2,1)S(1)} collective-permute-done((bf16[4,192,768]{2,1,0:T(8,128)(2,1)}, bf16[4,192,768]{2,1,0:T(8,128)(2,1)S(1)}, u32[]{:S(2)}, u32[]{:S(2)}) %collective-permute-start.53) | collective-permute-done | bytes 1179680 | tf_op jit(solution)/shard_map/ppermute | solution.py:337
  535.6 2.6 add_add_fusion
  538.2 3.8 fusion.98
  551.9 14.9 %reduce-scatter.11.cloned.1.call-done = bf16[1,192,768]{2,1,0:T(8,128)(2,1)} async-done(((bf16[4,192,768]{2,1,0:T(8,128)(2,1)}), bf16[1,192,768]{2,1,0:T(8,128)(2,1)}) %reduce-scatter.11.cloned.1.call-update) | async-done | bytes 294928 | tf_op jit(solution)/shard_map/reduce_scatter | solution.py:391
  (392 shorter events, 107.9 us)
Async XLA Ops:
  7.2 59.7 %copy-start.15 = (s32[1,512]{1,0:T(1,128)S(1)}, s32[1,512]{1,0:T(1,128)}, u32[]{:S(2)}) copy-start(s32[1,512]{1,0:T(1,128)} %seg_row.3) | copy-start | bytes 6148
  7.2 95.8 %all-gather.7.cloned.1.call-start = ((), (), s32[]{:S(2)}) async-start(), calls=%async_computation.8 | async-start | bytes 1474560 | tf_op jit(solution)/shard_map/all_gather | solution.py:341
  10.0 95.6 %all-gather.9.cloned.1.call-start = ((), (), s32[]{:S(2)}) async-start(), calls=%async_computation.9 | async-start | bytes 1474560 | tf_op jit(solution)/shard_map/all_gather | solution.py:341
  41.0 29.2 %collective-permute-start.18 = (bf16[4,104,768]{2,1,0:T(8,128)(2,1)S(1)}, bf16[4,104,768]{2,1,0:T(8,128)(2,1)}, u32[]{:S(2)}, u32[]{:S(2)}) collective-permute-start(bf16[4,104,768]{2,1,0:T(8,128)(2,1)S(1)} %bitcast.384), channel_id=1, source_target_pairs={{0,2},{2,0},{1,3},{3,1},{4,6},{6,4},{5,7},{7,5},{8,10},{10,8},{9,1... | collective-permute-start | bytes 1916936 | tf_op jit(solution)/shard_map/ppermute | solution.py:337
  42.8 27.5 %collective-permute-start.19 = (bf16[4,104,768]{2,1,0:T(8,128)(2,1)S(1)}, bf16[4,104,768]{2,1,0:T(8,128)(2,1)S(1)}, u32[]{:S(2)}, u32[]{:S(2)}) collective-permute-start(bf16[4,104,768]{2,1,0:T(8,128)(2,1)S(1)} %bitcast.385), channel_id=1, source_target_pairs={{0,4},{4,0},{1,5},{5,1},{2,6},{6,2},{3,7},{7,3},{8,12},{12,8},{9,1... | collective-permute-start | bytes 1916936 | tf_op jit(solution)/shard_map/ppermute | solution.py:337
  44.2 44.0 %collective-permute-start.22 = (bf16[4,104,768]{2,1,0:T(8,128)(2,1)S(1)}, bf16[4,104,768]{2,1,0:T(8,128)(2,1)}, u32[]{:S(2)}, u32[]{:S(2)}) collective-permute-start(bf16[4,104,768]{2,1,0:T(8,128)(2,1)S(1)} %bitcast.386), channel_id=1, source_target_pairs={{0,1},{1,0},{2,3},{3,2},{4,5},{5,4},{6,7},{7,6},{8,9},{9,8},{10,11... | collective-permute-start | bytes 1916936 | tf_op jit(solution)/shard_map/ppermute | solution.py:337
  62.6 19.5 %collective-permute-start = (bf16[4,104,768]{2,1,0:T(8,128)(2,1)S(1)}, bf16[4,104,768]{2,1,0:T(8,128)(2,1)S(1)}, u32[]{:S(2)}, u32[]{:S(2)}) collective-permute-start(bf16[4,104,768]{2,1,0:T(8,128)(2,1)S(1)} %bitcast.380), channel_id=1, source_target_pairs={{0,2},{2,0},{1,3},{3,1},{4,6},{6,4},{5,7},{7,5},{8,10},{10,8},{9,1... | collective-permute-start | bytes 1916936 | tf_op jit(solution)/shard_map/ppermute | solution.py:337
  63.9 15.4 %collective-permute-start.1 = (bf16[4,104,768]{2,1,0:T(8,128)(2,1)S(1)}, bf16[4,104,768]{2,1,0:T(8,128)(2,1)S(1)}, u32[]{:S(2)}, u32[]{:S(2)}) collective-permute-start(bf16[4,104,768]{2,1,0:T(8,128)(2,1)S(1)} %bitcast.381), channel_id=1, source_target_pairs={{0,4},{4,0},{1,5},{5,1},{2,6},{6,2},{3,7},{7,3},{8,12},{12,8},{9,1... | collective-permute-start | bytes 1916936 | tf_op jit(solution)/shard_map/ppermute | solution.py:337
  66.2 477.2 %reduce-scatter.5.cloned.1.call-start = ((), (), s32[]{:S(2)}) async-start(), calls=%async_computation.4 | async-start | bytes 798720 | tf_op jit(solution)/shard_map/reduce_scatter | solution.py:391
  70.3 24.6 %collective-permute-start.4 = (bf16[4,104,768]{2,1,0:T(8,128)(2,1)S(1)}, bf16[4,104,768]{2,1,0:T(8,128)(2,1)S(1)}, u32[]{:S(2)}, u32[]{:S(2)}) collective-permute-start(bf16[4,104,768]{2,1,0:T(8,128)(2,1)S(1)} %bitcast.383), channel_id=1, source_target_pairs={{0,1},{1,0},{2,3},{3,2},{4,5},{5,4},{6,7},{7,6},{8,9},{9,8},{10,11... | collective-permute-start | bytes 1916936 | tf_op jit(solution)/shard_map/ppermute | solution.py:337
  70.3 16.3 %collective-permute-start.20 = (bf16[2,104,768]{2,1,0:T(8,128)(2,1)S(1)}, bf16[2,104,768]{2,1,0:T(8,128)(2,1)S(1)}, u32[]{:S(2)}, u32[]{:S(2)}) collective-permute-start(bf16[2,104,768]{2,1,0:T(8,128)(2,1)S(1)} %slice.581), channel_id=1, source_target_pairs={{0,2},{2,0},{1,3},{3,1},{4,6},{6,4},{5,7},{7,5},{8,10},{10,8},{9,1... | collective-permute-start | bytes 958472 | tf_op jit(solution)/shard_map/ppermute | solution.py:337
  79.3 8.9 %collective-permute-start.21 = (bf16[2,104,768]{2,1,0:T(8,128)(2,1)S(1)}, bf16[2,104,768]{2,1,0:T(8,128)(2,1)S(1)}, u32[]{:S(2)}, u32[]{:S(2)}) collective-permute-start(bf16[2,104,768]{2,1,0:T(8,128)(2,1)S(1)} %slice.582), channel_id=1, source_target_pairs={{0,4},{4,0},{1,5},{5,1},{2,6},{6,2},{3,7},{7,3},{8,12},{12,8},{9,1... | collective-permute-start | bytes 958472 | tf_op jit(solution)/shard_map/ppermute | solution.py:337
  82.1 9.5 %collective-permute-start.2 = (bf16[2,104,768]{2,1,0:T(8,128)(2,1)S(1)}, bf16[2,104,768]{2,1,0:T(8,128)(2,1)S(1)}, u32[]{:S(2)}, u32[]{:S(2)}) collective-permute-start(bf16[2,104,768]{2,1,0:T(8,128)(2,1)S(1)} %slice.568), channel_id=1, source_target_pairs={{0,2},{2,0},{1,3},{3,1},{4,6},{6,4},{5,7},{7,5},{8,10},{10,8},{9,1... | collective-permute-start | bytes 958472 | tf_op jit(solution)/shard_map/ppermute | solution.py:337
  86.6 7.4 %collective-permute-start.3 = (bf16[2,104,768]{2,1,0:T(8,128)(2,1)S(1)}, bf16[2,104,768]{2,1,0:T(8,128)(2,1)S(1)}, u32[]{:S(2)}, u32[]{:S(2)}) collective-permute-start(bf16[2,104,768]{2,1,0:T(8,128)(2,1)S(1)} %slice.569), channel_id=1, source_target_pairs={{0,4},{4,0},{1,5},{5,1},{2,6},{6,2},{3,7},{7,3},{8,12},{12,8},{9,1... | collective-permute-start | bytes 958472 | tf_op jit(solution)/shard_map/ppermute | solution.py:337
  88.2 8.1 %collective-permute-start.23 = (bf16[4,104,768]{2,1,0:T(8,128)(2,1)}, bf16[4,104,768]{2,1,0:T(8,128)(2,1)S(1)}, u32[]{:S(2)}, u32[]{:S(2)}) collective-permute-start(bf16[4,104,768]{2,1,0:T(8,128)(2,1)} %collective-permute-done.18), channel_id=1, source_target_pairs={{0,1},{1,0},{2,3},{3,2},{4,5},{5,4},{6,7},{7,6},{8,9},{9,8},{10,11... | collective-permute-start | bytes 1916936 | tf_op jit(solution)/shard_map/ppermute | solution.py:337
  88.3 8.1 %collective-permute-start.24 = (bf16[4,104,768]{2,1,0:T(8,128)(2,1)S(1)}, bf16[4,104,768]{2,1,0:T(8,128)(2,1)S(1)}, u32[]{:S(2)}, u32[]{:S(2)}) collective-permute-start(bf16[4,104,768]{2,1,0:T(8,128)(2,1)S(1)} %collective-permute-done.19), channel_id=1, source_target_pairs={{0,1},{1,0},{2,3},{3,2},{4,5},{5,4},{6,7},{7,6},{8,9},{9,8},{10,11... | collective-permute-start | bytes 1916936 | tf_op jit(solution)/shard_map/ppermute | solution.py:337
  91.6 6.8 %collective-permute-start.5 = (bf16[4,104,768]{2,1,0:T(8,128)(2,1)S(1)}, bf16[4,104,768]{2,1,0:T(8,128)(2,1)S(1)}, u32[]{:S(2)}, u32[]{:S(2)}) collective-permute-start(bf16[4,104,768]{2,1,0:T(8,128)(2,1)S(1)} %collective-permute-done), channel_id=1, source_target_pairs={{0,1},{1,0},{2,3},{3,2},{4,5},{5,4},{6,7},{7,6},{8,9},{9,8},{10,11... | collective-permute-start | bytes 1916936 | tf_op jit(solution)/shard_map/ppermute | solution.py:337
  94.0 5.4 collective-permute-start.6
  94.9 2.1 collective-permute-start.25
  96.3 1.6 collective-permute-start.26
  96.4 3.9 collective-permute-start.7
  97.0 3.3 collective-permute-start.8
  103.0 36.0 %collective-permute-start.9 = (bf16[4,192,768]{2,1,0:T(8,128)(2,1)}, bf16[4,192,768]{2,1,0:T(8,128)(2,1)}, u32[]{:S(2)}, u32[]{:S(2)}) collective-permute-start(bf16[4,192,768]{2,1,0:T(8,128)(2,1)} %bitcast.422), channel_id=1, source_target_pairs={{0,4},{4,0},{1,5},{5,1},{2,6},{6,2},{3,7},{7,3},{8,12},{12,8},{9,1... | collective-permute-start | bytes 3538952 | tf_op jit(solution)/shard_map/ppermute | solution.py:337
  104.5 36.7 %collective-permute-start.10 = (bf16[4,192,768]{2,1,0:T(8,128)(2,1)}, bf16[4,192,768]{2,1,0:T(8,128)(2,1)}, u32[]{:S(2)}, u32[]{:S(2)}) collective-permute-start(bf16[4,192,768]{2,1,0:T(8,128)(2,1)} %bitcast.423), channel_id=1, source_target_pairs={{0,2},{2,0},{1,3},{3,1},{4,6},{6,4},{5,7},{7,5},{8,10},{10,8},{9,1... | collective-permute-start | bytes 3538952 | tf_op jit(solution)/shard_map/ppermute | solution.py:337
  105.6 54.1 %collective-permute-start.13 = (bf16[4,192,768]{2,1,0:T(8,128)(2,1)}, bf16[4,192,768]{2,1,0:T(8,128)(2,1)}, u32[]{:S(2)}, u32[]{:S(2)}) collective-permute-start(bf16[4,192,768]{2,1,0:T(8,128)(2,1)} %bitcast.424), channel_id=1, source_target_pairs={{0,1},{1,0},{2,3},{3,2},{4,5},{5,4},{6,7},{7,6},{8,9},{9,8},{10,11... | collective-permute-start | bytes 3538952 | tf_op jit(solution)/shard_map/ppermute | solution.py:337
  105.6 51.8 %collective-permute-start.27 = (bf16[4,192,768]{2,1,0:T(8,128)(2,1)}, bf16[4,192,768]{2,1,0:T(8,128)(2,1)}, u32[]{:S(2)}, u32[]{:S(2)}) collective-permute-start(bf16[4,192,768]{2,1,0:T(8,128)(2,1)} %bitcast.427), channel_id=1, source_target_pairs={{0,4},{4,0},{1,5},{5,1},{2,6},{6,2},{3,7},{7,3},{8,12},{12,8},{9,1... | collective-permute-start | bytes 3538952 | tf_op jit(solution)/shard_map/ppermute | solution.py:337
  106.1 53.6 %collective-permute-start.28 = (bf16[4,192,768]{2,1,0:T(8,128)(2,1)}, bf16[4,192,768]{2,1,0:T(8,128)(2,1)}, u32[]{:S(2)}, u32[]{:S(2)}) collective-permute-start(bf16[4,192,768]{2,1,0:T(8,128)(2,1)} %bitcast.428), channel_id=1, source_target_pairs={{0,2},{2,0},{1,3},{3,1},{4,6},{6,4},{5,7},{7,5},{8,10},{10,8},{9,1... | collective-permute-start | bytes 3538952 | tf_op jit(solution)/shard_map/ppermute | solution.py:337
  140.1 31.5 %collective-permute-start.11 = (bf16[2,192,768]{2,1,0:T(8,128)(2,1)S(1)}, bf16[2,192,768]{2,1,0:T(8,128)(2,1)}, u32[]{:S(2)}, u32[]{:S(2)}) collective-permute-start(bf16[2,192,768]{2,1,0:T(8,128)(2,1)S(1)} %slice.579), channel_id=1, source_target_pairs={{0,2},{2,0},{1,3},{3,1},{4,6},{6,4},{5,7},{7,5},{8,10},{10,8},{9,1... | collective-permute-start | bytes 1769480 | tf_op jit(solution)/shard_map/ppermute | solution.py:337
  142.3 29.8 %collective-permute-start.12 = (bf16[2,192,768]{2,1,0:T(8,128)(2,1)S(1)}, bf16[2,192,768]{2,1,0:T(8,128)(2,1)}, u32[]{:S(2)}, u32[]{:S(2)}) collective-permute-start(bf16[2,192,768]{2,1,0:T(8,128)(2,1)S(1)} %slice.580), channel_id=1, source_target_pairs={{0,4},{4,0},{1,5},{5,1},{2,6},{6,2},{3,7},{7,3},{8,12},{12,8},{9,1... | collective-permute-start | bytes 1769480 | tf_op jit(solution)/shard_map/ppermute | solution.py:337
  158.5 24.5 %collective-permute-start.29 = (bf16[2,192,768]{2,1,0:T(8,128)(2,1)S(1)}, bf16[2,192,768]{2,1,0:T(8,128)(2,1)S(1)}, u32[]{:S(2)}, u32[]{:S(2)}) collective-permute-start(bf16[2,192,768]{2,1,0:T(8,128)(2,1)S(1)} %slice.592), channel_id=1, source_target_pairs={{0,2},{2,0},{1,3},{3,1},{4,6},{6,4},{5,7},{7,5},{8,10},{10,8},{9,1... | collective-permute-start | bytes 1769480 | tf_op jit(solution)/shard_map/ppermute | solution.py:337
  159.7 52.0 %collective-permute-start.14 = (bf16[4,192,768]{2,1,0:T(8,128)(2,1)}, bf16[4,192,768]{2,1,0:T(8,128)(2,1)}, u32[]{:S(2)}, u32[]{:S(2)}) collective-permute-start(bf16[4,192,768]{2,1,0:T(8,128)(2,1)} %collective-permute-done.9.refs_6_.refs_7_), channel_id=1, source_target_pairs={{0,1},{1,0},{2,3},{3,2},{4,5},{5,4},{6,7},{7,6},{8,9},{9,8},{10,11... | collective-permute-start | bytes 3538952 | tf_op jit(solution)/shard_map/ppermute | solution.py:337
  159.7 52.4 %collective-permute-start.15 = (bf16[4,192,768]{2,1,0:T(8,128)(2,1)}, bf16[4,192,768]{2,1,0:T(8,128)(2,1)}, u32[]{:S(2)}, u32[]{:S(2)}) collective-permute-start(bf16[4,192,768]{2,1,0:T(8,128)(2,1)} %collective-permute-done.10.refs_7_.refs_8_), channel_id=1, source_target_pairs={{0,1},{1,0},{2,3},{3,2},{4,5},{5,4},{6,7},{7,6},{8,9},{9,8},{10,11... | collective-permute-start | bytes 3538952 | tf_op jit(solution)/shard_map/ppermute | solution.py:337
  171.6 39.4 %collective-permute-start.30 = (bf16[2,192,768]{2,1,0:T(8,128)(2,1)S(1)}, bf16[2,192,768]{2,1,0:T(8,128)(2,1)}, u32[]{:S(2)}, u32[]{:S(2)}) collective-permute-start(bf16[2,192,768]{2,1,0:T(8,128)(2,1)S(1)} %slice.593), channel_id=1, source_target_pairs={{0,4},{4,0},{1,5},{5,1},{2,6},{6,2},{3,7},{7,3},{8,12},{12,8},{9,1... | collective-permute-start | bytes 1769480 | tf_op jit(solution)/shard_map/ppermute | solution.py:337
  172.1 39.0 %collective-permute-start.16 = (bf16[2,192,768]{2,1,0:T(8,128)(2,1)}, bf16[2,192,768]{2,1,0:T(8,128)(2,1)}, u32[]{:S(2)}, u32[]{:S(2)}) collective-permute-start(bf16[2,192,768]{2,1,0:T(8,128)(2,1)} %collective-permute-done.11.refs_8_.refs_9_), channel_id=1, source_target_pairs={{0,1},{1,0},{2,3},{3,2},{4,5},{5,4},{6,7},{7,6},{8,9},{9,8},{10,11... | collective-permute-start | bytes 1769480 | tf_op jit(solution)/shard_map/ppermute | solution.py:337
  183.0 28.6 %collective-permute-start.17 = (bf16[2,192,768]{2,1,0:T(8,128)(2,1)}, bf16[2,192,768]{2,1,0:T(8,128)(2,1)}, u32[]{:S(2)}, u32[]{:S(2)}) collective-permute-start(bf16[2,192,768]{2,1,0:T(8,128)(2,1)} %collective-permute-done.12.refs_9_.refs_10_), channel_id=1, source_target_pairs={{0,1},{1,0},{2,3},{3,2},{4,5},{5,4},{6,7},{7,6},{8,9},{9,8},{10,11... | collective-permute-start | bytes 1769480 | tf_op jit(solution)/shard_map/ppermute | solution.py:337
  211.0 43.8 %collective-permute-start.31 = (bf16[4,192,768]{2,1,0:T(8,128)(2,1)S(1)}, bf16[4,192,768]{2,1,0:T(8,128)(2,1)S(1)}, u32[]{:S(2)}, u32[]{:S(2)}) collective-permute-start(bf16[4,192,768]{2,1,0:T(8,128)(2,1)S(1)} %bitcast.430), channel_id=1, source_target_pairs={{0,1},{1,0},{2,3},{3,2},{4,5},{5,4},{6,7},{7,6},{8,9},{9,8},{10,11... | collective-permute-start | bytes 3538952 | tf_op jit(solution)/shard_map/ppermute | solution.py:337
  211.1 43.8 %collective-permute-start.32 = (bf16[4,192,768]{2,1,0:T(8,128)(2,1)}, bf16[4,192,768]{2,1,0:T(8,128)(2,1)S(1)}, u32[]{:S(2)}, u32[]{:S(2)}) collective-permute-start(bf16[4,192,768]{2,1,0:T(8,128)(2,1)} %collective-permute-done.27.refs_7_), channel_id=1, source_target_pairs={{0,1},{1,0},{2,3},{3,2},{4,5},{5,4},{6,7},{7,6},{8,9},{9,8},{10,11... | collective-permute-start | bytes 3538952 | tf_op jit(solution)/shard_map/ppermute | solution.py:337
  211.6 43.3 %collective-permute-start.33 = (bf16[4,192,768]{2,1,0:T(8,128)(2,1)}, bf16[4,192,768]{2,1,0:T(8,128)(2,1)S(1)}, u32[]{:S(2)}, u32[]{:S(2)}) collective-permute-start(bf16[4,192,768]{2,1,0:T(8,128)(2,1)} %collective-permute-done.28.refs_8_), channel_id=1, source_target_pairs={{0,1},{1,0},{2,3},{3,2},{4,5},{5,4},{6,7},{7,6},{8,9},{9,8},{10,11... | collective-permute-start | bytes 3538952 | tf_op jit(solution)/shard_map/ppermute | solution.py:337
  211.7 43.2 %collective-permute-start.34 = (bf16[2,192,768]{2,1,0:T(8,128)(2,1)S(1)}, bf16[2,192,768]{2,1,0:T(8,128)(2,1)S(1)}, u32[]{:S(2)}, u32[]{:S(2)}) collective-permute-start(bf16[2,192,768]{2,1,0:T(8,128)(2,1)S(1)} %copy-done.24), channel_id=1, source_target_pairs={{0,1},{1,0},{2,3},{3,2},{4,5},{5,4},{6,7},{7,6},{8,9},{9,8},{10,11... | collective-permute-start | bytes 1769480 | tf_op jit(solution)/shard_map/ppermute | solution.py:337
  212.1 42.7 %collective-permute-start.35 = (bf16[2,192,768]{2,1,0:T(8,128)(2,1)}, bf16[2,192,768]{2,1,0:T(8,128)(2,1)S(1)}, u32[]{:S(2)}, u32[]{:S(2)}) collective-permute-start(bf16[2,192,768]{2,1,0:T(8,128)(2,1)} %collective-permute-done.30.refs_10_), channel_id=1, source_target_pairs={{0,1},{1,0},{2,3},{3,2},{4,5},{5,4},{6,7},{7,6},{8,9},{9,8},{10,11... | collective-permute-start | bytes 1769480 | tf_op jit(solution)/shard_map/ppermute | solution.py:337
  310.9 32.5 %copy-start.29 = (bf16[512,768]{1,0:T(8,128)(2,1)S(1)}, bf16[512,768]{1,0:T(8,128)(2,1)}, u32[]{:S(2)}) copy-start(bf16[512,768]{1,0:T(8,128)(2,1)} %get-tuple-element.154.refs_1_.mix) | copy-start | bytes 2359300
  371.5 31.6 %collective-permute-start.36 = (bf16[4,4,104,768]{3,2,1,0:T(8,128)(2,1)}, bf16[4,4,104,768]{3,2,1,0:T(8,128)(2,1)}, u32[]{:S(2)}, u32[]{:S(2)}) collective-permute-start(bf16[4,4,104,768]{3,2,1,0:T(8,128)(2,1)} %pad_maximum_fusion.4), channel_id=1, source_target_pairs={{0,1},{1,0},{2,3},{3,2},{4,5},{5,4},{6,7},{7,6},{8,9},{9,8},{10,11... | collective-permute-start | bytes 7667720 | tf_op jit(solution)/shard_map/ppermute | solution.py:337
  384.0 51.6 %collective-permute-start.46 = (bf16[4,4,192,768]{3,2,1,0:T(8,128)(2,1)}, bf16[4,4,192,768]{3,2,1,0:T(8,128)(2,1)}, u32[]{:S(2)}, u32[]{:S(2)}) collective-permute-start(bf16[4,4,192,768]{3,2,1,0:T(8,128)(2,1)} %pad_maximum_fusion.2), channel_id=1, source_target_pairs={{0,1},{1,0},{2,3},{3,2},{4,5},{5,4},{6,7},{7,6},{8,9},{9,8},{10,11... | collective-permute-start | bytes 14155784 | tf_op jit(solution)/shard_map/ppermute | solution.py:337
  391.1 26.0 %collective-permute-start.41 = (bf16[4,4,104,768]{3,2,1,0:T(8,128)(2,1)}, bf16[4,4,104,768]{3,2,1,0:T(8,128)(2,1)}, u32[]{:S(2)}, u32[]{:S(2)}) collective-permute-start(bf16[4,4,104,768]{3,2,1,0:T(8,128)(2,1)} %pad_maximum_fusion.5), channel_id=1, source_target_pairs={{0,1},{1,0},{2,3},{3,2},{4,5},{5,4},{6,7},{7,6},{8,9},{9,8},{10,11... | collective-permute-start | bytes 7667720 | tf_op jit(solution)/shard_map/ppermute | solution.py:337
  402.6 77.8 %collective-permute-start.51 = (bf16[4,4,192,768]{3,2,1,0:T(8,128)(2,1)}, bf16[4,4,192,768]{3,2,1,0:T(8,128)(2,1)}, u32[]{:S(2)}, u32[]{:S(2)}) collective-permute-start(bf16[4,4,192,768]{3,2,1,0:T(8,128)(2,1)} %pad_maximum_fusion.3), channel_id=1, source_target_pairs={{0,1},{1,0},{2,3},{3,2},{4,5},{5,4},{6,7},{7,6},{8,9},{9,8},{10,11... | collective-permute-start | bytes 14155784 | tf_op jit(solution)/shard_map/ppermute | solution.py:337
  405.2 9.9 %collective-permute-start.37 = (bf16[2,104,768]{2,1,0:T(8,128)(2,1)S(1)}, bf16[2,104,768]{2,1,0:T(8,128)(2,1)S(1)}, u32[]{:S(2)}, u32[]{:S(2)}) collective-permute-start(bf16[2,104,768]{2,1,0:T(8,128)(2,1)S(1)} %get-tuple-element.268), channel_id=1, source_target_pairs={{0,2},{2,0},{1,3},{3,1},{4,6},{6,4},{5,7},{7,5},{8,10},{10,8},{9,1... | collective-permute-start | bytes 958472 | tf_op jit(solution)/shard_map/ppermute | solution.py:337
  406.3 9.6 %collective-permute-start.39 = (bf16[2,104,768]{2,1,0:T(8,128)(2,1)S(1)}, bf16[2,104,768]{2,1,0:T(8,128)(2,1)S(1)}, u32[]{:S(2)}, u32[]{:S(2)}) collective-permute-start(bf16[2,104,768]{2,1,0:T(8,128)(2,1)S(1)} %get-tuple-element.269), channel_id=1, source_target_pairs={{0,4},{4,0},{1,5},{5,1},{2,6},{6,2},{3,7},{7,3},{8,12},{12,8},{9,1... | collective-permute-start | bytes 958472 | tf_op jit(solution)/shard_map/ppermute | solution.py:337
  415.2 15.9 %collective-permute-start.38 = (bf16[4,104,768]{2,1,0:T(8,128)(2,1)S(1)}, bf16[4,104,768]{2,1,0:T(8,128)(2,1)S(1)}, u32[]{:S(2)}, u32[]{:S(2)}) collective-permute-start(bf16[4,104,768]{2,1,0:T(8,128)(2,1)S(1)} %fusion.29), channel_id=1, source_target_pairs={{0,4},{4,0},{1,5},{5,1},{2,6},{6,2},{3,7},{7,3},{8,12},{12,8},{9,1... | collective-permute-start | bytes 1916936 | tf_op jit(solution)/shard_map/ppermute | solution.py:337
  416.1 17.4 %collective-permute-start.40 = (bf16[4,104,768]{2,1,0:T(8,128)(2,1)S(1)}, bf16[4,104,768]{2,1,0:T(8,128)(2,1)S(1)}, u32[]{:S(2)}, u32[]{:S(2)}) collective-permute-start(bf16[4,104,768]{2,1,0:T(8,128)(2,1)S(1)} %fusion.28), channel_id=1, source_target_pairs={{0,2},{2,0},{1,3},{3,1},{4,6},{6,4},{5,7},{7,5},{8,10},{10,8},{9,1... | collective-permute-start | bytes 1916936 | tf_op jit(solution)/shard_map/ppermute | solution.py:337
  418.9 26.0 %collective-permute-start.42 = (bf16[2,104,768]{2,1,0:T(8,128)(2,1)S(1)}, bf16[2,104,768]{2,1,0:T(8,128)(2,1)S(1)}, u32[]{:S(2)}, u32[]{:S(2)}) collective-permute-start(bf16[2,104,768]{2,1,0:T(8,128)(2,1)S(1)} %get-tuple-element.270), channel_id=1, source_target_pairs={{0,2},{2,0},{1,3},{3,1},{4,6},{6,4},{5,7},{7,5},{8,10},{10,8},{9,1... | collective-permute-start | bytes 958472 | tf_op jit(solution)/shard_map/ppermute | solution.py:337
  431.1 16.0 %collective-permute-start.44 = (bf16[2,104,768]{2,1,0:T(8,128)(2,1)S(1)}, bf16[2,104,768]{2,1,0:T(8,128)(2,1)S(1)}, u32[]{:S(2)}, u32[]{:S(2)}) collective-permute-start(bf16[2,104,768]{2,1,0:T(8,128)(2,1)S(1)} %get-tuple-element.271), channel_id=1, source_target_pairs={{0,4},{4,0},{1,5},{5,1},{2,6},{6,2},{3,7},{7,3},{8,12},{12,8},{9,1... | collective-permute-start | bytes 958472 | tf_op jit(solution)/shard_map/ppermute | solution.py:337
  435.5 108.8 %reduce-scatter.7.cloned.1.call-start = ((), (), s32[]{:S(2)}) async-start(), calls=%async_computation.5 | async-start | bytes 798720 | tf_op jit(solution)/shard_map/reduce_scatter | solution.py:391
  443.9 16.5 %collective-permute-start.47 = (bf16[2,192,768]{2,1,0:T(8,128)(2,1)}, bf16[2,192,768]{2,1,0:T(8,128)(2,1)S(1)}, u32[]{:S(2)}, u32[]{:S(2)}) collective-permute-start(bf16[2,192,768]{2,1,0:T(8,128)(2,1)} %get-tuple-element.185), channel_id=1, source_target_pairs={{0,2},{2,0},{1,3},{3,1},{4,6},{6,4},{5,7},{7,5},{8,10},{10,8},{9,1... | collective-permute-start | bytes 1769480 | tf_op jit(solution)/shard_map/ppermute | solution.py:337
  445.0 33.0 %collective-permute-start.43 = (bf16[4,104,768]{2,1,0:T(8,128)(2,1)S(1)}, bf16[4,104,768]{2,1,0:T(8,128)(2,1)S(1)}, u32[]{:S(2)}, u32[]{:S(2)}) collective-permute-start(bf16[4,104,768]{2,1,0:T(8,128)(2,1)S(1)} %fusion.27), channel_id=1, source_target_pairs={{0,4},{4,0},{1,5},{5,1},{2,6},{6,2},{3,7},{7,3},{8,12},{12,8},{9,1... | collective-permute-start | bytes 1916936 | tf_op jit(solution)/shard_map/ppermute | solution.py:337
  446.6 28.5 %collective-permute-start.49 = (bf16[2,192,768]{2,1,0:T(8,128)(2,1)}, bf16[2,192,768]{2,1,0:T(8,128)(2,1)S(1)}, u32[]{:S(2)}, u32[]{:S(2)}) collective-permute-start(bf16[2,192,768]{2,1,0:T(8,128)(2,1)} %get-tuple-element.187), channel_id=1, source_target_pairs={{0,4},{4,0},{1,5},{5,1},{2,6},{6,2},{3,7},{7,3},{8,12},{12,8},{9,1... | collective-permute-start | bytes 1769480 | tf_op jit(solution)/shard_map/ppermute | solution.py:337
  447.2 30.8 %collective-permute-start.45 = (bf16[4,104,768]{2,1,0:T(8,128)(2,1)S(1)}, bf16[4,104,768]{2,1,0:T(8,128)(2,1)S(1)}, u32[]{:S(2)}, u32[]{:S(2)}) collective-permute-start(bf16[4,104,768]{2,1,0:T(8,128)(2,1)S(1)} %fusion.26), channel_id=1, source_target_pairs={{0,2},{2,0},{1,3},{3,1},{4,6},{6,4},{5,7},{7,5},{8,10},{10,8},{9,1... | collective-permute-start | bytes 1916936 | tf_op jit(solution)/shard_map/ppermute | solution.py:337
  462.4 38.1 %collective-permute-start.48 = (bf16[4,192,768]{2,1,0:T(8,128)(2,1)}, bf16[4,192,768]{2,1,0:T(8,128)(2,1)}, u32[]{:S(2)}, u32[]{:S(2)}) collective-permute-start(bf16[4,192,768]{2,1,0:T(8,128)(2,1)} %add_dynamic-update-slice_fusion.3), channel_id=1, source_target_pairs={{0,4},{4,0},{1,5},{5,1},{2,6},{6,2},{3,7},{7,3},{8,12},{12,8},{9,1... | collective-permute-start | bytes 3538952 | tf_op jit(solution)/shard_map/ppermute | solution.py:337
  477.1 25.9 %collective-permute-start.50 = (bf16[4,192,768]{2,1,0:T(8,128)(2,1)}, bf16[4,192,768]{2,1,0:T(8,128)(2,1)}, u32[]{:S(2)}, u32[]{:S(2)}) collective-permute-start(bf16[4,192,768]{2,1,0:T(8,128)(2,1)} %add_dynamic-update-slice_fusion.2), channel_id=1, source_target_pairs={{0,2},{2,0},{1,3},{3,1},{4,6},{6,4},{5,7},{7,5},{8,10},{10,8},{9,1... | collective-permute-start | bytes 3538952 | tf_op jit(solution)/shard_map/ppermute | solution.py:337
  480.4 70.4 %reduce-scatter.9.cloned.1.call-start = ((), (), s32[]{:S(2)}) async-start(), calls=%async_computation.6 | async-start | bytes 1474560 | tf_op jit(solution)/shard_map/reduce_scatter | solution.py:391
  488.8 20.4 %collective-permute-start.52 = (bf16[2,192,768]{2,1,0:T(8,128)(2,1)}, bf16[2,192,768]{2,1,0:T(8,128)(2,1)S(1)}, u32[]{:S(2)}, u32[]{:S(2)}) collective-permute-start(bf16[2,192,768]{2,1,0:T(8,128)(2,1)} %get-tuple-element.198), channel_id=1, source_target_pairs={{0,2},{2,0},{1,3},{3,1},{4,6},{6,4},{5,7},{7,5},{8,10},{10,8},{9,1... | collective-permute-start | bytes 1769480 | tf_op jit(solution)/shard_map/ppermute | solution.py:337
  489.8 22.8 %collective-permute-start.54 = (bf16[2,192,768]{2,1,0:T(8,128)(2,1)}, bf16[2,192,768]{2,1,0:T(8,128)(2,1)S(1)}, u32[]{:S(2)}, u32[]{:S(2)}) collective-permute-start(bf16[2,192,768]{2,1,0:T(8,128)(2,1)} %get-tuple-element.200), channel_id=1, source_target_pairs={{0,4},{4,0},{1,5},{5,1},{2,6},{6,2},{3,7},{7,3},{8,12},{12,8},{9,1... | collective-permute-start | bytes 1769480 | tf_op jit(solution)/shard_map/ppermute | solution.py:337
  505.8 61.0 %reduce-scatter.11.cloned.1.call-start = ((), (), s32[]{:S(2)}) async-start(), calls=%async_computation.7 | async-start | bytes 1474560 | tf_op jit(solution)/shard_map/reduce_scatter | solution.py:391
  511.2 22.7 %collective-permute-start.53 = (bf16[4,192,768]{2,1,0:T(8,128)(2,1)}, bf16[4,192,768]{2,1,0:T(8,128)(2,1)S(1)}, u32[]{:S(2)}, u32[]{:S(2)}) collective-permute-start(bf16[4,192,768]{2,1,0:T(8,128)(2,1)} %add_dynamic-update-slice_fusion.1), channel_id=1, source_target_pairs={{0,4},{4,0},{1,5},{5,1},{2,6},{6,2},{3,7},{7,3},{8,12},{12,8},{9,1... | collective-permute-start | bytes 3538952 | tf_op jit(solution)/shard_map/ppermute | solution.py:337
  515.8 19.8 %collective-permute-start.55 = (bf16[4,192,768]{2,1,0:T(8,128)(2,1)}, bf16[4,192,768]{2,1,0:T(8,128)(2,1)S(1)}, u32[]{:S(2)}, u32[]{:S(2)}) collective-permute-start(bf16[4,192,768]{2,1,0:T(8,128)(2,1)} %add_dynamic-update-slice_fusion), channel_id=1, source_target_pairs={{0,2},{2,0},{1,3},{3,1},{4,6},{6,4},{5,7},{7,5},{8,10},{10,8},{9,1... | collective-permute-start | bytes 3538952 | tf_op jit(solution)/shard_map/ppermute | solution.py:337
  (34 other events, 314.6 us)
Sparse Core Ops, SparseCore 0:
  10.2 40.7 all-gather.6
  66.3 28.8 all-gather.8
  435.7 22.1 reduce-scatter.4
  480.5 22.0 reduce-scatter.6
  505.9 28.4 reduce-scatter.8
  538.3 28.4 reduce-scatter.10

commit v2 on v1

v2 whole, which is shorter than its diff:
```python
import functools
import math

import jax
import jax.numpy as jnp
from jax import lax
from jax.experimental import pallas as pl
from jax.experimental.pallas import tpu as pltpu
from jax.sharding import Mesh, PartitionSpec as P

HEADS = 12
HEAD_DIM = 64
EPSILON = 1e-12
MASKED = -1e30
BF = jnp.bfloat16
F32 = jnp.float32
NT = (((1,), (1,)), ((), ()))
TN = (((0,), (0,)), ((), ()))
NN = (((1,), (0,)), ((), ()))
PARTS = 8
LANES = 128
SMALL_ROWS = 16
VMEM = pl.BlockSpec(memory_space=pltpu.VMEM)
SMEM = pl.BlockSpec(memory_space=pltpu.SMEM)


def mm(a, b, dims=NN):
    return lax.dot_general(a, b, dims, preferred_element_type=F32)


def shape(rows, cols, dtype=BF):
    return jax.ShapeDtypeStruct((rows, cols), dtype)


def call(kernel, out_shapes, scratch, *args, far=()):
    return list(pl.pallas_call(
        kernel,
        out_shape=out_shapes,
        in_specs=[SMEM if a.ndim == 1 else VMEM for a in args] + [pl.BlockSpec(memory_space=pl.ANY)] * len(far),
        out_specs=[VMEM] * len(out_shapes),
        scratch_shapes=scratch,
        compiler_params=pltpu.CompilerParams(vmem_limit_bytes=VMEM_BYTES),
    )(*args, *far))


VMEM_BYTES = 56 * 1024 * 1024


def windows(length):
    tiles = length // LANES
    return [
        (t, max(0, t - 1) * LANES, min(tiles, t + 2) * LANES) for t in range(tiles)
    ]


def far_place(at, part):
    return (at[0] ^ (part % 2)) * 4 + (at[1] ^ (part // 2 % 2)) * 2 + (at[2] ^ (part // 4))


def assemble(slabs, depth, at, pieces, wt, wt_out, small, up_bias, all_qkv, all_out, landing, sems):
    width = wt.shape[1]
    n_qkv, n_out = 3 * width // (PARTS * depth), width // (PARTS * depth)
    rest = n_qkv + n_out
    rows = landing.shape[1]
    copies, done = [], 0
    for i, piece in enumerate(pieces):
        n = piece.shape[0]
        copies.append(pltpu.make_async_copy(piece.at[:, pl.ds(0, rows), :], landing.at[pl.ds(done, n)], sems.at[i]))
        copies[-1].start()
        done += n
    small[...] = jnp.zeros_like(small)
    up_bias[...] = jnp.zeros_like(up_bias)
    done = 0
    for index, (piece, copy) in enumerate(zip(pieces, copies)):
        copy.wait()
        for i in range(piece.shape[0]):
            if slabs:
                part, first = slabs[index]
                device = (first + i) * PARTS + far_place(at, part)
            else:
                part, device = i // depth, i
            slab = landing[done].astype(F32)
            done += 1
            all_qkv[pl.ds(pl.multiple_of(device * n_qkv, 8), n_qkv), :] = slab[:n_qkv]
            all_out[pl.ds(pl.multiple_of(device * n_out, 8), n_out), :] = slab[n_qkv:rest]
            small[...] += slab[rest : rest + 8]
            line = slab[rest + 8 : rest + 9]
            if not slabs:
                shift = (i % depth - i // PARTS) * (up_bias.shape[1] // depth)
                line = pltpu.roll(line, shift % width, 1)
            up_bias[part : part + 1, :] += line[:, : up_bias.shape[1]]
    wt[...] = all_qkv[...].astype(BF)
    wt_out[...] = all_out[...].astype(BF)


def attention_forward_kernel(slabs, depth, x, seg_row, key_col, *refs):
    refs = list(refs)
    length, width = x.shape
    if slabs is None:
        wt, small, qkv, mix, lse_rows, mask = refs
    else:
        count = len(slabs) or 1
        at, pieces, refs = refs[0], refs[1 : 1 + count], refs[1 + count :]
        qkv, mix, lse_rows, wt, wt_out, small, up_bias, mask, all_qkv, all_out, landing, sems = refs
        assemble(slabs, depth, at, pieces, wt, wt_out, small, up_bias, all_qkv, all_out, landing, sems)
    for part in range(3):
        cols = slice(part * width, (part + 1) * width)
        out = mm(x[...], wt[cols, :], NT)
        if part != 1:
            out += small[part // 2 : part // 2 + 1, :]
        qkv[:, cols] = out.astype(BF)
    for t, low, high in windows(length):
        keys = lax.broadcasted_iota(jnp.int32, (high - low, LANES), 0) + low
        rows = lax.broadcasted_iota(jnp.int32, (high - low, LANES), 1) + t * LANES
        same = key_col[low:high, :] == seg_row[:, t * LANES : (t + 1) * LANES]
        mask[t, : high - low, :] = jnp.where(same | (rows == keys), 0.0, MASKED)

    def pair(p, carry):
        at_q = pl.multiple_of(p * LANES, LANES)
        at_k = pl.multiple_of(at_q + width, LANES)
        at_v = pl.multiple_of(at_q + 2 * width, LANES)
        lane = lax.broadcasted_iota(jnp.int32, (LANES, LANES), 1)
        for t, low, high in windows(length):
            here = slice(t * LANES, (t + 1) * LANES)
            q = qkv[here, pl.ds(at_q, LANES)] * HEAD_DIM ** (-0.5)
            k = qkv[low:high, pl.ds(at_k, LANES)]
            v = qkv[low:high, pl.ds(at_v, LANES)]
            outs = []
            for h in range(2):
                mine = (lane < HEAD_DIM) == (h == 0)
                s = mm(k, jnp.where(mine, q, 0).astype(BF), NT) + mask[t, : high - low, :]
                top = jnp.max(s, 0, keepdims=True)
                e = jnp.exp(s - top)
                total = jnp.sum(e, 0, keepdims=True)
                outs.append(mm((e * (1.0 / total)).astype(BF), v, TN))
                lse_rows[2 * p + h, :, here] = top + jnp.log(total)
            mix[here, pl.ds(at_q, LANES)] = jnp.where(lane < HEAD_DIM, outs[0], outs[1]).astype(BF)
        return carry

    lax.fori_loop(0, width // LANES, pair, 0)


def attention_forward(x, marks, weights, at=None, slabs=None, depth=0, rows_up=0):
    length, width = x.shape
    shapes = [shape(length, 3 * width), shape(length, width), jax.ShapeDtypeStruct((HEADS, 1, length), F32)]
    scratch = [pltpu.VMEM((length // LANES, 3 * LANES, LANES), F32)]
    args, far = list(weights), []
    if slabs is not None:
        args, far = [at], args
        shapes += [
            shape(3 * width, width), shape(width, width), shape(8, width, F32), shape(PARTS, depth * rows_up, F32),
        ]
        rows = 4 * width // (PARTS * depth) + SMALL_ROWS
        scratch += [
            pltpu.VMEM((3 * width, width), F32), pltpu.VMEM((width, width), F32),
            pltpu.VMEM((PARTS * depth, rows, width), BF), pltpu.SemaphoreType.DMA((len(far),)),
        ]
    return call(
        functools.partial(attention_forward_kernel, slabs, depth),
        shapes, scratch, x, marks[0], marks[1], *args, far=far,
    )


def attention_backward_kernel(halves, fix, clear_first, qkv, mix, lse_rows, seg_row, key_col, wt, *refs):
    refs = list(refs)
    dmix, refs = refs[:halves], refs[halves:]
    dr1, refs = refs[:halves], refs[halves:]
    if fix:
        dmix_fix, dr1_fix, *refs = refs
    dqkv, sums, dx, first, mask, dq_sum = refs
    length, width = mix.shape
    for t, low, high in windows(length):
        keys = lax.broadcasted_iota(jnp.int32, (high - low, LANES), 0) + low
        rows = lax.broadcasted_iota(jnp.int32, (high - low, LANES), 1) + t * LANES
        same = key_col[low:high, :] == seg_row[:, t * LANES : (t + 1) * LANES]
        mask[t, : high - low, :] = jnp.where(same | (rows == keys), 0.0, MASKED)

    def pair(p, carry):
        at = pl.multiple_of(p * LANES, LANES)
        at_k = pl.multiple_of(at + width, LANES)
        at_v = pl.multiple_of(at + 2 * width, LANES)
        lane = lax.broadcasted_iota(jnp.int32, (length, LANES), 1)
        q = qkv[:, pl.ds(at, LANES)] * HEAD_DIM ** (-0.5)
        dm = jnp.concatenate([half[:, pl.ds(at, LANES)] for half in dmix], 0)
        if fix:
            n = dmix_fix.shape[0]
            dm = jnp.concatenate([dm[:n] + dmix_fix[:, pl.ds(at, LANES)], dm[n:]], 0)
        product = dm.astype(F32) * mix[:, pl.ds(at, LANES)].astype(F32)
        ones_lane = lax.broadcasted_iota(jnp.int32, (8, LANES), 1)
        q_h, dm_h, lse_h, delta_h = [], [], [], []
        for h in range(2):
            mine = (lane < HEAD_DIM) == (h == 0)
            q_h.append(jnp.where(mine, q, 0).astype(BF))
            dm_h.append(jnp.where(mine, dm, 0).astype(BF))
            picks = jnp.where((ones_lane < HEAD_DIM) == (h == 0), 1.0, 0.0)
            delta_h.append(
                lax.dot_general(picks, product, NT, precision=lax.Precision.HIGHEST, preferred_element_type=F32)[:1, :]
            )
            lse_h.append(lse_rows[2 * p + h])
        dq_sum[...] = jnp.zeros_like(dq_sum)
        for t, low, high in windows(length):
            here = slice(t * LANES, (t + 1) * LANES)
            k = qkv[here, pl.ds(at_k, LANES)]
            v = qkv[here, pl.ds(at_v, LANES)]
            dk = jnp.zeros((LANES, LANES), F32)
            dv = jnp.zeros((LANES, LANES), F32)
            dq = jnp.zeros((high - low, LANES), F32)
            cover = jnp.concatenate(
                [
                    mask[r, t * LANES - low_r : (t + 1) * LANES - low_r, :]
                    for r, low_r, _ in windows(length)
                    if low <= r * LANES < high
                ],
                1,
            )
            for h in range(2):
                mine = (lane[:LANES] < HEAD_DIM) == (h == 0)
                q_one, dm_one = q_h[h][low:high], dm_h[h][low:high]
                s = mm(k, q_one, NT) + cover
                a = jnp.exp(s - lse_h[h][:, low:high])
                da = mm(v, dm_one, NT)
                ds = (a * (da - delta_h[h][:, low:high])).astype(BF)
                dv += mm(a.astype(BF), dm_one)
                dk += mm(ds, q_one)
                dq += mm(ds, jnp.where(mine, k, 0).astype(BF), TN)
            dqkv[here, pl.ds(at_k, LANES)] = dk.astype(BF)
            dqkv[here, pl.ds(at_v, LANES)] = dv.astype(BF)
            dq_sum[low:high, :] += dq
        dqkv[:, pl.ds(at, LANES)] = (dq_sum[...] * HEAD_DIM ** (-0.5)).astype(BF)
        return carry

    lax.fori_loop(0, width // LANES, pair, 0)
    sums[...] = jnp.zeros_like(sums)
    for row, part in ((0, 0), (1, 2)):
        cols = slice(part * width, (part + 1) * width)
        sums[row : row + 1, :] = mm(jnp.ones((8, length), BF), dqkv[:, cols])[:1, :]
    count = length // halves
    for i in range(halves):
        rows = slice(i * count, (i + 1) * count)
        out = mm(dqkv[rows, :], wt[...]) + dr1[i][...]
        if i == 0:
            if fix:
                n = dr1_fix.shape[0]
                out = jnp.concatenate([out[:n] + dr1_fix[...], out[n:]], 0)
            first[...] = out[: first.shape[0]]
            if clear_first:
                out = jnp.where(lax.broadcasted_iota(jnp.int32, out.shape, 0) == 0, 0.0, out)
        dx[rows, :] = out


def attention_backward(qkv, mix, lse_rows, marks, wt, dmix, dr1, fix=(), clear_first=False):
    length, width = mix.shape
    shapes = [shape(length, 3 * width), shape(8, width, F32), shape(length, width, F32), shape(16, width, F32)]
    scratch = [
        pltpu.VMEM((length // LANES, 3 * LANES, LANES), F32),
        pltpu.VMEM((length, LANES), F32),
    ]
    return call(
        functools.partial(attention_backward_kernel, len(dmix), bool(fix), clear_first),
        shapes, scratch, qkv, mix, lse_rows, marks[0], marks[1], wt, *dmix, *dr1, *fix,
    )


def attention_grads_kernel(depth, n_small, natural, at, dqkv, x, do, mix, *refs):
    refs = list(refs)
    smalls, ups, refs = refs[:n_small], refs[n_small : 2 * n_small - 1], refs[2 * n_small - 1 :]
    sent, here, by_y, by_x, both_a, both_b, all_qkv, all_out, lines = refs
    width = x.shape[1]
    n_qkv, n_out = 3 * width // (PARTS * depth), width // (PARTS * depth)
    for part in range(3):
        rows = slice(part * width, (part + 1) * width)
        all_qkv[rows, :] = mm(dqkv[:, rows], x[...], TN)
    all_out[...] = mm(do[...], mix[...], TN)
    small = sum(s[...] for s in smalls)
    up = sum(u[...] for u in ups)
    up = jnp.concatenate([up, jnp.zeros((PARTS, width - up.shape[1]), F32)], 1)
    for part in range(PARTS):
        lines[part] = up[part : part + 1]
    half = both_a.shape[0]
    for part in (4, 5, 6, 7, 3, 1, 2, 0):
        place = far_place(at, part)
        line = lax.broadcasted_iota(jnp.int32, (SMALL_ROWS - 8, width), 0) == 0
        for i in range(depth):
            device = i * PARTS + place
            tail = [small, jnp.where(line, lines[lax.div(device, depth) if natural else part], 0.0)]
            slab = jnp.concatenate(
                [
                    all_qkv[pl.ds(pl.multiple_of(device * n_qkv, 8), n_qkv), :],
                    all_out[pl.ds(pl.multiple_of(device * n_out, 8), n_out), :],
                    *tail,
                ],
                0,
            ).astype(BF)
            if part > 3:
                sent[part - 4, i] = slab
            elif part == 3:
                (both_a if i < half else both_b)[i % half] = slab
            else:
                (here, by_y, by_x)[part][i] = slab


def attention_grads(depth, at, natural, dqkv, x, do, mix, smalls, ups):
    length, width = x.shape
    rows = 4 * width // (PARTS * depth) + SMALL_ROWS
    out = lambda *lead: jax.ShapeDtypeStruct((*lead, rows, width), BF)
    shapes = [out(4, depth), out(depth), out(depth), out(depth), out(depth // 2), out(depth // 2)]
    scratch = [
        pltpu.VMEM((3 * width, width), F32), pltpu.VMEM((width, width), F32), pltpu.VMEM((PARTS, 1, width), F32),
    ]
    return call(
        functools.partial(attention_grads_kernel, depth, len(smalls), natural),
        shapes, scratch, at, dqkv, x, do, mix, *smalls, *ups,
    )


def norm(values):
    centred = values - jnp.mean(values, -1, keepdims=True)
    inverse = lax.rsqrt(jnp.mean(centred * centred, -1, keepdims=True) + EPSILON)
    return centred * inverse, inverse


def norm_back(upstream, scaled, inverse, gain):
    through = upstream * gain
    return inverse * (
        through
        - jnp.mean(through, -1, keepdims=True)
        - scaled * jnp.mean(through * scaled, -1, keepdims=True)
    )


def normal_terms(u):
    size = jnp.abs(u) * (1.0 / math.sqrt(2.0))
    bell = jnp.exp(-(size * size))
    s = 1.0 / (1.0 + 0.3275911 * size)
    tail = s * (0.5 * 0.254829592 + s * (0.5 * -0.284496736 + s * (0.5 * 1.421413741 + s * (0.5 * -1.453152027 + s * (0.5 * 1.061405429)))))
    tail = tail * bell
    return jnp.where(u > 0, 1.0 - tail, tail), bell * (1.0 / math.sqrt(2.0 * math.pi))


def feed_kernel(pieces_at, skip_rows, start, clear_first, backward, *refs):
    refs = list(refs)
    take = lambda n: [refs.pop(0) for _ in range(n)]
    x, mix, w_out, vectors, up_bias = take(5)
    (cot,) = take(1) if backward else (None,)
    pieces = take(len(pieces_at))
    if backward:
        y, n1_out, g_out, du_out, df_out, do_out, dr1_out, dm_out, small, up_small, slabs, sems, slope = refs
        small[...] = jnp.zeros_like(small)
        up_small[...] = jnp.zeros_like(up_small)
    else:
        y, slabs, sems = refs
    count, width = y.shape
    half = slabs.shape[1] // 2
    each = slabs.shape[0] // PARTS
    copies = []
    for i, (piece, at) in enumerate(zip(pieces, pieces_at)):
        n = piece.shape[0]
        copies.append(
            pltpu.make_async_copy(piece.at[:, pl.ds(skip_rows, 2 * half), :], slabs.at[pl.ds(at, n)], sems.at[i])
        )
        copies[-1].start()

    def weights(part, lower):
        for copy, at in zip(list(copies), pieces_at):
            if copy is not None and at < (part + 1) * each:
                copy.wait()
                copies[copies.index(copy)] = None
        top = half if lower else 0
        return slabs[part * each : (part + 1) * each, top : top + half, :].reshape(each * half, width)

    b_out, b_down, shift_one, shift_two, gain_one, gain_two = (vectors[i : i + 1, :] for i in range(2, 8))
    here = slice(start, start + count)
    r1 = x[here, :].astype(F32) + mm(mix[here, :], w_out[...], NT) + b_out
    z1, q1 = norm(r1)
    n1 = (z1 * gain_one + shift_one).astype(BF)
    acc = n1.astype(F32) + b_down
    for part in range(PARTS):
        u = mm(n1, weights(part, False), NT) + up_bias[part : part + 1, :]
        size = u.shape[1]
        cols = slice(part * size, (part + 1) * size)
        big, bell = normal_terms(u)
        g = (u * big).astype(BF)
        if backward:
            g_out[:, cols] = g
            slope[:, cols] = big + u * bell
        acc += mm(g, weights(part, True))
    z2, q2 = norm(acc)
    y[...] = (z2 * gain_two + shift_two).astype(BF)
    if backward:
        e = cot[here, :].astype(F32)
        if clear_first:
            e = jnp.where(lax.broadcasted_iota(jnp.int32, e.shape, 0) + start == 0, 0.0, e)
        small[5:6, :] += jnp.sum(e, 0, keepdims=True)
        small[7:8, :] += jnp.sum(e * z2, 0, keepdims=True)
        dr2 = norm_back(e, z2, q2, gain_two)
        df = dr2.astype(BF)
        small[3:4, :] += jnp.sum(df.astype(F32), 0, keepdims=True)
        dn1 = dr2
        for part in range(PARTS):
            da = mm(df, weights(part, True), NT)
            size = da.shape[1]
            cols = slice(part * size, (part + 1) * size)
            du = (da * slope[:, cols]).astype(BF)
            du_out[:, cols] = du
            up_small[part : part + 1, :] += jnp.sum(du.astype(F32), 0, keepdims=True)
            dn1 += mm(du, weights(part, False))
        small[4:5, :] += jnp.sum(dn1, 0, keepdims=True)
        small[6:7, :] += jnp.sum(dn1 * z1, 0, keepdims=True)
        dr1 = norm_back(dn1, z1, q1, gain_one)
        do = dr1.astype(BF)
        small[2:3, :] += jnp.sum(do.astype(F32), 0, keepdims=True)
        dm_out[...] = mm(do, w_out[...]).astype(BF)
        n1_out[...] = n1
        df_out[...] = df
        do_out[...] = do
        dr1_out[...] = dr1


def feed(x, mix, w_out, vectors, up_bias, pieces, pieces_at, cot=None, start=0, count=None, clear_first=False, skip_rows=0):
    width = x.shape[1]
    count = count or x.shape[0]
    hidden = PARTS * up_bias.shape[1]
    wide, high = shape(count, width), shape(count, hidden)
    rows = pieces[0].shape[1] - skip_rows
    shapes = [wide]
    scratch = [pltpu.VMEM((2 * hidden // rows, rows, width), BF), pltpu.SemaphoreType.DMA((len(pieces),))]
    args = [x, mix, w_out, vectors, up_bias]
    if cot is not None:
        args.append(cot)
        shapes += [wide, high, high, wide, wide, shape(count, width, F32), wide, shape(8, width, F32), shape(*up_bias.shape, F32)]
        scratch.append(pltpu.VMEM((count, hidden), F32))
    return call(
        functools.partial(feed_kernel, pieces_at, skip_rows, start, clear_first, cot is not None),
        shapes, scratch, *args, far=pieces,
    )


def feed_grads_kernel(first, layout, halves, received, *refs):
    refs = list(refs)
    n1, df, g, du = (refs[i * halves : (i + 1) * halves] for i in range(4))
    refs = refs[4 * halves :]
    got = [refs.pop(0) for _ in range(received)]
    stacked = layout is None
    for index in range(refs[0].shape[0] if stacked else len(layout)):
        part = first + index
        outs = [refs[0].at[index]] if stacked else [refs.pop(0) for _ in range(layout[index])]
        size = g[0].shape[1] // PARTS
        cols = slice(part * size, (part + 1) * size)
        for lower, (left, right) in enumerate(((du, n1), (g, df))):
            full = sum(mm(a[:, cols], b[...], TN) for a, b in zip(left, right))
            at = 0
            for out in outs:
                slabs, half = out.shape[0], out.shape[1] // 2
                rows = slice(lower * half, (lower + 1) * half)
                value = full[at * half : (at + slabs) * half].reshape(slabs, half, out.shape[2])
                if received:
                    value += got[0][index, at : at + slabs, rows, :].astype(F32)
                out[:, rows, :] = value.astype(BF)
                at += slabs


def feed_grads(first, shapes, layout, n1, df, g, du, *received):
    width = n1[0].shape[1]
    outs = [jax.ShapeDtypeStruct((*lead, width), BF) for lead in shapes]
    return call(
        functools.partial(feed_grads_kernel, first, layout, len(n1), len(received)),
        outs, [], *n1, *df, *g, *du, *received,
    )


def feed_grads_all(halves_n, depth, half, n1, df, g, du, store):
    for part in range(PARTS):
        size = g[0].shape[1] // PARTS
        cols = slice(part * size, (part + 1) * size)
        for lower, (left, right) in enumerate(((du, n1), (g, df))):
            full = sum(mm(a[:, cols], b[...], TN) for a, b in zip(left, right)).astype(BF)
            store(part, lower, full.reshape(depth, half, -1))


def feed_grads_spread_kernel(depth, halves, at, *refs):
    refs = list(refs)
    n1, df, g, du = (refs[i * halves : (i + 1) * halves] for i in range(4))
    sent, here, by_y, by_x, both_a, both_b, all_rows = refs[4 * halves :]
    half = all_rows.shape[1] // 2

    def store(part, lower, value):
        all_rows[part * depth : (part + 1) * depth, lower * half : (lower + 1) * half, :] = value

    feed_grads_all(halves, depth, half, n1, df, g, du, store)
    split = both_a.shape[0]
    for part in (4, 5, 6, 7, 3, 1, 2, 0):
        place = far_place(at, part)
        for i in range(depth):
            slab = all_rows[i * PARTS + place]
            if part > 3:
                sent[part - 4, i] = slab
            elif part == 3:
                (both_a if i < split else both_b)[i % split] = slab
            else:
                (here, by_y, by_x)[part][i] = slab


def feed_grads_order_kernel(depth, halves, at, *refs):
    refs = list(refs)
    n1, df, g, du = (refs[i * halves : (i + 1) * halves] for i in range(4))
    (out,) = refs[4 * halves :]
    half = out.shape[1] // 2

    def store(part, lower, value):
        place = far_place(at, part)
        for i in range(depth):
            out[i * PARTS + place, lower * half : (lower + 1) * half, :] = value[i]

    feed_grads_all(halves, depth, half, n1, df, g, du, store)


def feed_grads_natural(spread, depth, half, at, n1, df, g, du):
    width = n1[0].shape[1]
    out = lambda *lead: jax.ShapeDtypeStruct((*lead, 2 * half, width), BF)
    if spread:
        shapes = [out(4, depth), out(depth), out(depth), out(depth), out(depth // 2), out(depth // 2)]
        scratch = [pltpu.VMEM((PARTS * depth, 2 * half, width), BF)]
    else:
        shapes, scratch = [out(PARTS * depth)], []
    kernel = feed_grads_spread_kernel if spread else feed_grads_order_kernel
    return call(functools.partial(kernel, depth, len(n1)), shapes, scratch, at, *n1, *df, *g, *du)


def after(values, *before):
    return lax.optimization_barrier((values, before))[0]


def swap(array, axis):
    return lax.ppermute(array, axis, [(0, 1), (1, 0)])


def swaps(arrays, axis):
    return [swap(a, axis) for a in arrays]


def marks_of(lengths, segments):
    length = segments.shape[1]
    place = lax.broadcasted_iota(jnp.int32, (1, length), 1)
    keys = jnp.where(place < lengths[:, None], segments, -1)
    return segments, keys.reshape(length, 1)


class Near:
    axes = ("z", "y", "x", "core")

    def __init__(self, shards):
        self.shards = shards
        self.depth = lax.axis_size("z")
        y, x, core = (lax.axis_index(name) for name in self.axes[1:])
        self.at = jnp.stack([y, x, core])
        self.z = lax.axis_index("z")
        self.device = self.z * PARTS + y * 4 + x * 2 + core
        w_qkv, w_out, w_up = shards[:3]
        self.n_qkv, self.n_out, self.n_up = w_qkv.shape[2], w_out.shape[2], w_up.shape[2]
        half = self.depth // 2
        own = [(0, 0), (1, 0), (2, 0), (3, 0), (3, half)]
        self.slabs = own + [(part + 4, first) for part, first in own]

    def slab_pair(self, index):
        w_qkv, w_out, w_up, w_down, biases, gains, up_bias = (s[index] for s in self.shards)
        width = w_qkv.shape[0]
        natural = lax.dynamic_update_slice(
            jnp.zeros((8, width), BF), jnp.concatenate([biases, gains], 0), (0, self.device * self.n_out)
        )
        line = lax.dynamic_update_slice(jnp.zeros((8, width), BF), up_bias[None], (0, self.z * self.n_up))
        attention = jnp.concatenate([w_qkv.T, w_out.T, natural, line], 0)
        return attention, jnp.concatenate([w_up.T, w_down], 0)

    def along_z(self, slab):
        return lax.all_gather(slab, "z", axis=0, tiled=False)

    def near(self, here):
        return [here, swap(here, "y"), swap(here, "x")]

    def diagonal(self, near):
        half = self.depth // 2
        return [swap(near[1][:half], "x"), swap(near[2][half:], "y")]

    def attend(self, x, marks, pieces):
        slabs = self.slabs if len(pieces) > 1 else []
        out = attention_forward(x, marks, pieces, self.at, slabs, self.depth, self.n_up)
        return dict(zip(("x", "qkv", "mix", "lse", "wt", "wt_out", "small", "up_bias"), [x, *out]))

    def feed(self, kept, pieces, cot, start, count, clear_first=False):
        pieces_at = [part * self.depth + first for part, first in self.slabs][: len(pieces)]
        out = feed(
            kept["x"], kept["mix"], kept["wt_out"], kept["small"], kept["up_bias"], pieces, pieces_at,
            cot, start, count, clear_first, pieces[0].shape[1] - 2 * self.n_up,
        )
        return dict(zip(("y", "n1", "g", "du", "df", "do", "dr1", "dm", "small", "up"), out))

    def feed_sent(self, halves):
        lists = [[h[name] for h in halves] for name in ("n1", "df", "g", "du")]
        (sent,) = feed_grads(4, [(4, self.depth, 2 * self.n_up)], None, *lists)
        return sent

    def feed_kept(self, halves, received):
        lists = [[h[name] for h in halves] for name in ("n1", "df", "g", "du")]
        full, half = (self.depth, 2 * self.n_up), (self.depth // 2, 2 * self.n_up)
        return feed_grads(0, [full, full, full, half, half], [1, 1, 1, 2], *lists, received)

    def feed_natural(self, halves, spread):
        lists = [[h[name] for h in halves] for name in ("n1", "df", "g", "du")]
        return feed_grads_natural(spread, self.depth, self.n_up, self.at, *lists)

    def reduce_diagonal(self, both):
        return [swap(both[0], "x"), swap(both[1], "y")]

    def add_diagonal(self, by_y, by_x, got):
        half = self.depth // 2
        return [by_y.at[:half].add(got[0]), by_x.at[half:].add(got[1])]

    def reduce_near(self, added):
        return [swap(added[0], "y"), swap(added[1], "x")]

    def reduce_z(self, here, got):
        return lax.psum_scatter(here + got[0] + got[1], "z", scatter_dimension=0, tiled=False)

    def attention_grads(self, kept, dqkv, do, smalls, ups, natural):
        sent, here, by_y, by_x, both_a, both_b = attention_grads(
            self.depth, self.at, natural, dqkv, kept["x"], do, kept["mix"], smalls, ups
        )
        return sent, [here, by_y, by_x, both_a, both_b]

    def add_received(self, kept, received):
        half = self.depth // 2
        here, by_y, by_x, both_a, both_b = kept
        return [
            here + received[0], by_y + received[1], by_x + received[2],
            both_a + received[3, :half], both_b + received[3, half:],
        ]

    def attention_outs(self, total, natural):
        total = total.astype(F32)
        n_qkv, n_out, n_up = self.n_qkv, self.n_out, self.n_up
        small = total[n_qkv + n_out :]
        own = lax.dynamic_slice(small, (0, self.device * n_out), (8, n_out))
        up = lax.dynamic_slice(small, (8, (self.device % self.depth if natural else self.z) * n_up), (1, n_up))[0]
        return total[:n_qkv].T, total[n_qkv : n_qkv + n_out].T, own[:6], own[6:], up

    def first_row_terms(self, fix):
        width = fix["n1"].shape[1]
        rows = jnp.stack([fix["n1"][0], fix["df"][0]]).reshape(1, 2 * width)
        table = jnp.stack([fix["du"][0].reshape(PARTS, self.depth, self.n_up), fix["g"][0].reshape(PARTS, self.depth, self.n_up)], 2)
        table = table.reshape(1, PARTS, -1)
        for axis in ("core", "x", "y"):
            n, far = table.shape[0], table.shape[1] // 2
            flat = jnp.concatenate([rows, table[:, far:].reshape(n, -1)], 1)
            got = swap(flat, axis)
            rows = jnp.concatenate([rows, got[:, : 2 * width]], 0)
            table = jnp.concatenate([table[:, :far], got[:, 2 * width :].reshape(n, far, -1)], 0)
        n = rows.shape[0]
        flat = jnp.concatenate([rows, table.reshape(n, -1)], 1)
        step = 1
        while step < self.depth:
            pairs = [(i, i ^ step) for i in range(self.depth)]
            flat = jnp.concatenate([flat, lax.ppermute(flat, "z", pairs)], 0)
            step *= 2
        own = flat[:, 2 * width :].reshape(flat.shape[0], self.depth, 2, self.n_up)
        own = lax.dynamic_index_in_dim(own, self.z, 1, keepdims=False)
        up = mm(own[:, 0], flat[:, :width], TN)
        down = mm(own[:, 1], flat[:, width : 2 * width], TN)
        return up, down


def near_body(tokens, skip_tokens, cot_first, cot_second, *rest):
    *shards, lengths, segments = rest
    link = Near(shards)
    marks = marks_of(lengths, segments)
    length = segments.shape[1]
    half = length // 2
    is_first = lax.broadcasted_iota(jnp.int32, (length, 1), 0) == 0

    slab_a1, slab_m1 = link.slab_pair(0)
    a1 = link.along_z(slab_a1)
    m1 = link.along_z(slab_m1)
    b2 = [lax.all_gather(after(jnp.concatenate(link.slab_pair(1), 0), a1), link.axes, axis=0, tiled=False)]
    a1 = link.near(a1)
    a1 += link.diagonal(a1)
    m1 = link.near(after(m1, a1))
    a1 += swaps(a1, "core")
    one = link.attend(*after((tokens, marks, a1), m1[0]))
    m1 = after(m1, one["mix"])
    m1 += link.diagonal(m1)
    m1 += swaps(m1, "core")
    one_a = link.feed(one, m1, cot_first, 0, half, True)
    one_b = link.feed(*after((one, m1, cot_first), one_a["y"]), half, half)
    (all_m1,) = link.feed_natural([one_a, one_b], False)
    sum_m1 = lax.psum_scatter(all_m1, link.axes, scatter_dimension=0, tiled=False).astype(F32)
    out_first = jnp.concatenate([one_a["y"], one_b["y"]], 0)
    second_in = jnp.where(is_first, out_first, skip_tokens)
    two = link.attend(*after((second_in, marks), all_m1), b2)
    two_a = link.feed(*after((two, b2, cot_second), two["mix"]), 0, half)
    two_b = link.feed(*after((two, b2, cot_second), two_a["y"]), half, half)
    sent_m2, *kept_m2 = link.feed_natural([two_a, two_b], True)
    dqkv2, sums2, grad_skip, first2 = attention_backward(
        two["qkv"], two["mix"], two["lse"], marks, two["wt"],
        *after(([two_a["dm"], two_b["dm"]], [two_a["dr1"], two_b["dr1"]]), kept_m2), clear_first=True,
    )
    kept_m2 = link.add_received(*after((kept_m2, swap(sent_m2, "core")), dqkv2))
    got_m2 = link.reduce_diagonal(kept_m2[3:])
    upstream = jnp.where(is_first[:16], cot_first[:16].astype(F32) + first2, 0.0)
    fix = link.feed(one, m1, after(upstream, kept_m2), 0, 16)
    added_m2 = link.add_diagonal(*after((kept_m2[1], kept_m2[2], got_m2), fix["y"]))
    got_m2 = link.reduce_near(added_m2)
    dqkv1, sums1, grad_tokens, _ = attention_backward(
        one["qkv"], one["mix"], one["lse"], marks, one["wt"],
        *after(([one_a["dm"], one_b["dm"]], [one_a["dr1"], one_b["dr1"]]), added_m2), fix=(fix["dm"], fix["dr1"]),
    )
    fix, one_a, one_b, two_a, two_b = after((fix, one_a, one_b, two_a, two_b), dqkv1)
    do1 = jnp.concatenate([one_a["do"], one_b["do"]], 0).at[:16].add(fix["do"])
    sent_a1, kept_a1 = link.attention_grads(
        one, dqkv1, do1,
        [sums1, one_a["small"], one_b["small"], fix["small"]], [one_a["up"], one_b["up"], fix["up"]], False,
    )
    sent_a2, kept_a2 = link.attention_grads(
        two, after(dqkv2, got_m2, sent_a1), jnp.concatenate([two_a["do"], two_b["do"]], 0),
        [sums2, two_a["small"], two_b["small"]], [two_a["up"], two_b["up"]], True,
    )
    sum_m2 = link.reduce_z(kept_m2[0], got_m2).astype(F32)
    kept_a1 = link.add_received(*after((kept_a1, swap(sent_a1, "core")), sent_a2))
    got_a1 = link.reduce_diagonal(kept_a1[3:])
    kept_a2 = link.add_received(*after((kept_a2, swap(sent_a2, "core")), kept_a1))
    got_a2 = link.reduce_diagonal(kept_a2[3:])
    got_a1 = link.reduce_near(link.add_diagonal(*after(kept_a1[1:3] + [got_a1], kept_a2)))
    got_a2 = link.reduce_near(link.add_diagonal(*kept_a2[1:3], got_a2))
    sum_a1 = link.reduce_z(after(kept_a1[0], sum_m2), got_a1)
    sum_a2 = link.reduce_z(after(kept_a2[0], sum_a1.astype(F32)), got_a2)

    n_up = link.n_up
    up_fix, down_fix = link.first_row_terms(fix)
    outs = [link.attention_outs(sum_a1, False), link.attention_outs(sum_a2, True)]
    pair = lambda i: jnp.stack([outs[0][i], outs[1][i]])
    return (
        out_first, jnp.concatenate([two_a["y"], two_b["y"]], 0), grad_tokens, grad_skip,
        pair(0), pair(1),
        jnp.stack([(sum_m1[:n_up] + up_fix).T, sum_m2[:n_up].T]),
        jnp.stack([sum_m1[n_up:] + down_fix, sum_m2[n_up:]]),
        pair(2), pair(3), pair(4),
    )


def far_body(tokens, skip_tokens, cot_first, cot_second, *rest):
    *shards, lengths, segments = rest
    axes = ("wide", "narrow")
    devices = lax.axis_size("wide") * lax.axis_size("narrow")
    marks = marks_of(lengths, segments)
    length, width = tokens.shape
    is_first = lax.broadcasted_iota(jnp.int32, (length, 1), 0) == 0
    gather = lambda a: lax.all_gather(a, axes, axis=0, tiled=True)
    scatter = lambda a: lax.psum_scatter(a, axes, scatter_dimension=0, tiled=True)

    def fetch(index):
        w_qkv, w_out, w_up, w_down, biases, gains, up_bias = (s[index] for s in shards)
        small = gather(jnp.concatenate([biases, gains], 0).T).T.astype(F32)
        up, down = (gather(w).reshape(PARTS, -1, width) for w in (w_up.T, w_down))
        both = jnp.concatenate([up, down], 1)
        return (
            gather(w_qkv.T), gather(w_out.T), small, gather(up_bias).astype(F32).reshape(PARTS, -1),
            [both],
        )

    def forward(x, weights):
        wt, wt_out, small, up_bias, pieces = weights
        qkv, mix, lse = attention_forward(x, marks, (wt, small))
        return (qkv, mix, lse), feed(x, mix, wt_out, small, up_bias, pieces, [0])[0]

    def backward(x, weights, kept, cot, clear_first):
        wt, wt_out, small, up_bias, pieces = weights
        qkv, mix, lse = kept
        y, n1, g, du, df, do, dr1, dm, sums, up_sums = feed(x, mix, wt_out, small, up_bias, pieces, [0], cot)
        dqkv, more, dx, first = attention_backward(qkv, mix, lse, marks, wt, [dm], [dr1], clear_first=clear_first)
        rows = 2 * up_bias.shape[1]
        lists = [[n1], [df], [g], [du]]
        parts = jnp.concatenate([feed_grads(i, [(4, 1, rows)], None, *lists)[0][:, 0] for i in (0, 4)], 0)
        up, down = (p.reshape(-1, width) for p in (parts[:, : rows // 2], parts[:, rows // 2 :]))
        sums = scatter((sums + more).T).T
        grads = (
            scatter(mm(dqkv, x, TN).astype(BF)).astype(F32).T,
            scatter(mm(do, mix, TN).astype(BF)).astype(F32).T,
            scatter(up).astype(F32).T,
            scatter(down).astype(F32),
            sums[:6], sums[6:], scatter(up_sums.reshape(-1)),
        )
        return y, dx, first, grads

    one, two = fetch(0), fetch(1)
    kept_one, out_first = forward(tokens, one)
    second_in = jnp.where(is_first, out_first, skip_tokens)
    kept_two, _ = forward(second_in, two)
    out_second, grad_skip, first, grads_two = backward(second_in, two, kept_two, cot_second, True)
    first = jnp.concatenate([first, jnp.zeros((length - first.shape[0], width), F32)], 0)
    upstream = cot_first.astype(F32) + jnp.where(is_first, first, 0.0)
    _, grad_tokens, _, grads_one = backward(tokens, one, kept_one, upstream, False)
    return (out_first, out_second, grad_tokens, grad_skip, *(jnp.stack(p) for p in zip(grads_one, grads_two)))


def solution(mesh):
    wide, narrow = mesh.shape["wide"], mesh.shape["narrow"]
    if narrow == 4 and wide % 4 == 0:
        mesh = Mesh(mesh.devices.reshape(wide // 2, 2, 2, 2), Near.axes)
        body, every = near_body, Near.axes
    else:
        body, every = far_body, ("wide", "narrow")
    rows, last, middle = P(every, None), P(None, None, every), P(None, every, None)
    return jax.shard_map(
        body,
        mesh=mesh,
        in_specs=(
            rows, rows, rows, rows, last, last, last, middle, last, last, P(None, every), P(every), rows,
        ),
        out_specs=(rows, rows, rows, rows, last, last, last, middle, last, last, P(None, every)),
        check_vma=False,
    )
```

time: 589 us -> 457 us (0.78)
  local copies, waits for them, and re-layouts: 71.2 us -> 28.4 us
  waiting for transfers between devices: 141 us -> 117 us
  other arithmetic: 60 us -> 37.7 us
  blocking collectives: 44.8 us -> 26.4 us
  matrix products: 16.1 us -> 0.45 us
  starting transfers between devices: 40.4 us -> 31.9 us
    ppermute x56 -> x36, waiting for transfers between devices: 126 us -> 87.1 us  [swap(): return lax.ppermute(array, axis, [(0, 1), (1, 0)])]
    unnamed x113 -> x127, local copies, waits for them, and re-layouts: 30.6 us -> 8.56 us
    all_gather x2 -> x1, blocking collectives: 44.8 us -> 26.4 us  [along_z(): return lax.all_gather(slab, 'z', axis=0, tiled=False)]
    dot_general x6 -> x2, matrix products: 16.1 us -> 0.45 us  [mm(): return lax.dot_general(a, b, dims, preferred_element_type=F32)]
    another operation x19 -> x9, other arithmetic: 20 us -> 5.67 us  [the longest x5 2.62 us: near_body(): pair = lambda i: jnp.stack([outs[0][i], outs[1][i]])]
    slice x53 -> x22, local copies, waits for them, and re-layouts: 21.3 us -> 11.2 us  [the longest x2 2.61 us: first_row_terms(): rows = jnp.stack([fix['n1'][0], fix['df'][0]]).reshape(1, 2 * width)]
    ppermute x0 -> x2, waiting for transfers between devices: none -> 8.81 us  [first_row_terms(): flat = jnp.concatenate([flat, lax.ppermute(flat, 'z', pairs)], 0)]
    ppermute x56 -> x36, starting transfers between devices: 40 us -> 31.6 us  [swap(): return lax.ppermute(array, axis, [(0, 1), (1, 0)])]
  transfers between devices with their start and end apart: 62 -> 44, of which waited for: 21 -> 22; matrix products, arithmetic and copies ran while one was open for 20% -> 11% of each run, Pallas kernels for 16% -> 43%
where the time goes in v2:
time: 457 us; the launch traced here: 450 us
  Pallas kernels  192 us (42%)
  waiting for transfers between devices  117 us (26%)
  other arithmetic  37.7 us (8%)
  starting transfers between devices  31.9 us (7%)
  local copies, waits for them, and re-layouts  28.4 us (6%)
  blocking collectives  26.4 us (6%)
  between operations  16.1 us (4%)
    pallas_call x13, Pallas kernels, call(): pl.pallas_call(kernel, out_shape=out_shapes, in_specs=[SMEM if a.ndim ==...  192 us
    ppermute x36, waiting for transfers between devices, swap(): return lax.ppermute(array, axis, [(0, 1), (1, 0)])  87.1 us
    ppermute x36, starting transfers between devices, swap(): return lax.ppermute(array, axis, [(0, 1), (1, 0)])  31.6 us
    all_gather x1, blocking collectives, along_z(): return lax.all_gather(slab, 'z', axis=0, tiled=False)  26.4 us
    reduce_scatter x3, waiting for transfers between devices, reduce_z(): lax.psum_scatter(here + got[0] + got[1], 'z', scatter_dimension=0, tiled=...  21.1 us
  transfers between devices with their start and end apart: 44, of which 22 were waited for; matrix products, arithmetic and copies ran while one was open for 11% of the time, Pallas kernels for 43%

profile of v2, /device:TPU:0, one launch (start us, length us, event | category | flops | bytes accessed | tf_op | source)
XLA Modules:
  0.0 450.3 jit_solution(5262881400639909756)
XLA Ops:
  7.3 1.0 slice_bitcast_fusion.6
  11.2 26.4 %all-gather = bf16[448,768]{1,0:T(8,128)(2,1)S(1)} all-gather(bf16[112,768]{1,0:T(8,128)(2,1)S(1)} %pad_maximum_fusion.7), channel_id=2, replica_groups=mesh['z'=4,'y'=2,'x'=2,'core'=2] {'z'}, dimensions={0}, use_global_device_ids=true | all-gather | bytes 860160 | tf_op jit(solution)/shard_map/all_gather | solution.py:575
  37.7 1.6 collective-permute-start.1
  39.3 1.6 collective-permute-start
  40.9 10.5 %collective-permute-done.1.refs_3_ = bf16[4,112,768]{2,1,0:T(8,128)(2,1)S(1)} collective-permute-done((bf16[4,112,768]{2,1,0:T(8,128)(2,1)S(1)}, bf16[4,112,768]{2,1,0:T(8,128)(2,1)S(1)}, u32[]{:S(2)}, u32[]{:S(2)}) %collective-permute-start.1) | collective-permute-done | bytes 688160 | tf_op jit(solution)/shard_map/ppermute | solution.py:534
  51.4 1.5 collective-permute-start.3
  52.9 2.2 collective-permute-done.refs_2_
  55.1 1.0 slice.486
  57.0 2.4 collective-permute-done.3.refs_5_
  59.3 10.6 %collective-permute-done.2.refs_4_ = bf16[2,112,768]{2,1,0:T(8,128)(2,1)} collective-permute-done((bf16[2,112,768]{2,1,0:T(8,128)(2,1)S(1)}, bf16[2,112,768]{2,1,0:T(8,128)(2,1)}, u32[]{:S(2)}, u32[]{:S(2)}) %collective-permute-start.2) | collective-permute-done | bytes 344096 | tf_op jit(solution)/shard_map/ppermute | solution.py:534
  69.9 2.7 collective-permute-start.9
  73.2 2.2 collective-permute-done.8.refs_10_
  79.0 14.9 %shard_map.212 = (bf16[512,2304]{1,0:T(8,128)(2,1)}, bf16[512,768]{1,0:T(8,128)(2,1)}, f32[12,1,512]{2,1,0:T(1,128)}, bf16[2304,768]{1,0:T(8,128)(2,1)}, bf16[76...) custom-call(bf16[512,768]{1,0:T(8,128)(2,1)} %x.1, s32[1,512]{1,0:T(1,128)} %seg_row.5, ...), custom_call_target="tpu_custom_call" | custom-call | tf_op jit(solution)/shard_map/pallas_call | solution.py:36
  93.9 14.3 %collective-permute-done.10.refs_8_ = bf16[4,192,768]{2,1,0:T(8,128)(2,1)S(1)} collective-permute-done((bf16[4,192,768]{2,1,0:T(8,128)(2,1)}, bf16[4,192,768]{2,1,0:T(8,128)(2,1)S(1)}, u32[]{:S(2)}, u32[]{:S(2)}) %collective-permute-start.10) | collective-permute-done | bytes 1179680 | tf_op jit(solution)/shard_map/ppermute | solution.py:534
  108.2 2.9 collective-permute-start.12
  111.9 7.1 %collective-permute-done.12.refs_10_ = bf16[2,192,768]{2,1,0:T(8,128)(2,1)S(1)} collective-permute-done((bf16[2,192,768]{2,1,0:T(8,128)(2,1)S(1)}, bf16[2,192,768]{2,1,0:T(8,128)(2,1)S(1)}, u32[]{:S(2)}, u32[]{:S(2)}) %collective-permute-start.12) | collective-permute-done | bytes 589856 | tf_op jit(solution)/shard_map/ppermute | solution.py:534
  119.0 2.1 collective-permute-done.11.refs_9_
  121.1 2.0 collective-permute-done.16.refs_14_
  125.2 17.3 %shard_map.213 = (bf16[256,768]{1,0:T(8,128)(2,1)}, bf16[256,768]{1,0:T(8,128)(2,1)}, bf16[256,3072]{1,0:T(8,128)(2,1)}, bf16[256,3072]{1,0:T(8,128)(2,1)}, bf16...) custom-call(bf16[512,768]{1,0:T(8,128)(2,1)} %x.1, ...), custom_call_target="tpu_custom_call" | custom-call | tf_op jit(solution)/shard_map/pallas_call | solution.py:36
  142.4 17.7 %shard_map.214 = (bf16[256,768]{1,0:T(8,128)(2,1)}, bf16[256,768]{1,0:T(8,128)(2,1)}, bf16[256,3072]{1,0:T(8,128)(2,1)}, bf16[256,3072]{1,0:T(8,128)(2,1)}, bf16...) custom-call(bf16[512,768]{1,0:T(8,128)(2,1)} %x.1, ...), custom_call_target="tpu_custom_call" | custom-call | tf_op jit(solution)/shard_map/pallas_call | solution.py:36
  160.1 12.4 %shard_map.215 = bf16[32,192,768]{2,1,0:T(8,128)(2,1)} custom-call(s32[3]{0:T(128)} %pad_add_fusion.refs_0_.at, bf16[256,768]{1,0:T(8,128)(2,1)} %get-tuple-element.334.refs_0_, bf16[256,768]{1,0:T(8,128)(2,1)} %get-tuple-element.335.refs_1_, bf16[256,768]{1,0:T(8,128)(2,1)} %get-tuple-element.336.refs_2_, bf16[256,768]{1,0:T(8,128)(2,1)} %get-tuple-element.337.refs_3_, ...), custom_call_target="tpu_custom_call" | custom-call | tf_op jit(solution)/shard_map/pallas_call | solution.py:36
  174.5 1.1 broadcast_select_fusion.x.refs_0_
  176.4 14.7 %shard_map.216 = (bf16[512,2304]{1,0:T(8,128)(2,1)}, bf16[512,768]{1,0:T(8,128)(2,1)}, f32[12,1,512]{2,1,0:T(1,128)}, bf16[2304,768]{1,0:T(8,128)(2,1)}, bf16[76...) custom-call(bf16[512,768]{1,0:T(8,128)(2,1)} %broadcast_select_fusion.x.refs_0_, s32[1,512]{1,0:T(1,128)} %seg_row.5, ...), custom_call_target="tpu_custom_call" | custom-call | tf_op jit(solution)/shard_map/pallas_call | solution.py:36
  191.2 19.1 %shard_map.217 = (bf16[256,768]{1,0:T(8,128)(2,1)}, bf16[256,768]{1,0:T(8,128)(2,1)}, bf16[256,3072]{1,0:T(8,128)(2,1)}, bf16[256,3072]{1,0:T(8,128)(2,1)}, bf16...) custom-call(bf16[512,768]{1,0:T(8,128)(2,1)} %broadcast_select_fusio, ...), custom_call_target="tpu_custom_call" | custom-call | tf_op jit(solution)/shard_map/pallas_call | solution.py:36
  210.3 19.5 %shard_map.218 = (bf16[256,768]{1,0:T(8,128)(2,1)}, bf16[256,768]{1,0:T(8,128)(2,1)}, bf16[256,3072]{1,0:T(8,128)(2,1)}, bf16[256,3072]{1,0:T(8,128)(2,1)}, bf16...) custom-call(bf16[512,768]{1,0:T(8,128)(2,1)} %broadcast_select_fusio, ...), custom_call_target="tpu_custom_call" | custom-call | tf_op jit(solution)/shard_map/pallas_call | solution.py:36
  229.7 12.2 %shard_map.219 = (bf16[4,4,192,768]{3,2,1,0:T(8,128)(2,1)}, bf16[4,192,768]{2,1,0:T(8,128)(2,1)}, bf16[4,192,768]{2,1,0:T(8,128)(2,1)}, bf16[4,192,768]{2,1,0:T(...) custom-call(s32[3]{0:T(128)} %pad_add_fusion.refs_0_.at, ...), custom_call_target="tpu_custom_call" | custom-call | tf_op jit(solution)/shard_map/pallas_call | solution.py:36
  243.6 19.2 %shard_map.220 = (bf16[512,2304]{1,0:T(8,128)(2,1)}, f32[8,768]{1,0:T(8,128)}, f32[512,768]{1,0:T(8,128)}, f32[16,768]{1,0:T(8,128)}) custom-call(bf16[512,2304]{1,0:T(8,128)(2,1)} %get-tuple-element.346.qkv, bf16[512,768]{1,0:T(8,128)(2,1)} %get-tuple-element.363.refs_1_.mix, f32[12,1,512]{2,1,0:T(1,128)} %get-tuple-element.348.lse_rows, s32[1,512]{1,0:T(1,128)} %seg_row.5, ...), custom_call_target="tpu_custom_call" | custom-call | tf_op jit(solution)/shard_map/pallas_call | solution.py:36
  262.9 1.6 bitcast_add_fusion.9
  264.4 1.7 collective-permute-start.20
  266.1 1.5 add_select_fusion.refs_5_
  267.6 2.4 bitcast_add_fusion
  270.0 10.9 %shard_map.221 = (bf16[16,768]{1,0:T(8,128)(2,1)}, bf16[16,768]{1,0:T(8,128)(2,1)}, bf16[16,3072]{1,0:T(8,128)(2,1)}, bf16[16,3072]{1,0:T(8,128)(2,1)}, bf16[16,...) custom-call(bf16[512,768]{1,0:T(8,128)(2,1)} %x.1, ...), custom_call_target="tpu_custom_call" | custom-call | tf_op jit(solution)/shard_map/pallas_call | solution.py:36
  281.0 6.1 %collective-permute-done.20 = bf16[2,192,768]{2,1,0:T(8,128)(2,1)S(1)} collective-permute-done((bf16[2,192,768]{2,1,0:T(8,128)(2,1)S(1)}, bf16[2,192,768]{2,1,0:T(8,128)(2,1)S(1)}, u32[]{:S(2)}, u32[]{:S(2)}) %collective-permute-start.20) | collective-permute-done | bytes 589856 | tf_op jit(solution)/shard_map/ppermute | solution.py:534
  287.8 2.5 collective-permute-start.22
  290.3 19.4 %shard_map.222 = (bf16[512,2304]{1,0:T(8,128)(2,1)}, f32[8,768]{1,0:T(8,128)}, f32[512,768]{1,0:T(8,128)}, f32[16,768]{1,0:T(8,128)}) custom-call(bf16[512,2304]{1,0:T(8,128)(2,1)} %get-tuple-element.315.qkv, bf16[512,768]{1,0:T(8,128)(2,1)} %get-tuple-element.318.refs_1_.mix, f32[12,1,512]{2,1,0:T(1,128)} %get-tuple-element.314.lse_rows, s32[1,512]{1,0:T(1,128)} %seg_row.5, ...), custom_call_target="tpu_custom_call" | custom-call | tf_op jit(solution)/shard_map/pallas_call | solution.py:36
  309.7 1.3 slice.454
  311.0 1.3 slice.455
  316.8 1.4 fusion.14
  319.0 1.2 pad_maximum_fusion.1
  321.8 7.6 %shard_map.223 = (bf16[4,4,112,768]{3,2,1,0:T(8,128)(2,1)}, bf16[4,112,768]{2,1,0:T(8,128)(2,1)}, bf16[4,112,768]{2,1,0:T(8,128)(2,1)}, bf16[4,112,768]{2,1,0:T(...) custom-call(s32[3]{0:T(128)} %pad_add_fusion.refs_0_.at, ...), custom_call_target="tpu_custom_call" | custom-call | tf_op jit(solution)/shard_map/pallas_call | solution.py:36
  331.0 3.2 collective-permute-done.33
  336.2 7.5 %shard_map.224 = (bf16[4,4,112,768]{3,2,1,0:T(8,128)(2,1)}, bf16[4,112,768]{2,1,0:T(8,128)(2,1)}, bf16[4,112,768]{2,1,0:T(8,128)(2,1)}, bf16[4,112,768]{2,1,0:T(...) custom-call(s32[3]{0:T(128)} %pad_add_fusion.refs_0_.at, ...), custom_call_target="tpu_custom_call" | custom-call | tf_op jit(solution)/shard_map/pallas_call | solution.py:36
  344.8 2.1 collective-permute-start.34
  346.9 1.7 collective-permute-done.34
  350.2 1.0 convert_element_type.23
  351.2 2.6 collective-permute-done.35
  354.5 2.8 add_add_fusion
  358.4 1.2 bitcast_add_fusion.13
  359.7 1.9 collective-permute-start.24
  361.7 1.7 bitcast_add_fusion.6
  363.5 2.1 bitcast_add_fusion.12
  365.6 1.9 collective-permute-start.31
  367.5 1.8 bitcast_add_fusion.4
  369.6 3.2 collective-permute-start.28
  373.7 3.1 collective-permute-done.31
  377.0 3.2 collective-permute-start.32
  380.1 9.0 %collective-permute-done.28 = bf16[4,112,768]{2,1,0:T(8,128)(2,1)S(1)} collective-permute-done((bf16[4,112,768]{2,1,0:T(8,128)(2,1)S(1)}, bf16[4,112,768]{2,1,0:T(8,128)(2,1)S(1)}, u32[]{:S(2)}, u32[]{:S(2)}) %collective-permute-start.28) | collective-permute-done | bytes 688160 | tf_op jit(solution)/shard_map/ppermute | solution.py:534
  389.8 1.0 add_add_fusion.2
  390.8 5.8 %collective-permute-done.29 = bf16[2,112,768]{2,1,0:T(8,128)(2,1)} collective-permute-done((bf16[2,112,768]{2,1,0:T(8,128)(2,1)}, bf16[2,112,768]{2,1,0:T(8,128)(2,1)}, u32[]{:S(2)}, u32[]{:S(2)}) %collective-permute-start.29) | collective-permute-done | bytes 344096 | tf_op jit(solution)/shard_map/ppermute | solution.py:534
  396.6 1.1 fusion.3
  398.9 8.8 %collective-permute-done.37 = bf16[16,2304]{1,0:T(8,128)(2,1)S(1)} collective-permute-done((bf16[16,2304]{1,0:T(8,128)(2,1)S(1)}, bf16[16,2304]{1,0:T(8,128)(2,1)S(1)}, u32[]{:S(2)}, u32[]{:S(2)}) %collective-permute-start.37) | collective-permute-done | bytes 73760 | tf_op jit(solution)/shard_map/ppermute | solution.py:662
  408.8 2.3 add_add_fusion.1
  412.5 1.0 convert_element_type.24
  417.1 21.1 %reduce-scatter.7.cloned.1.call-done = bf16[1,112,768]{2,1,0:T(8,128)(2,1)} async-done(((bf16[4,112,768]{2,1,0:T(8,128)(2,1)}), bf16[1,112,768]{2,1,0:T(8,128)(2,1)}) %reduce-scatter.7.cloned.1.call-update) | async-done | bytes 172048 | tf_op jit(solution)/shard_map/reduce_scatter | solution.py:622
  (281 shorter events, 44.3 us)
Async XLA Ops:
  7.2 62.7 %all-gather.6.cloned.1.call-start = ((), (), s32[]{:S(2)}) async-start(), calls=%async_computation.8 | async-start | bytes 1474560 | tf_op jit(solution)/shard_map/all_gather | solution.py:575
  10.0 166.4 %all-gather.8.cloned.1.call-start = ((), (), s32[]{:S(2)}) async-start(), calls=%async_computation.9 | async-start | bytes 15409152 | tf_op jit(solution)/shard_map/all_gather | solution.py:682
  11.1 26.5 %copy-start.18 = (bf16[304,768]{1,0:T(8,128)(2,1)}, bf16[304,768]{1,0:T(8,128)(2,1)S(1)}, u32[]{:S(2)}) copy-start(bf16[304,768]{1,0:T(8,128)(2,1)S(1)} %bitcast_dynamic-update-slice_fusion.1) | copy-start | bytes 1400836
  11.2 66.6 %copy-start.47 = (s32[1,512]{1,0:T(1,128)S(1)}, s32[1,512]{1,0:T(1,128)}, u32[]{:S(2)}) copy-start(s32[1,512]{1,0:T(1,128)} %seg_row.5) | copy-start | bytes 6148
  37.6 41.4 %copy-start.11 = (bf16[448,768]{1,0:T(8,128)(2,1)}, bf16[448,768]{1,0:T(8,128)(2,1)S(1)}, u32[]{:S(2)}) copy-start(bf16[448,768]{1,0:T(8,128)(2,1)S(1)} %all-gather) | copy-start | bytes 2064388
  37.6 312.6 %reduce-scatter.9.cloned.1.call-start = ((), (), s32[]{:S(2)}) async-start(), calls=%async_computation.6 | async-start | bytes 9732096 | tf_op jit(solution)/shard_map/reduce_scatter | solution.py:694
  37.7 13.7 %collective-permute-start.1 = (bf16[4,112,768]{2,1,0:T(8,128)(2,1)S(1)}, bf16[4,112,768]{2,1,0:T(8,128)(2,1)S(1)}, u32[]{:S(2)}, u32[]{:S(2)}) collective-permute-start(bf16[4,112,768]{2,1,0:T(8,128)(2,1)S(1)} %bitcast.166), channel_id=1, source_target_pairs={{0,2},{2,0},{1,3},{3,1},{4,6},{6,4},{5,7},{7,5},{8,10},{10,8},{9,1... | collective-permute-start | bytes 2064392 | tf_op jit(solution)/shard_map/ppermute | solution.py:534
  39.3 15.8 %collective-permute-start = (bf16[4,112,768]{2,1,0:T(8,128)(2,1)S(1)}, bf16[4,112,768]{2,1,0:T(8,128)(2,1)}, u32[]{:S(2)}, u32[]{:S(2)}) collective-permute-start(bf16[4,112,768]{2,1,0:T(8,128)(2,1)S(1)} %bitcast.167), channel_id=1, source_target_pairs={{0,4},{4,0},{1,5},{5,1},{2,6},{6,2},{3,7},{7,3},{8,12},{12,8},{9,1... | collective-permute-start | bytes 2064392 | tf_op jit(solution)/shard_map/ppermute | solution.py:534
  51.4 4.8 %copy-start.13 = (bf16[4,112,768]{2,1,0:T(8,128)(2,1)}, bf16[4,112,768]{2,1,0:T(8,128)(2,1)S(1)}, u32[]{:S(2)}) copy-start(bf16[4,112,768]{2,1,0:T(8,128)(2,1)S(1)} %collective-permute-done.1.refs_3_) | copy-start | bytes 2064388
  51.4 7.9 %collective-permute-start.3 = (bf16[2,112,768]{2,1,0:T(8,128)(2,1)S(1)}, bf16[2,112,768]{2,1,0:T(8,128)(2,1)S(1)}, u32[]{:S(2)}, u32[]{:S(2)}) collective-permute-start(bf16[2,112,768]{2,1,0:T(8,128)(2,1)S(1)} %slice.487), channel_id=1, source_target_pairs={{0,4},{4,0},{1,5},{5,1},{2,6},{6,2},{3,7},{7,3},{8,12},{12,8},{9,1... | collective-permute-start | bytes 1032200 | tf_op jit(solution)/shard_map/ppermute | solution.py:534
  56.1 13.8 %collective-permute-start.2 = (bf16[2,112,768]{2,1,0:T(8,128)(2,1)S(1)}, bf16[2,112,768]{2,1,0:T(8,128)(2,1)}, u32[]{:S(2)}, u32[]{:S(2)}) collective-permute-start(bf16[2,112,768]{2,1,0:T(8,128)(2,1)S(1)} %slice.486), channel_id=1, source_target_pairs={{0,2},{2,0},{1,3},{3,1},{4,6},{6,4},{5,7},{7,5},{8,10},{10,8},{9,1... | collective-permute-start | bytes 1032200 | tf_op jit(solution)/shard_map/ppermute | solution.py:534
  57.0 16.2 %collective-permute-start.4 = (bf16[4,112,768]{2,1,0:T(8,128)(2,1)S(1)}, bf16[4,112,768]{2,1,0:T(8,128)(2,1)}, u32[]{:S(2)}, u32[]{:S(2)}) collective-permute-start(bf16[4,112,768]{2,1,0:T(8,128)(2,1)S(1)} %bitcast.168), channel_id=1, source_target_pairs={{0,1},{1,0},{2,3},{3,2},{4,5},{5,4},{6,7},{7,6},{8,9},{9,8},{10,11... | collective-permute-start | bytes 2064392 | tf_op jit(solution)/shard_map/ppermute | solution.py:534
  59.3 19.7 %copy-start.37 = (bf16[2,112,768]{2,1,0:T(8,128)(2,1)}, bf16[2,112,768]{2,1,0:T(8,128)(2,1)S(1)}, u32[]{:S(2)}) copy-start(bf16[2,112,768]{2,1,0:T(8,128)(2,1)S(1)} %collective-permute-done.3.refs_5_) | copy-start | bytes 1032196
  69.9 38.2 %collective-permute-start.10 = (bf16[4,192,768]{2,1,0:T(8,128)(2,1)}, bf16[4,192,768]{2,1,0:T(8,128)(2,1)S(1)}, u32[]{:S(2)}, u32[]{:S(2)}) collective-permute-start(bf16[4,192,768]{2,1,0:T(8,128)(2,1)} %bitcast.160), channel_id=1, source_target_pairs={{0,2},{2,0},{1,3},{3,1},{4,6},{6,4},{5,7},{7,5},{8,10},{10,8},{9,1... | collective-permute-start | bytes 3538952 | tf_op jit(solution)/shard_map/ppermute | solution.py:534
  69.9 38.2 %collective-permute-start.9 = (bf16[4,192,768]{2,1,0:T(8,128)(2,1)}, bf16[4,192,768]{2,1,0:T(8,128)(2,1)S(1)}, u32[]{:S(2)}, u32[]{:S(2)}) collective-permute-start(bf16[4,192,768]{2,1,0:T(8,128)(2,1)} %bitcast.161), channel_id=1, source_target_pairs={{0,4},{4,0},{1,5},{5,1},{2,6},{6,2},{3,7},{7,3},{8,12},{12,8},{9,1... | collective-permute-start | bytes 3538952 | tf_op jit(solution)/shard_map/ppermute | solution.py:534
  72.7 5.1 %collective-permute-start.6 = (bf16[4,112,768]{2,1,0:T(8,128)(2,1)}, bf16[4,112,768]{2,1,0:T(8,128)(2,1)}, u32[]{:S(2)}, u32[]{:S(2)}) collective-permute-start(bf16[4,112,768]{2,1,0:T(8,128)(2,1)} %copy-done.13), channel_id=1, source_target_pairs={{0,1},{1,0},{2,3},{3,2},{4,5},{5,4},{6,7},{7,6},{8,9},{9,8},{10,11... | collective-permute-start | bytes 2064392 | tf_op jit(solution)/shard_map/ppermute | solution.py:534
  72.7 2.8 collective-permute-start.8
  73.2 5.0 %collective-permute-start.5 = (bf16[4,112,768]{2,1,0:T(8,128)(2,1)}, bf16[4,112,768]{2,1,0:T(8,128)(2,1)}, u32[]{:S(2)}, u32[]{:S(2)}) collective-permute-start(bf16[4,112,768]{2,1,0:T(8,128)(2,1)} %collective-permute-done.refs_2_), channel_id=1, source_target_pairs={{0,1},{1,0},{2,3},{3,2},{4,5},{5,4},{6,7},{7,6},{8,9},{9,8},{10,11... | collective-permute-start | bytes 2064392 | tf_op jit(solution)/shard_map/ppermute | solution.py:534
  76.1 2.0 collective-permute-start.7
  108.2 10.8 %collective-permute-start.12 = (bf16[2,192,768]{2,1,0:T(8,128)(2,1)S(1)}, bf16[2,192,768]{2,1,0:T(8,128)(2,1)S(1)}, u32[]{:S(2)}, u32[]{:S(2)}) collective-permute-start(bf16[2,192,768]{2,1,0:T(8,128)(2,1)S(1)} %slice.412), channel_id=1, source_target_pairs={{0,4},{4,0},{1,5},{5,1},{2,6},{6,2},{3,7},{7,3},{8,12},{12,8},{9,1... | collective-permute-start | bytes 1769480 | tf_op jit(solution)/shard_map/ppermute | solution.py:534
  111.1 9.9 %collective-permute-start.11 = (bf16[2,192,768]{2,1,0:T(8,128)(2,1)S(1)}, bf16[2,192,768]{2,1,0:T(8,128)(2,1)S(1)}, u32[]{:S(2)}, u32[]{:S(2)}) collective-permute-start(bf16[2,192,768]{2,1,0:T(8,128)(2,1)S(1)} %slice.411), channel_id=1, source_target_pairs={{0,2},{2,0},{1,3},{3,1},{4,6},{6,4},{5,7},{7,5},{8,10},{10,8},{9,1... | collective-permute-start | bytes 1769480 | tf_op jit(solution)/shard_map/ppermute | solution.py:534
  111.2 11.9 %collective-permute-start.13 = (bf16[4,192,768]{2,1,0:T(8,128)(2,1)S(1)}, bf16[4,192,768]{2,1,0:T(8,128)(2,1)S(1)}, u32[]{:S(2)}, u32[]{:S(2)}) collective-permute-start(bf16[4,192,768]{2,1,0:T(8,128)(2,1)S(1)} %bitcast.165), channel_id=1, source_target_pairs={{0,1},{1,0},{2,3},{3,2},{4,5},{5,4},{6,7},{7,6},{8,9},{9,8},{10,11... | collective-permute-start | bytes 3538952 | tf_op jit(solution)/shard_map/ppermute | solution.py:534
  111.3 11.8 %collective-permute-start.14 = (bf16[4,192,768]{2,1,0:T(8,128)(2,1)S(1)}, bf16[4,192,768]{2,1,0:T(8,128)(2,1)S(1)}, u32[]{:S(2)}, u32[]{:S(2)}) collective-permute-start(bf16[4,192,768]{2,1,0:T(8,128)(2,1)S(1)} %collective-permute-done.9.refs_7_), channel_id=1, source_target_pairs={{0,1},{1,0},{2,3},{3,2},{4,5},{5,4},{6,7},{7,6},{8,9},{9,8},{10,11... | collective-permute-start | bytes 3538952 | tf_op jit(solution)/shard_map/ppermute | solution.py:534
  111.8 11.3 %collective-permute-start.15 = (bf16[4,192,768]{2,1,0:T(8,128)(2,1)S(1)}, bf16[4,192,768]{2,1,0:T(8,128)(2,1)S(1)}, u32[]{:S(2)}, u32[]{:S(2)}) collective-permute-start(bf16[4,192,768]{2,1,0:T(8,128)(2,1)S(1)} %collective-permute-done.10.refs_8_), channel_id=1, source_target_pairs={{0,1},{1,0},{2,3},{3,2},{4,5},{5,4},{6,7},{7,6},{8,9},{9,8},{10,11... | collective-permute-start | bytes 3538952 | tf_op jit(solution)/shard_map/ppermute | solution.py:534
  119.0 4.9 %copy-start.6 = (bf16[2,192,768]{2,1,0:T(8,128)(2,1)}, bf16[2,192,768]{2,1,0:T(8,128)(2,1)S(1)}, u32[]{:S(2)}) copy-start(bf16[2,192,768]{2,1,0:T(8,128)(2,1)S(1)} %collective-permute-done.12.refs_10_) | copy-start | bytes 1769476
  119.0 2.1 collective-permute-start.17
  121.1 2.0 collective-permute-start.16
  172.5 239.0 %reduce-scatter.11.cloned.1.call-start = ((), (), s32[]{:S(2)}) async-start(), calls=%async_computation.7 | async-start | bytes 1474560 | tf_op jit(solution)/shard_map/reduce_scatter | solution.py:622
  241.9 20.9 %collective-permute-start.18 = (bf16[4,4,192,768]{3,2,1,0:T(8,128)(2,1)}, bf16[4,4,192,768]{3,2,1,0:T(8,128)(2,1)}, u32[]{:S(2)}, u32[]{:S(2)}) collective-permute-start(bf16[4,4,192,768]{3,2,1,0:T(8,128)(2,1)} %get-tuple-element.390), channel_id=1, source_target_pairs={{0,1},{1,0},{2,3},{3,2},{4,5},{5,4},{6,7},{7,6},{8,9},{9,8},{10,11... | collective-permute-start | bytes 14155784 | tf_op jit(solution)/shard_map/ppermute | solution.py:534
  243.6 19.2 %copy-start.25 = (bf16[2,192,768]{2,1,0:T(8,128)(2,1)S(1)}, bf16[2,192,768]{2,1,0:T(8,128)(2,1)}, u32[]{:S(2)}) copy-start(bf16[2,192,768]{2,1,0:T(8,128)(2,1)} %get-tuple-element.396) | copy-start | bytes 1769476
  243.6 19.2 %copy-start.26 = (bf16[2,192,768]{2,1,0:T(8,128)(2,1)S(1)}, bf16[2,192,768]{2,1,0:T(8,128)(2,1)}, u32[]{:S(2)}) copy-start(bf16[2,192,768]{2,1,0:T(8,128)(2,1)} %get-tuple-element.397) | copy-start | bytes 1769476
  262.8 4.8 %copy-start.14 = (bf16[4,192,768]{2,1,0:T(8,128)(2,1)S(1)}, bf16[4,192,768]{2,1,0:T(8,128)(2,1)}, u32[]{:S(2)}) copy-start(bf16[4,192,768]{2,1,0:T(8,128)(2,1)} %get-tuple-element.392) | copy-start | bytes 3538948
  262.9 4.8 %copy-start.15 = (bf16[4,192,768]{2,1,0:T(8,128)(2,1)S(1)}, bf16[4,192,768]{2,1,0:T(8,128)(2,1)}, u32[]{:S(2)}) copy-start(bf16[4,192,768]{2,1,0:T(8,128)(2,1)} %get-tuple-element.394) | copy-start | bytes 3538948
  262.9 4.8 %copy-start.16 = (bf16[4,192,768]{2,1,0:T(8,128)(2,1)S(1)}, bf16[4,192,768]{2,1,0:T(8,128)(2,1)}, u32[]{:S(2)}) copy-start(bf16[4,192,768]{2,1,0:T(8,128)(2,1)} %get-tuple-element.395) | copy-start | bytes 3538948
  264.4 22.7 %collective-permute-start.20 = (bf16[2,192,768]{2,1,0:T(8,128)(2,1)S(1)}, bf16[2,192,768]{2,1,0:T(8,128)(2,1)S(1)}, u32[]{:S(2)}, u32[]{:S(2)}) collective-permute-start(bf16[2,192,768]{2,1,0:T(8,128)(2,1)S(1)} %get-tuple-element.533), channel_id=1, source_target_pairs={{0,4},{4,0},{1,5},{5,1},{2,6},{6,2},{3,7},{7,3},{8,12},{12,8},{9,1... | collective-permute-start | bytes 1769480 | tf_op jit(solution)/shard_map/ppermute | solution.py:534
  266.1 21.0 %collective-permute-start.19 = (bf16[2,192,768]{2,1,0:T(8,128)(2,1)S(1)}, bf16[2,192,768]{2,1,0:T(8,128)(2,1)S(1)}, u32[]{:S(2)}, u32[]{:S(2)}) collective-permute-start(bf16[2,192,768]{2,1,0:T(8,128)(2,1)S(1)} %get-tuple-element.534), channel_id=1, source_target_pairs={{0,2},{2,0},{1,3},{3,1},{4,6},{6,4},{5,7},{7,5},{8,10},{10,8},{9,1... | collective-permute-start | bytes 1769480 | tf_op jit(solution)/shard_map/ppermute | solution.py:534
  287.4 48.8 %collective-permute-start.23 = (bf16[4,192,768]{2,1,0:T(8,128)(2,1)S(1)}, bf16[4,192,768]{2,1,0:T(8,128)(2,1)}, u32[]{:S(2)}, u32[]{:S(2)}) collective-permute-start(bf16[4,192,768]{2,1,0:T(8,128)(2,1)S(1)} %add_dynamic-update-slice_fusion), channel_id=1, source_target_pairs={{0,2},{2,0},{1,3},{3,1},{4,6},{6,4},{5,7},{7,5},{8,10},{10,8},{9,1... | collective-permute-start | bytes 3538952 | tf_op jit(solution)/shard_map/ppermute | solution.py:534
  287.8 48.4 %collective-permute-start.22 = (bf16[4,192,768]{2,1,0:T(8,128)(2,1)S(1)}, bf16[4,192,768]{2,1,0:T(8,128)(2,1)}, u32[]{:S(2)}, u32[]{:S(2)}) collective-permute-start(bf16[4,192,768]{2,1,0:T(8,128)(2,1)S(1)} %add_dynamic-update-slice_fusion.1), channel_id=1, source_target_pairs={{0,4},{4,0},{1,5},{5,1},{2,6},{6,2},{3,7},{7,3},{8,12},{12,8},{9,1... | collective-permute-start | bytes 3538952 | tf_op jit(solution)/shard_map/ppermute | solution.py:534
  321.8 8.3 %copy-start.31 = (bf16[256,768]{1,0:T(8,128)(2,1)S(1)}, bf16[256,768]{1,0:T(8,128)(2,1)}, u32[]{:S(2)}) copy-start(bf16[256,768]{1,0:T(8,128)(2,1)} %get-tuple-element.456) | copy-start | bytes 1179652
  321.8 8.3 %copy-start.32 = (bf16[256,768]{1,0:T(8,128)(2,1)S(1)}, bf16[256,768]{1,0:T(8,128)(2,1)}, u32[]{:S(2)}) copy-start(bf16[256,768]{1,0:T(8,128)(2,1)} %get-tuple-element.457) | copy-start | bytes 1179652
  329.4 28.0 %collective-permute-start.21 = (bf16[4,4,112,768]{3,2,1,0:T(8,128)(2,1)}, bf16[4,4,112,768]{3,2,1,0:T(8,128)(2,1)}, u32[]{:S(2)}, u32[]{:S(2)}) collective-permute-start(bf16[4,4,112,768]{3,2,1,0:T(8,128)(2,1)} %get-tuple-element.454), channel_id=1, source_target_pairs={{0,1},{1,0},{2,3},{3,2},{4,5},{5,4},{6,7},{7,6},{8,9},{9,8},{10,11... | collective-permute-start | bytes 8257544 | tf_op jit(solution)/shard_map/ppermute | solution.py:534
  329.5 4.7 %collective-permute-start.33 = (bf16[1,4608]{1,0:T(2,128)(2,1)S(1)}, bf16[1,4608]{1,0:T(2,128)(2,1)S(1)}, u32[]{:S(2)}, u32[]{:S(2)}) collective-permute-start(bf16[1,4608]{1,0:T(2,128)(2,1)S(1)} %pad_maximum_fusion.13), channel_id=1, source_target_pairs={{0,1},{1,0},{2,3},{3,2},{4,5},{5,4},{6,7},{7,6},{8,9},{9,8},{10,11... | collective-permute-start | bytes 27656 | tf_op jit(solution)/shard_map/ppermute | solution.py:534
  336.1 7.9 %copy-start.45 = (bf16[1,4,768]{2,1,0:T(4,128)(2,1)}, bf16[1,4,768]{2,1,0:T(4,128)(2,1)S(1)}, u32[]{:S(2)}) copy-start(bf16[1,4,768]{2,1,0:T(4,128)(2,1)S(1)} %reshape.302) | copy-start | bytes 18436
  336.2 7.9 %copy-start.46 = (bf16[1,4,768]{2,1,0:T(4,128)(2,1)S(1)}, bf16[1,4,768]{2,1,0:T(4,128)(2,1)}, u32[]{:S(2)}) copy-start(bf16[1,4,768]{2,1,0:T(4,128)(2,1)} %get-tuple-element.552) | copy-start | bytes 18436
  343.7 19.7 %collective-permute-start.26 = (bf16[4,4,112,768]{3,2,1,0:T(8,128)(2,1)}, bf16[4,4,112,768]{3,2,1,0:T(8,128)(2,1)}, u32[]{:S(2)}, u32[]{:S(2)}) collective-permute-start(bf16[4,4,112,768]{3,2,1,0:T(8,128)(2,1)} %get-tuple-element.463), channel_id=1, source_target_pairs={{0,1},{1,0},{2,3},{3,2},{4,5},{5,4},{6,7},{7,6},{8,9},{9,8},{10,11... | collective-permute-start | bytes 8257544 | tf_op jit(solution)/shard_map/ppermute | solution.py:534
  344.8 3.8 collective-permute-start.34
  348.6 24.4 %copy-start.42 = (bf16[2,1536]{1,0:T(2,128)(2,1)}, bf16[2,1536]{1,0:T(2,128)(2,1)S(1)}, u32[]{:S(2)}) copy-start(bf16[2,1536]{1,0:T(2,128)(2,1)S(1)} %get-tuple-element.550) | copy-start | bytes 18436
  350.0 3.8 collective-permute-start.35
  357.3 4.4 copy-start.19
  357.3 57.9 %reduce-scatter.5.cloned.1.call-start = ((), (), s32[]{:S(2)}) async-start(), calls=%async_computation.4 | async-start | bytes 860160 | tf_op jit(solution)/shard_map/reduce_scatter | solution.py:622
  359.5 10.0 %collective-permute-start.25 = (bf16[2,112,768]{2,1,0:T(8,128)(2,1)S(1)}, bf16[2,112,768]{2,1,0:T(8,128)(2,1)S(1)}, u32[]{:S(2)}, u32[]{:S(2)}) collective-permute-start(bf16[2,112,768]{2,1,0:T(8,128)(2,1)S(1)} %get-tuple-element.543), channel_id=1, source_target_pairs={{0,4},{4,0},{1,5},{5,1},{2,6},{6,2},{3,7},{7,3},{8,12},{12,8},{9,1... | collective-permute-start | bytes 1032200 | tf_op jit(solution)/shard_map/ppermute | solution.py:534
  359.7 9.8 %collective-permute-start.24 = (bf16[2,112,768]{2,1,0:T(8,128)(2,1)S(1)}, bf16[2,112,768]{2,1,0:T(8,128)(2,1)S(1)}, u32[]{:S(2)}, u32[]{:S(2)}) collective-permute-start(bf16[2,112,768]{2,1,0:T(8,128)(2,1)S(1)} %get-tuple-element.544), channel_id=1, source_target_pairs={{0,2},{2,0},{1,3},{3,1},{4,6},{6,4},{5,7},{7,5},{8,10},{10,8},{9,1... | collective-permute-start | bytes 1032200 | tf_op jit(solution)/shard_map/ppermute | solution.py:534
  365.6 11.3 %collective-permute-start.31 = (bf16[2,112,768]{2,1,0:T(8,128)(2,1)S(1)}, bf16[2,112,768]{2,1,0:T(8,128)(2,1)S(1)}, u32[]{:S(2)}, u32[]{:S(2)}) collective-permute-start(bf16[2,112,768]{2,1,0:T(8,128)(2,1)S(1)} %get-tuple-element.539), channel_id=1, source_target_pairs={{0,4},{4,0},{1,5},{5,1},{2,6},{6,2},{3,7},{7,3},{8,12},{12,8},{9,1... | collective-permute-start | bytes 1032200 | tf_op jit(solution)/shard_map/ppermute | solution.py:534
  369.6 19.5 %collective-permute-start.28 = (bf16[4,112,768]{2,1,0:T(8,128)(2,1)S(1)}, bf16[4,112,768]{2,1,0:T(8,128)(2,1)S(1)}, u32[]{:S(2)}, u32[]{:S(2)}) collective-permute-start(bf16[4,112,768]{2,1,0:T(8,128)(2,1)S(1)} %add_dynamic-update-slice_fusion.2), channel_id=1, source_target_pairs={{0,2},{2,0},{1,3},{3,1},{4,6},{6,4},{5,7},{7,5},{8,10},{10,8},{9,1... | collective-permute-start | bytes 2064392 | tf_op jit(solution)/shard_map/ppermute | solution.py:534
  372.9 16.9 %collective-permute-start.27 = (bf16[4,112,768]{2,1,0:T(8,128)(2,1)S(1)}, bf16[4,112,768]{2,1,0:T(8,128)(2,1)S(1)}, u32[]{:S(2)}, u32[]{:S(2)}) collective-permute-start(bf16[4,112,768]{2,1,0:T(8,128)(2,1)S(1)} %add_dynamic-update-slice_fusion.3), channel_id=1, source_target_pairs={{0,4},{4,0},{1,5},{5,1},{2,6},{6,2},{3,7},{7,3},{8,12},{12,8},{9,1... | collective-permute-start | bytes 2064392 | tf_op jit(solution)/shard_map/ppermute | solution.py:534
  373.7 24.1 %collective-permute-start.36 = (bf16[8,2304]{1,0:T(8,128)(2,1)}, bf16[8,2304]{1,0:T(8,128)(2,1)S(1)}, u32[]{:S(2)}, u32[]{:S(2)}) collective-permute-start(bf16[8,2304]{1,0:T(8,128)(2,1)} %pad_maximum_fusion.11), channel_id=1, source_target_pairs={{0,8},{8,0},{16,24},{24,16},{1,9},{9,1},{17,25},{25,17},{2,10},{10... | collective-permute-start | bytes 110600 | tf_op jit(solution)/shard_map/ppermute | solution.py:662
  373.7 22.9 %collective-permute-start.29 = (bf16[2,112,768]{2,1,0:T(8,128)(2,1)}, bf16[2,112,768]{2,1,0:T(8,128)(2,1)}, u32[]{:S(2)}, u32[]{:S(2)}) collective-permute-start(bf16[2,112,768]{2,1,0:T(8,128)(2,1)} %get-tuple-element.538), channel_id=1, source_target_pairs={{0,2},{2,0},{1,3},{3,1},{4,6},{6,4},{5,7},{7,5},{8,10},{10,8},{9,1... | collective-permute-start | bytes 1032200 | tf_op jit(solution)/shard_map/ppermute | solution.py:534
  377.0 31.0 %collective-permute-start.32 = (bf16[4,112,768]{2,1,0:T(8,128)(2,1)S(1)}, bf16[4,112,768]{2,1,0:T(8,128)(2,1)}, u32[]{:S(2)}, u32[]{:S(2)}) collective-permute-start(bf16[4,112,768]{2,1,0:T(8,128)(2,1)S(1)} %fusion.2), channel_id=1, source_target_pairs={{0,2},{2,0},{1,3},{3,1},{4,6},{6,4},{5,7},{7,5},{8,10},{10,8},{9,1... | collective-permute-start | bytes 2064392 | tf_op jit(solution)/shard_map/ppermute | solution.py:534
  390.8 7.0 %copy-start.43 = (bf16[2,1536]{1,0:T(2,128)(2,1)S(1)}, bf16[2,1536]{1,0:T(2,128)(2,1)}, u32[]{:S(2)}) copy-start(bf16[2,1536]{1,0:T(2,128)(2,1)} %copy-done.42) | copy-start | bytes 18436
  390.8 7.2 %copy-start.29 = (bf16[256,768]{1,0:T(8,128)(2,1)S(1)}, bf16[256,768]{1,0:T(8,128)(2,1)}, u32[]{:S(2)}) copy-start(bf16[256,768]{1,0:T(8,128)(2,1)} %get-tuple-element.435) | copy-start | bytes 1179652
  390.8 7.2 %copy-start.30 = (bf16[256,768]{1,0:T(8,128)(2,1)S(1)}, bf16[256,768]{1,0:T(8,128)(2,1)}, u32[]{:S(2)}) copy-start(bf16[256,768]{1,0:T(8,128)(2,1)} %get-tuple-element.436) | copy-start | bytes 1179652
  390.8 47.4 %reduce-scatter.7.cloned.1.call-start = ((), (), s32[]{:S(2)}) async-start(), calls=%async_computation.5 | async-start | bytes 860160 | tf_op jit(solution)/shard_map/reduce_scatter | solution.py:622
  397.7 11.1 %collective-permute-start.30 = (bf16[4,112,768]{2,1,0:T(8,128)(2,1)S(1)}, bf16[4,112,768]{2,1,0:T(8,128)(2,1)}, u32[]{:S(2)}, u32[]{:S(2)}) collective-permute-start(bf16[4,112,768]{2,1,0:T(8,128)(2,1)S(1)} %fusion.3), channel_id=1, source_target_pairs={{0,4},{4,0},{1,5},{5,1},{2,6},{6,2},{3,7},{7,3},{8,12},{12,8},{9,1... | collective-permute-start | bytes 2064392 | tf_op jit(solution)/shard_map/ppermute | solution.py:534
  397.9 9.8 %collective-permute-start.37 = (bf16[16,2304]{1,0:T(8,128)(2,1)S(1)}, bf16[16,2304]{1,0:T(8,128)(2,1)S(1)}, u32[]{:S(2)}, u32[]{:S(2)}) collective-permute-start(bf16[16,2304]{1,0:T(8,128)(2,1)S(1)} %pad_maximum_fusion.10), channel_id=1, source_target_pairs={{0,16},{8,24},{16,0},{24,8},{1,17},{9,25},{17,1},{25,9},{2,18},{10... | collective-permute-start | bytes 221192 | tf_op jit(solution)/shard_map/ppermute | solution.py:662
  (36 other events, 89.6 us)
Sparse Core Ops, SparseCore 0:
  10.2 38.6 all-gather.5
  51.8 118.9 all-gather.7
  176.8 141.8 reduce-scatter.8
  357.4 30.4 reduce-scatter.10
  390.9 23.5 reduce-scatter.4
  416.7 21.4 reduce-scatter.6

commit v3 on v2

--- a/solution.py
+++ b/solution.py
@@ -32,15 +32,19 @@
     return jax.ShapeDtypeStruct((rows, cols), dtype)
 
 
-def call(kernel, out_shapes, scratch, *args, far=()):
+def call(kernel, out_shapes, scratch, work, *args, far=(), far_outs=0, wait=()):
+    before, ahead = len(args) + len(far), len(wait)
+    inner = kernel
+    kernel = lambda *refs: inner(*refs[:before], *refs[before + ahead :])
     return list(pl.pallas_call(
         kernel,
         out_shape=out_shapes,
-        in_specs=[SMEM if a.ndim == 1 else VMEM for a in args] + [pl.BlockSpec(memory_space=pl.ANY)] * len(far),
-        out_specs=[VMEM] * len(out_shapes),
+        in_specs=[SMEM if a.ndim == 1 else VMEM for a in args] + [pl.BlockSpec(memory_space=pl.ANY)] * (len(far) + ahead),
+        out_specs=[VMEM] * (len(out_shapes) - far_outs) + [pl.BlockSpec(memory_space=pl.ANY)] * far_outs,
         scratch_shapes=scratch,
         compiler_params=pltpu.CompilerParams(vmem_limit_bytes=VMEM_BYTES),
-    )(*args, *far))
+        cost_estimate=pl.CostEstimate(flops=int(work * 1.15e9), bytes_accessed=0, transcendentals=0),
+    )(*args, *far, *wait))
 
 
 VMEM_BYTES = 56 * 1024 * 1024
@@ -157,17 +161,29 @@
         ]
     return call(
         functools.partial(attention_forward_kernel, slabs, depth),
-        shapes, scratch, x, marks[0], marks[1], *args, far=far,
+        shapes, scratch, 15, x, marks[0], marks[1], *args, far=far,
     )
 
 
-def attention_backward_kernel(halves, fix, clear_first, qkv, mix, lse_rows, seg_row, key_col, wt, *refs):
+def attention_backward_kernel(fix, clear_first, depth, natural, n_small, *refs):
     refs = list(refs)
-    dmix, refs = refs[:halves], refs[halves:]
-    dr1, refs = refs[:halves], refs[halves:]
-    if fix:
-        dmix_fix, dr1_fix, *refs = refs
-    dqkv, sums, dx, first, mask, dq_sum = refs
+    take = lambda n: [refs.pop(0) for _ in range(n)]
+    grads = depth > 0
+    (at,) = take(1) if grads else (None,)
+    qkv, mix, lse_rows, seg_row, key_col, dmix = take(6)
+    dmix_fix, dr1_fix = take(2) if fix else (None, None)
+    (do_fix,) = take(1) if fix and grads else (None,)
+    smalls, ups = take(n_small), take(n_small)
+    far = take(4 if grads else 2)
+    if grads:
+        dx, first, sent, kept, mask, dq_sum, dqkv, all_qkv, all_out, lines, *near, sems = refs
+        wt, dr1, x, do = near
+    else:
+        dqkv, sums, dx, first, mask, dq_sum, *near, sems = refs
+        wt, dr1 = near
+    copies = [pltpu.make_async_copy(a, b, sems.at[i]) for i, (a, b) in enumerate(zip(far, near))]
+    for copy in copies:
+        copy.start()
     length, width = mix.shape
     for t, low, high in windows(length):
         keys = lax.broadcasted_iota(jnp.int32, (high - low, LANES), 0) + low
@@ -176,16 +192,16 @@
         mask[t, : high - low, :] = jnp.where(same | (rows == keys), 0.0, MASKED)
 
     def pair(p, carry):
-        at = pl.multiple_of(p * LANES, LANES)
-        at_k = pl.multiple_of(at + width, LANES)
-        at_v = pl.multiple_of(at + 2 * width, LANES)
+        at_q = pl.multiple_of(p * LANES, LANES)
+        at_k = pl.multiple_of(at_q + width, LANES)
+        at_v = pl.multiple_of(at_q + 2 * width, LANES)
         lane = lax.broadcasted_iota(jnp.int32, (length, LANES), 1)
-        q = qkv[:, pl.ds(at, LANES)] * HEAD_DIM ** (-0.5)
-        dm = jnp.concatenate([half[:, pl.ds(at, LANES)] for half in dmix], 0)
+        q = qkv[:, pl.ds(at_q, LANES)] * HEAD_DIM ** (-0.5)
+        dm = dmix[:, pl.ds(at_q, LANES)]
         if fix:
             n = dmix_fix.shape[0]
-            dm = jnp.concatenate([dm[:n] + dmix_fix[:, pl.ds(at, LANES)], dm[n:]], 0)
-        product = dm.astype(F32) * mix[:, pl.ds(at, LANES)].astype(F32)
+            dm = jnp.concatenate([dm[:n] + dmix_fix[:, pl.ds(at_q, LANES)], dm[n:]], 0)
+        product = dm.astype(F32) * mix[:, pl.ds(at_q, LANES)].astype(F32)
         ones_lane = lax.broadcasted_iota(jnp.int32, (8, LANES), 1)
         q_h, dm_h, lse_h, delta_h = [], [], [], []
         for h in range(2):
@@ -226,60 +242,43 @@
             dqkv[here, pl.ds(at_k, LANES)] = dk.astype(BF)
             dqkv[here, pl.ds(at_v, LANES)] = dv.astype(BF)
             dq_sum[low:high, :] += dq
-        dqkv[:, pl.ds(at, LANES)] = (dq_sum[...] * HEAD_DIM ** (-0.5)).astype(BF)
+        dqkv[:, pl.ds(at_q, LANES)] = (dq_sum[...] * HEAD_DIM ** (-0.5)).astype(BF)
         return carry
 
     lax.fori_loop(0, width // LANES, pair, 0)
-    sums[...] = jnp.zeros_like(sums)
-    for row, part in ((0, 0), (1, 2)):
-        cols = slice(part * width, (part + 1) * width)
-        sums[row : row + 1, :] = mm(jnp.ones((8, length), BF), dqkv[:, cols])[:1, :]
-    count = length // halves
-    for i in range(halves):
-        rows = slice(i * count, (i + 1) * count)
-        out = mm(dqkv[rows, :], wt[...]) + dr1[i][...]
-        if i == 0:
-            if fix:
-                n = dr1_fix.shape[0]
-                out = jnp.concatenate([out[:n] + dr1_fix[...], out[n:]], 0)
-            first[...] = out[: first.shape[0]]
-            if clear_first:
-                out = jnp.where(lax.broadcasted_iota(jnp.int32, out.shape, 0) == 0, 0.0, out)
-        dx[rows, :] = out
-
-
-def attention_backward(qkv, mix, lse_rows, marks, wt, dmix, dr1, fix=(), clear_first=False):
-    length, width = mix.shape
-    shapes = [shape(length, 3 * width), shape(8, width, F32), shape(length, width, F32), shape(16, width, F32)]
-    scratch = [
-        pltpu.VMEM((length // LANES, 3 * LANES, LANES), F32),
-        pltpu.VMEM((length, LANES), F32),
+    for copy in copies:
+        copy.wait()
+    sum_rows = [
+        mm(jnp.ones((8, length), BF), dqkv[:, part * width : (part + 1) * width])[:1, :] for part in (0, 2)
     ]
-    return call(
-        functools.partial(attention_backward_kernel, len(dmix), bool(fix), clear_first),
-        shapes, scratch, qkv, mix, lse_rows, marks[0], marks[1], wt, *dmix, *dr1, *fix,
-    )
-
-
-def attention_grads_kernel(depth, n_small, natural, at, dqkv, x, do, mix, *refs):
-    refs = list(refs)
-    smalls, ups, refs = refs[:n_small], refs[n_small : 2 * n_small - 1], refs[2 * n_small - 1 :]
-    sent, here, by_y, by_x, both_a, both_b, all_qkv, all_out, lines = refs
-    width = x.shape[1]
+    if not grads:
+        sums[...] = jnp.concatenate([*sum_rows, jnp.zeros((6, width), F32)], 0)
+    out = mm(dqkv[...], wt[...]) + dr1[...]
+    if fix:
+        n = dr1_fix.shape[0]
+        out = jnp.concatenate([out[:n] + dr1_fix[...], out[n:]], 0)
+    first[...] = out[: first.shape[0]]
+    if clear_first:
+        out = jnp.where(lax.broadcasted_iota(jnp.int32, out.shape, 0) == 0, 0.0, out)
+    dx[...] = out
+    if not grads:
+        return
     n_qkv, n_out = 3 * width // (PARTS * depth), width // (PARTS * depth)
     for part in range(3):
         rows = slice(part * width, (part + 1) * width)
         all_qkv[rows, :] = mm(dqkv[:, rows], x[...], TN)
+    if fix:
+        n = do_fix.shape[0]
+        do[:n, :] = do[:n, :] + do_fix[...]
     all_out[...] = mm(do[...], mix[...], TN)
-    small = sum(s[...] for s in smalls)
+    small = jnp.concatenate([*sum_rows, jnp.zeros((6, width), F32)], 0) + sum(s[...] for s in smalls)
     up = sum(u[...] for u in ups)
     up = jnp.concatenate([up, jnp.zeros((PARTS, width - up.shape[1]), F32)], 1)
     for part in range(PARTS):
         lines[part] = up[part : part + 1]
-    half = both_a.shape[0]
-    for part in (4, 5, 6, 7, 3, 1, 2, 0):
+    line = lax.broadcasted_iota(jnp.int32, (SMALL_ROWS - 8, width), 0) == 0
+    for part in range(PARTS):
         place = far_place(at, part)
-        line = lax.broadcasted_iota(jnp.int32, (SMALL_ROWS - 8, width), 0) == 0
         for i in range(depth):
             device = i * PARTS + place
             tail = [small, jnp.where(line, lines[lax.div(device, depth) if natural else part], 0.0)]
@@ -291,25 +290,31 @@
                 ],
                 0,
             ).astype(BF)
-            if part > 3:
-                sent[part - 4, i] = slab
-            elif part == 3:
-                (both_a if i < half else both_b)[i % half] = slab
-            else:
-                (here, by_y, by_x)[part][i] = slab
-
-
-def attention_grads(depth, at, natural, dqkv, x, do, mix, smalls, ups):
-    length, width = x.shape
-    rows = 4 * width // (PARTS * depth) + SMALL_ROWS
-    out = lambda *lead: jax.ShapeDtypeStruct((*lead, rows, width), BF)
-    shapes = [out(4, depth), out(depth), out(depth), out(depth), out(depth // 2), out(depth // 2)]
+            (sent if part > 3 else kept)[part % 4, i] = slab
+
+
+def attention_backward(qkv, mix, lse_rows, marks, dmix, fix, far, clear_first, depth=0, at=None, smalls=(), ups=(), natural=False, wait=()):
+    length, width = mix.shape
+    tail = [shape(length, width, F32), shape(16, width, F32)]
     scratch = [
-        pltpu.VMEM((3 * width, width), F32), pltpu.VMEM((width, width), F32), pltpu.VMEM((PARTS, 1, width), F32),
+        pltpu.VMEM((length // LANES, 3 * LANES, LANES), F32),
+        pltpu.VMEM((length, LANES), F32),
     ]
+    args = [qkv, mix, lse_rows, marks[0], marks[1], dmix, *fix, *smalls, *ups]
+    if depth:
+        rows = 4 * width // (PARTS * depth) + SMALL_ROWS
+        shapes = tail + [jax.ShapeDtypeStruct((4, depth, rows, width), BF)] * 2
+        scratch += [
+            pltpu.VMEM((length, 3 * width), BF), pltpu.VMEM((3 * width, width), F32), pltpu.VMEM((width, width), F32),
+            pltpu.VMEM((PARTS, 1, width), F32),
+        ]
+        args = [at, *args]
+    else:
+        shapes = [shape(length, 3 * width), shape(8, width, F32)] + tail
+    scratch += [pltpu.VMEM(a.shape, a.dtype) for a in far] + [pltpu.SemaphoreType.DMA((len(far),))]
     return call(
-        functools.partial(attention_grads_kernel, depth, len(smalls), natural),
-        shapes, scratch, at, dqkv, x, do, mix, *smalls, *ups,
+        functools.partial(attention_backward_kernel, bool(fix), clear_first, depth, natural, len(smalls)),
+        shapes, scratch, 22, *args, far=far, wait=wait,
     )
 
 
@@ -337,101 +342,173 @@
     return jnp.where(u > 0, 1.0 - tail, tail), bell * (1.0 / math.sqrt(2.0 * math.pi))
 
 
-def feed_kernel(pieces_at, skip_rows, start, clear_first, backward, *refs):
+def feed_kernel(mode, pieces_at, skip_rows, clear_first, depth, *refs):
     refs = list(refs)
     take = lambda n: [refs.pop(0) for _ in range(n)]
+    (at,) = take(1) if depth else (None,)
     x, mix, w_out, vectors, up_bias = take(5)
+    backward = mode != "forward"
     (cot,) = take(1) if backward else (None,)
     pieces = take(len(pieces_at))
+    (y,) = take(1)
     if backward:
-        y, n1_out, g_out, du_out, df_out, do_out, dr1_out, dm_out, small, up_small, slabs, sems, slope = refs
+        do_out, dr1_out, dm_out, small, up_small = take(5)
+        if mode == "rows":
+            n1_s, g_s, du_s, df_s = take(4)
+        elif mode == "order":
+            (whole,) = take(1)
+        else:
+            sent, kept = take(2)
+    slabs, sems, z1_s, q1_s = take(4)
+    if backward:
+        (slope,) = take(1)
+        if mode != "rows":
+            n1_s, g_s, du_s, df_s, stage, out_sems = take(6)
         small[...] = jnp.zeros_like(small)
         up_small[...] = jnp.zeros_like(up_small)
     else:
-        y, slabs, sems = refs
+        (n1_s,) = take(1)
     count, width = y.shape
     half = slabs.shape[1] // 2
     each = slabs.shape[0] // PARTS
     copies = []
-    for i, (piece, at) in enumerate(zip(pieces, pieces_at)):
-        n = piece.shape[0]
+    for i, (piece, begin) in enumerate(zip(pieces, pieces_at)):
         copies.append(
-            pltpu.make_async_copy(piece.at[:, pl.ds(skip_rows, 2 * half), :], slabs.at[pl.ds(at, n)], sems.at[i])
+            pltpu.make_async_copy(
+                piece.at[:, pl.ds(skip_rows, 2 * half), :], slabs.at[pl.ds(begin, piece.shape[0])], sems.at[i]
+            )
         )
         copies[-1].start()
 
     def weights(part, lower):
-        for copy, at in zip(list(copies), pieces_at):
-            if copy is not None and at < (part + 1) * each:
-                copy.wait()
-                copies[copies.index(copy)] = None
         top = half if lower else 0
         return slabs[part * each : (part + 1) * each, top : top + half, :].reshape(each * half, width)
 
     b_out, b_down, shift_one, shift_two, gain_one, gain_two = (vectors[i : i + 1, :] for i in range(2, 8))
-    here = slice(start, start + count)
-    r1 = x[here, :].astype(F32) + mm(mix[here, :], w_out[...], NT) + b_out
+    r1 = x[:count, :].astype(F32) + mm(mix[:count, :], w_out[...], NT) + b_out
     z1, q1 = norm(r1)
-    n1 = (z1 * gain_one + shift_one).astype(BF)
-    acc = n1.astype(F32) + b_down
+    z1_s[...] = z1
+    q1_s[...] = q1
+    n1_s[...] = (z1 * gain_one + shift_one).astype(BF)
+    for copy in copies:
+        copy.wait()
+    tile = min(256, count)
+
+    def rows_step(i, carry):
+        here = pl.ds(pl.multiple_of(i * tile, tile), tile)
+        n1 = n1_s[here, :]
+        acc = n1.astype(F32) + b_down
+        for part in range(PARTS):
+            u = mm(n1, weights(part, False), NT) + up_bias[part : part + 1, :]
+            size = u.shape[1]
+            cols = slice(part * size, (part + 1) * size)
+            big, bell = normal_terms(u)
+            g = (u * big).astype(BF)
+            if backward:
+                g_s[here, cols] = g
+                slope[:, cols] = big + u * bell
+            acc += mm(g, weights(part, True))
+        z2, q2 = norm(acc)
+        y[here, :] = (z2 * gain_two + shift_two).astype(BF)
+        if backward:
+            e = cot[here, :].astype(F32)
+            if clear_first:
+                e = jnp.where(lax.broadcasted_iota(jnp.int32, e.shape, 0) + i * tile == 0, 0.0, e)
+            small[5:6, :] += jnp.sum(e, 0, keepdims=True)
+            small[7:8, :] += jnp.sum(e * z2, 0, keepdims=True)
+            dr2 = norm_back(e, z2, q2, gain_two)
+            df = dr2.astype(BF)
+            df_s[here, :] = df
+            small[3:4, :] += jnp.sum(df.astype(F32), 0, keepdims=True)
+            dn1 = dr2
+            for part in range(PARTS):
+                da = mm(df, weights(part, True), NT)
+                size = da.shape[1]
+                cols = slice(part * size, (part + 1) * size)
+                du = (da * slope[:, cols]).astype(BF)
+                du_s[here, cols] = du
+                up_small[part : part + 1, :] += jnp.sum(du.astype(F32), 0, keepdims=True)
+                dn1 += mm(du, weights(part, False))
+            z1 = z1_s[here, :]
+            small[4:5, :] += jnp.sum(dn1, 0, keepdims=True)
+            small[6:7, :] += jnp.sum(dn1 * z1, 0, keepdims=True)
+            dr1 = norm_back(dn1, z1, q1_s[here, :], gain_one)
+            do = dr1.astype(BF)
+            small[2:3, :] += jnp.sum(do.astype(F32), 0, keepdims=True)
+            dm_out[here, :] = mm(do, w_out[...]).astype(BF)
+            do_out[here, :] = do
+            dr1_out[here, :] = dr1
+        return carry
+
+    lax.fori_loop(0, count // tile, rows_step, 0)
+    if mode not in ("order", "spread"):
+        return
     for part in range(PARTS):
-        u = mm(n1, weights(part, False), NT) + up_bias[part : part + 1, :]
-        size = u.shape[1]
+        slot = part % 2
+        if part > 1:
+            for i in range(depth):
+                pltpu.make_async_copy(stage.at[slot, i], stage.at[slot, i], out_sems.at[slot, i]).wait()
+        size = g_s.shape[1] // PARTS
         cols = slice(part * size, (part + 1) * size)
-        big, bell = normal_terms(u)
-        g = (u * big).astype(BF)
-        if backward:
-            g_out[:, cols] = g
-            slope[:, cols] = big + u * bell
-        acc += mm(g, weights(part, True))
-    z2, q2 = norm(acc)
-    y[...] = (z2 * gain_two + shift_two).astype(BF)
-    if backward:
-        e = cot[here, :].astype(F32)
-        if clear_first:
-            e = jnp.where(lax.broadcasted_iota(jnp.int32, e.shape, 0) + start == 0, 0.0, e)
-        small[5:6, :] += jnp.sum(e, 0, keepdims=True)
-        small[7:8, :] += jnp.sum(e * z2, 0, keepdims=True)
-        dr2 = norm_back(e, z2, q2, gain_two)
-        df = dr2.astype(BF)
-        small[3:4, :] += jnp.sum(df.astype(F32), 0, keepdims=True)
-        dn1 = dr2
-        for part in range(PARTS):
-            da = mm(df, weights(part, True), NT)
-            size = da.shape[1]
-            cols = slice(part * size, (part + 1) * size)
-            du = (da * slope[:, cols]).astype(BF)
-            du_out[:, cols] = du
-            up_small[part : part + 1, :] += jnp.sum(du.astype(F32), 0, keepdims=True)
-            dn1 += mm(du, weights(part, False))
-        small[4:5, :] += jnp.sum(dn1, 0, keepdims=True)
-        small[6:7, :] += jnp.sum(dn1 * z1, 0, keepdims=True)
-        dr1 = norm_back(dn1, z1, q1, gain_one)
-        do = dr1.astype(BF)
-        small[2:3, :] += jnp.sum(do.astype(F32), 0, keepdims=True)
-        dm_out[...] = mm(do, w_out[...]).astype(BF)
-        n1_out[...] = n1
-        df_out[...] = df
-        do_out[...] = do
-        dr1_out[...] = dr1
-
-
-def feed(x, mix, w_out, vectors, up_bias, pieces, pieces_at, cot=None, start=0, count=None, clear_first=False, skip_rows=0):
+        for lower, (left, right) in enumerate(((du_s, n1_s), (g_s, df_s))):
+            full = mm(left[:, cols], right[...], TN).astype(BF).reshape(depth, half, width)
+            stage[slot, :, lower * half : (lower + 1) * half, :] = full
+        for i in range(depth):
+            src, sem = stage.at[slot, i], out_sems.at[slot, i]
+            if mode == "order":
+                pltpu.make_async_copy(src, whole.at[i * PARTS + far_place(at, part)], sem).start()
+            else:
+                device = part * depth + i
+                z, y_bit, x_bit, core_bit = device // PARTS, device // 4 % 2, device // 2 % 2, device % 2
+                code = (at[0] ^ y_bit) + 2 * (at[1] ^ x_bit)
+
+                @pl.when(at[2] == core_bit)
+                def _():
+                    pltpu.make_async_copy(src, kept.at[code, z], sem).start()
+
+                @pl.when(at[2] != core_bit)
+                def _():
+                    pltpu.make_async_copy(src, sent.at[code, z], sem).start()
+
+    for slot in range(2):
+        for i in range(depth):
+            pltpu.make_async_copy(stage.at[slot, i], stage.at[slot, i], out_sems.at[slot, i]).wait()
+
+
+def feed(mode, x, mix, w_out, vectors, up_bias, pieces, pieces_at, cot=None, count=None, clear_first=False, skip_rows=0, depth=0, at=None, wait=()):
     width = x.shape[1]
     count = count or x.shape[0]
     hidden = PARTS * up_bias.shape[1]
     wide, high = shape(count, width), shape(count, hidden)
     rows = pieces[0].shape[1] - skip_rows
+    tile = min(256, count)
     shapes = [wide]
-    scratch = [pltpu.VMEM((2 * hidden // rows, rows, width), BF), pltpu.SemaphoreType.DMA((len(pieces),))]
+    scratch = [
+        pltpu.VMEM((2 * hidden // rows, rows, width), BF), pltpu.SemaphoreType.DMA((len(pieces),)),
+        pltpu.VMEM((count, width), F32), pltpu.VMEM((count, 1), F32),
+    ]
     args = [x, mix, w_out, vectors, up_bias]
-    if cot is not None:
+    far_outs = 0
+    kept = [wide, high, high, wide]
+    in_vmem = [pltpu.VMEM(k.shape, BF) for k in kept]
+    if mode == "forward":
+        scratch.append(in_vmem[0])
+    else:
         args.append(cot)
-        shapes += [wide, high, high, wide, wide, shape(count, width, F32), wide, shape(8, width, F32), shape(*up_bias.shape, F32)]
-        scratch.append(pltpu.VMEM((count, hidden), F32))
+        shapes += [wide, shape(count, width, F32), wide, shape(8, width, F32), shape(*up_bias.shape, F32)]
+        scratch.append(pltpu.VMEM((tile, hidden), F32))
+        if mode == "rows":
+            shapes += kept
+        else:
+            scratch += in_vmem + [pltpu.VMEM((2, depth, rows, width), BF), pltpu.SemaphoreType.DMA((2, depth))]
+            out = lambda *lead: jax.ShapeDtypeStruct((*lead, rows, width), BF)
+            outs = [out(PARTS * depth)] if mode == "order" else [out(4, depth), out(4, depth)]
+            shapes += outs
+            far_outs = len(outs)
+            args = [at, *args]
     return call(
-        functools.partial(feed_kernel, pieces_at, skip_rows, start, clear_first, cot is not None),
-        shapes, scratch, *args, far=pieces,
+        functools.partial(feed_kernel, mode, pieces_at, skip_rows, clear_first, depth),
+        shapes, scratch, 40 if count > 16 else 12, *args, far=pieces, far_outs=far_outs, wait=wait,
     )
 
 
@@ -464,66 +541,34 @@
     outs = [jax.ShapeDtypeStruct((*lead, width), BF) for lead in shapes]
     return call(
         functools.partial(feed_grads_kernel, first, layout, len(n1), len(received)),
-        outs, [], *n1, *df, *g, *du, *received,
+        outs, [], 8, *n1, *df, *g, *du, *received,
     )
 
 
-def feed_grads_all(halves_n, depth, half, n1, df, g, du, store):
-    for part in range(PARTS):
-        size = g[0].shape[1] // PARTS
-        cols = slice(part * size, (part + 1) * size)
-        for lower, (left, right) in enumerate(((du, n1), (g, df))):
-            full = sum(mm(a[:, cols], b[...], TN) for a, b in zip(left, right)).astype(BF)
-            store(part, lower, full.reshape(depth, half, -1))
-
-
-def feed_grads_spread_kernel(depth, halves, at, *refs):
-    refs = list(refs)
-    n1, df, g, du = (refs[i * halves : (i + 1) * halves] for i in range(4))
-    sent, here, by_y, by_x, both_a, both_b, all_rows = refs[4 * halves :]
-    half = all_rows.shape[1] // 2
-
-    def store(part, lower, value):
-        all_rows[part * depth : (part + 1) * depth, lower * half : (lower + 1) * half, :] = value
-
-    feed_grads_all(halves, depth, half, n1, df, g, du, store)
-    split = both_a.shape[0]
-    for part in (4, 5, 6, 7, 3, 1, 2, 0):
-        place = far_place(at, part)
-        for i in range(depth):
-            slab = all_rows[i * PARTS + place]
-            if part > 3:
-                sent[part - 4, i] = slab
-            elif part == 3:
-                (both_a if i < split else both_b)[i % split] = slab
-            else:
-                (here, by_y, by_x)[part][i] = slab
-
-
-def feed_grads_order_kernel(depth, halves, at, *refs):
-    refs = list(refs)
-    n1, df, g, du = (refs[i * halves : (i + 1) * halves] for i in range(4))
-    (out,) = refs[4 * halves :]
-    half = out.shape[1] // 2
-
-    def store(part, lower, value):
-        place = far_place(at, part)
-        for i in range(depth):
-            out[i * PARTS + place, lower * half : (lower + 1) * half, :] = value[i]
-
-    feed_grads_all(halves, depth, half, n1, df, g, du, store)
-
-
-def feed_grads_natural(spread, depth, half, at, n1, df, g, du):
-    width = n1[0].shape[1]
-    out = lambda *lead: jax.ShapeDtypeStruct((*lead, 2 * half, width), BF)
-    if spread:
-        shapes = [out(4, depth), out(depth), out(depth), out(depth), out(depth // 2), out(depth // 2)]
-        scratch = [pltpu.VMEM((PARTS * depth, 2 * half, width), BF)]
-    else:
-        shapes, scratch = [out(PARTS * depth)], []
-    kernel = feed_grads_spread_kernel if spread else feed_grads_order_kernel
-    return call(functools.partial(kernel, depth, len(n1)), shapes, scratch, at, *n1, *df, *g, *du)
+def add_parts_kernel(kept, received, here, by_y, by_x, both_a, both_b):
+    half = both_a.shape[0]
+    for part, out in enumerate((here, by_y, by_x)):
+        out[...] = kept[part] + received[part]
+    both_a[...] = kept[3, :half] + received[3, :half]
+    both_b[...] = kept[3, half:] + received[3, half:]
+
+
+def add_parts(kept, received, wait=()):
+    depth, rows, width = kept.shape[1:]
+    out = lambda n: jax.ShapeDtypeStruct((n, rows, width), BF)
+    shapes = [out(depth), out(depth), out(depth), out(depth // 2), out(depth // 2)]
+    return call(add_parts_kernel, shapes, [], 4, kept, received, wait=wait)
+
+
+def join_kernel(one, one_y, one_x, two, two_y, two_x, out):
+    rows = one.shape[1]
+    out[:, :rows, :] = one[...] + one_y[...] + one_x[...]
+    out[:, rows:, :] = two[...] + two_y[...] + two_x[...]
+
+
+def join(one, two, wait=()):
+    depth, rows, width = one[0].shape
+    return call(join_kernel, [jax.ShapeDtypeStruct((depth, 2 * rows, width), BF)], [], 3, *one, *two, wait=wait)[0]
 
 
 def after(values, *before):
@@ -586,27 +631,19 @@
         out = attention_forward(x, marks, pieces, self.at, slabs, self.depth, self.n_up)
         return dict(zip(("x", "qkv", "mix", "lse", "wt", "wt_out", "small", "up_bias"), [x, *out]))
 
-    def feed(self, kept, pieces, cot, start, count, clear_first=False):
-        pieces_at = [part * self.depth + first for part, first in self.slabs][: len(pieces)]
+    def feed(self, mode, kept, pieces, cot, count=None, clear_first=False, wait=()):
+        if len(pieces) > 1:
+            pieces_at = [part * self.depth + first for part, first in self.slabs]
+        else:
+            pieces_at = [0]
+        grads = mode != "rows"
         out = feed(
-            kept["x"], kept["mix"], kept["wt_out"], kept["small"], kept["up_bias"], pieces, pieces_at,
-            cot, start, count, clear_first, pieces[0].shape[1] - 2 * self.n_up,
+            mode, kept["x"], kept["mix"], kept["wt_out"], kept["small"], kept["up_bias"], pieces, pieces_at,
+            cot, count, clear_first, pieces[0].shape[1] - 2 * self.n_up,
+            self.depth if grads else 0, self.at if grads else None, wait,
         )
-        return dict(zip(("y", "n1", "g", "du", "df", "do", "dr1", "dm", "small", "up"), out))
-
-    def feed_sent(self, halves):
-        lists = [[h[name] for h in halves] for name in ("n1", "df", "g", "du")]
-        (sent,) = feed_grads(4, [(4, self.depth, 2 * self.n_up)], None, *lists)
-        return sent
-
-    def feed_kept(self, halves, received):
-        lists = [[h[name] for h in halves] for name in ("n1", "df", "g", "du")]
-        full, half = (self.depth, 2 * self.n_up), (self.depth // 2, 2 * self.n_up)
-        return feed_grads(0, [full, full, full, half, half], [1, 1, 1, 2], *lists, received)
-
-    def feed_natural(self, halves, spread):
-        lists = [[h[name] for h in halves] for name in ("n1", "df", "g", "du")]
-        return feed_grads_natural(spread, self.depth, self.n_up, self.at, *lists)
+        last = {"rows": ("n1", "g", "du", "df"), "order": ("all",), "spread": ("sent", "kept")}[mode]
+        return dict(zip(("y", "do", "dr1", "dm", "small", "up") + last, out))
 
     def reduce_diagonal(self, both):
         return [swap(both[0], "x"), swap(both[1], "y")]
@@ -621,19 +658,12 @@
     def reduce_z(self, here, got):
         return lax.psum_scatter(here + got[0] + got[1], "z", scatter_dimension=0, tiled=False)
 
-    def attention_grads(self, kept, dqkv, do, smalls, ups, natural):
-        sent, here, by_y, by_x, both_a, both_b = attention_grads(
-            self.depth, self.at, natural, dqkv, kept["x"], do, kept["mix"], smalls, ups
+    def attend_back(self, kept, marks, back, fix, clear_first, natural, wait=()):
+        smalls, ups = [f["small"] for f in [back, *fix]], [f["up"] for f in [back, *fix]]
+        return attention_backward(
+            kept["qkv"], kept["mix"], kept["lse"], marks, back["dm"], [f[n] for f in fix for n in ("dm", "dr1", "do")],
+            [kept["wt"], back["dr1"], kept["x"], back["do"]], clear_first, self.depth, self.at, smalls, ups, natural, wait,
         )
-        return sent, [here, by_y, by_x, both_a, both_b]
-
-    def add_received(self, kept, received):
-        half = self.depth // 2
-        here, by_y, by_x, both_a, both_b = kept
-        return [
-            here + received[0], by_y + received[1], by_x + received[2],
-            both_a + received[3, :half], both_b + received[3, half:],
-        ]
 
     def attention_outs(self, total, natural):
         total = total.astype(F32)
@@ -673,7 +703,6 @@
     link = Near(shards)
     marks = marks_of(lengths, segments)
     length = segments.shape[1]
-    half = length // 2
     is_first = lax.broadcasted_iota(jnp.int32, (length, 1), 0) == 0
 
     slab_a1, slab_m1 = link.slab_pair(0)
@@ -682,62 +711,55 @@
     b2 = [lax.all_gather(after(jnp.concatenate(link.slab_pair(1), 0), a1), link.axes, axis=0, tiled=False)]
     a1 = link.near(a1)
     a1 += link.diagonal(a1)
-    m1 = link.near(after(m1, a1))
+    m1 = link.near(after(m1, a1[:3]))
     a1 += swaps(a1, "core")
     one = link.attend(*after((tokens, marks, a1), m1[0]))
     m1 = after(m1, one["mix"])
     m1 += link.diagonal(m1)
     m1 += swaps(m1, "core")
-    one_a = link.feed(one, m1, cot_first, 0, half, True)
-    one_b = link.feed(*after((one, m1, cot_first), one_a["y"]), half, half)
-    (all_m1,) = link.feed_natural([one_a, one_b], False)
-    sum_m1 = lax.psum_scatter(all_m1, link.axes, scatter_dimension=0, tiled=False).astype(F32)
-    out_first = jnp.concatenate([one_a["y"], one_b["y"]], 0)
+    back_one = link.feed("order", one, m1, cot_first, None, True)
+    sum_m1 = lax.psum_scatter(back_one["all"], link.axes, scatter_dimension=0, tiled=False)
+    out_first = back_one["y"]
     second_in = jnp.where(is_first, out_first, skip_tokens)
-    two = link.attend(*after((second_in, marks), all_m1), b2)
-    two_a = link.feed(*after((two, b2, cot_second), two["mix"]), 0, half)
-    two_b = link.feed(*after((two, b2, cot_second), two_a["y"]), half, half)
-    sent_m2, *kept_m2 = link.feed_natural([two_a, two_b], True)
-    dqkv2, sums2, grad_skip, first2 = attention_backward(
-        two["qkv"], two["mix"], two["lse"], marks, two["wt"],
-        *after(([two_a["dm"], two_b["dm"]], [two_a["dr1"], two_b["dr1"]]), kept_m2), clear_first=True,
+    two = link.attend(second_in, marks, b2)
+    back_two = link.feed("spread", two, b2, cot_second)
+    received_m2 = swap(back_two["sent"], "core")
+    grad_skip, first2, sent_a2, kept_a2 = link.attend_back(two, marks, back_two, [], True, True)
+    kept_m2, received_m2, sent_a2, kept_a2 = after((back_two["kept"], received_m2, sent_a2, kept_a2), first2)
+    received_a2 = swap(sent_a2, "core")
+    kept_m2 = add_parts(kept_m2, received_m2)
+    got_m2 = link.reduce_diagonal(kept_m2[3:])
+    kept_a2 = add_parts(kept_a2, received_a2)
+    got_a2 = link.reduce_diagonal(kept_a2[3:])
+    upstream = jnp.where(is_first[:16], cot_first[:16].astype(F32) + first2, 0.0)
+    fix = link.feed("rows", one, m1, after(upstream, kept_m2, kept_a2), 16)
+    kept_m2, got_m2, kept_a2, got_a2 = after((kept_m2, got_m2, kept_a2, got_a2), fix["y"])
+    added_m2 = link.add_diagonal(*kept_m2[1:3], got_m2)
+    got_m2 = link.reduce_near(added_m2)
+    grad_tokens, _, sent_a1, kept_a1 = link.attend_back(
+        one, marks, *after((back_one, [fix]), added_m2), False, False
     )
-    kept_m2 = link.add_received(*after((kept_m2, swap(sent_m2, "core")), dqkv2))
-    got_m2 = link.reduce_diagonal(kept_m2[3:])
-    upstream = jnp.where(is_first[:16], cot_first[:16].astype(F32) + first2, 0.0)
-    fix = link.feed(one, m1, after(upstream, kept_m2), 0, 16)
-    added_m2 = link.add_diagonal(*after((kept_m2[1], kept_m2[2], got_m2), fix["y"]))
-    got_m2 = link.reduce_near(added_m2)
-    dqkv1, sums1, grad_tokens, _ = attention_backward(
-        one["qkv"], one["mix"], one["lse"], marks, one["wt"],
-        *after(([one_a["dm"], one_b["dm"]], [one_a["dr1"], one_b["dr1"]]), added_m2), fix=(fix["dm"], fix["dr1"]),
+    kept_m2, got_m2, kept_a2, got_a2, sent_a1, sum_m1 = after(
+        (kept_m2, got_m2, kept_a2, got_a2, sent_a1, sum_m1), kept_a1
     )
-    fix, one_a, one_b, two_a, two_b = after((fix, one_a, one_b, two_a, two_b), dqkv1)
-    do1 = jnp.concatenate([one_a["do"], one_b["do"]], 0).at[:16].add(fix["do"])
-    sent_a1, kept_a1 = link.attention_grads(
-        one, dqkv1, do1,
-        [sums1, one_a["small"], one_b["small"], fix["small"]], [one_a["up"], one_b["up"], fix["up"]], False,
-    )
-    sent_a2, kept_a2 = link.attention_grads(
-        two, after(dqkv2, got_m2, sent_a1), jnp.concatenate([two_a["do"], two_b["do"]], 0),
-        [sums2, two_a["small"], two_b["small"]], [two_a["up"], two_b["up"]], True,
-    )
-    sum_m2 = link.reduce_z(kept_m2[0], got_m2).astype(F32)
-    kept_a1 = link.add_received(*after((kept_a1, swap(sent_a1, "core")), sent_a2))
+    received_a1 = swap(sent_a1, "core")
+    sum_m2 = link.reduce_z(kept_m2[0], got_m2)
+    got_a2 = link.reduce_near(link.add_diagonal(*kept_a2[1:3], got_a2))
+    kept_a1 = add_parts(kept_a1, received_a1)
     got_a1 = link.reduce_diagonal(kept_a1[3:])
-    kept_a2 = link.add_received(*after((kept_a2, swap(sent_a2, "core")), kept_a1))
-    got_a2 = link.reduce_diagonal(kept_a2[3:])
-    got_a1 = link.reduce_near(link.add_diagonal(*after(kept_a1[1:3] + [got_a1], kept_a2)))
-    got_a2 = link.reduce_near(link.add_diagonal(*kept_a2[1:3], got_a2))
-    sum_a1 = link.reduce_z(after(kept_a1[0], sum_m2), got_a1)
-    sum_a2 = link.reduce_z(after(kept_a2[0], sum_a1.astype(F32)), got_a2)
+    got_a1 = link.reduce_near(link.add_diagonal(*kept_a1[1:3], got_a1))
+    fix = after(fix, kept_a1)
+    both = join([kept_a1[0], *got_a1], [kept_a2[0], *got_a2], [sum_m2])
+    both = lax.psum_scatter(both, "z", scatter_dimension=0, tiled=False)
+    sum_a1, sum_a2 = both[: both.shape[0] // 2], both[both.shape[0] // 2 :]
 
     n_up = link.n_up
     up_fix, down_fix = link.first_row_terms(fix)
+    sum_m1, sum_m2 = sum_m1.astype(F32), sum_m2.astype(F32)
     outs = [link.attention_outs(sum_a1, False), link.attention_outs(sum_a2, True)]
     pair = lambda i: jnp.stack([outs[0][i], outs[1][i]])
     return (
-        out_first, jnp.concatenate([two_a["y"], two_b["y"]], 0), grad_tokens, grad_skip,
+        out_first, back_two["y"], grad_tokens, grad_skip,
         pair(0), pair(1),
         jnp.stack([(sum_m1[:n_up] + up_fix).T, sum_m2[:n_up].T]),
         jnp.stack([sum_m1[n_up:] + down_fix, sum_m2[n_up:]]),
@@ -768,13 +790,13 @@
     def forward(x, weights):
         wt, wt_out, small, up_bias, pieces = weights
         qkv, mix, lse = attention_forward(x, marks, (wt, small))
-        return (qkv, mix, lse), feed(x, mix, wt_out, small, up_bias, pieces, [0])[0]
+        return (qkv, mix, lse), feed("forward", x, mix, wt_out, small, up_bias, pieces, [0])[0]
 
     def backward(x, weights, kept, cot, clear_first):
         wt, wt_out, small, up_bias, pieces = weights
         qkv, mix, lse = kept
-        y, n1, g, du, df, do, dr1, dm, sums, up_sums = feed(x, mix, wt_out, small, up_bias, pieces, [0], cot)
-        dqkv, more, dx, first = attention_backward(qkv, mix, lse, marks, wt, [dm], [dr1], clear_first=clear_first)
+        y, do, dr1, dm, sums, up_sums, n1, g, du, df = feed("rows", x, mix, wt_out, small, up_bias, pieces, [0], cot)
+        dqkv, more, dx, first = attention_backward(qkv, mix, lse, marks, dm, [], [wt, dr1], clear_first)
         rows = 2 * up_bias.shape[1]
         lists = [[n1], [df], [g], [du]]
         parts = jnp.concatenate([feed_grads(i, [(4, 1, rows)], None, *lists)[0][:, 0] for i in (0, 4)], 0)

time: 457 us -> 430 us (0.941)
  other arithmetic: 37.7 us -> 14 us
  waiting for transfers between devices: 117 us -> 136 us
  local copies, waits for them, and re-layouts: 28.4 us -> 17.5 us
  Pallas kernels: 192 us -> 186 us
    reduce_scatter x3 -> x1, waiting for transfers between devices: 21.1 us -> 0.02 us  [reduce_z(): lax.psum_scatter(here + got[0] + got[1], 'z', scatter_dimension=0, tiled=...]
    ppermute x36, waiting for transfers between devices: 87.1 us -> 106 us  [swap(): return lax.ppermute(array, axis, [(0, 1), (1, 0)])]
    reduce_scatter x1 -> x2, waiting for transfers between devices: 0.01 us -> 15.2 us  [the longest x1 11.2 us: near_body(): both = lax.psum_scatter(both, 'z', scatter_dimension=0, tiled=False)]
    add x6 -> x0, other arithmetic: 10.7 us -> none  [the longest x2 4.12 us: add_received(): by_x + received[2]]
    pallas_call x13 -> x11, Pallas kernels: 192 us -> 186 us  [call(): pl.pallas_call(kernel, out_shape=out_shapes, in_specs=[SMEM if a.ndim ==...]
    ppermute x36, starting transfers between devices: 31.6 us -> 26.7 us  [swap(): return lax.ppermute(array, axis, [(0, 1), (1, 0)])]
  transfers between devices with their start and end apart: 44 -> 43, of which waited for: 22 -> 20; matrix products, arithmetic and copies ran while one was open for 11% -> 4% of each run, Pallas kernels for 43% -> 43%
where the time goes in v3:
time: 430 us; the launch traced here: 425 us
  Pallas kernels  186 us (43%)
  waiting for transfers between devices  136 us (32%)
  starting transfers between devices  28.5 us (7%)
  blocking collectives  26.4 us (6%)
  local copies, waits for them, and re-layouts  17.5 us (4%)
  between operations  15.6 us (4%)
  other arithmetic  14 us (3%)
    pallas_call x11, Pallas kernels, call(): pl.pallas_call(kernel, out_shape=out_shapes, in_specs=[SMEM if a.ndim ==...  186 us
    ppermute x36, waiting for transfers between devices, swap(): return lax.ppermute(array, axis, [(0, 1), (1, 0)])  106 us
    ppermute x36, starting transfers between devices, swap(): return lax.ppermute(array, axis, [(0, 1), (1, 0)])  26.7 us
    all_gather x1, blocking collectives, along_z(): return lax.all_gather(slab, 'z', axis=0, tiled=False)  26.4 us
    ppermute x2, waiting for transfers between devices, first_row_terms(): flat = jnp.concatenate([flat, lax.ppermute(flat, 'z', pairs)], 0)  12.8 us
    reduce_scatter x1, waiting for transfers between devices, near_body(): both = lax.psum_scatter(both, 'z', scatter_dimension=0, tiled=False)  11.2 us
  transfers between devices with their start and end apart: 43, of which 20 were waited for; matrix products, arithmetic and copies ran while one was open for 4% of the time, Pallas kernels for 43%

profile of v3, /device:TPU:0, one launch (start us, length us, event | category | flops | bytes accessed | tf_op | source)
XLA Modules:
  0.0 424.7 jit_solution(3271574004572230791)
XLA Ops:
  7.3 1.0 slice_bitcast_fusion.4
  8.3 1.0 slice_bitcast_fusion.5
  11.2 26.4 %all-gather = bf16[448,768]{1,0:T(8,128)(2,1)S(1)} all-gather(bf16[112,768]{1,0:T(8,128)(2,1)S(1)} %pad_maximum_fusion.4), channel_id=2, replica_groups=mesh['z'=4,'y'=2,'x'=2,'core'=2] {'z'}, dimensions={0}, use_global_device_ids=true | all-gather | bytes 860160 | tf_op jit(solution)/shard_map/all_gather | solution.py:620
  37.7 1.7 collective-permute-start
  39.4 1.5 collective-permute-start.1
  40.9 10.6 %collective-permute-done.refs_5_ = bf16[4,112,768]{2,1,0:T(8,128)(2,1)S(1)} collective-permute-done((bf16[4,112,768]{2,1,0:T(8,128)(2,1)S(1)}, bf16[4,112,768]{2,1,0:T(8,128)(2,1)S(1)}, u32[]{:S(2)}, u32[]{:S(2)}) %collective-permute-start) | collective-permute-done | bytes 688160 | tf_op jit(solution)/shard_map/ppermute | solution.py:579
  51.5 1.2 collective-permute-start.2
  52.8 2.6 collective-permute-done.1.refs_6_
  55.3 1.0 slice.403
  57.4 2.2 collective-permute-done.2.refs_7_
  59.6 4.2 collective-permute-done.3.refs_8_
  65.1 2.2 collective-permute-start.10
  67.4 0.9 copy.50.refs_2_
  68.3 15.4 %shard_map.212 = (bf16[512,2304]{1,0:T(8,128)(2,1)}, bf16[512,768]{1,0:T(8,128)(2,1)}, f32[12,1,512]{2,1,0:T(1,128)}, bf16[2304,768]{1,0:T(8,128)(2,1)}, bf16[76...) custom-call(bf16[512,768]{1,0:T(8,128)(2,1)} %refs_16_, s32[1,512]{1,0:T(1,128)} %refs_4_.3, ...), custom_call_target="tpu_custom_call" | custom-call | flops 17250000896 | tf_op jit(solution)/shard_map/pallas_call | solution.py:39
  83.6 22.6 %collective-permute-done.10.refs_9_.refs_8_ = bf16[4,192,768]{2,1,0:T(8,128)(2,1)S(1)} collective-permute-done((bf16[4,192,768]{2,1,0:T(8,128)(2,1)}, bf16[4,192,768]{2,1,0:T(8,128)(2,1)S(1)}, u32[]{:S(2)}, u32[]{:S(2)}) %collective-permute-start.10) | collective-permute-done | bytes 1179680 | tf_op jit(solution)/shard_map/ppermute | solution.py:579
  106.2 1.6 slice.344
  107.8 2.4 collective-permute-start.11
  111.0 11.8 %collective-permute-done.11.refs_10_.refs_9_ = bf16[2,192,768]{2,1,0:T(8,128)(2,1)S(1)} collective-permute-done((bf16[2,192,768]{2,1,0:T(8,128)(2,1)S(1)}, bf16[2,192,768]{2,1,0:T(8,128)(2,1)S(1)}, u32[]{:S(2)}, u32[]{:S(2)}) %collective-permute-start.11) | collective-permute-done | bytes 589856 | tf_op jit(solution)/shard_map/ppermute | solution.py:579
  122.8 1.7 collective-permute-done.12.refs_11_.refs_10_
  124.5 0.9 copy.52.refs_2_.refs_5_
  125.8 1.9 collective-permute-done.17.refs_16_.refs_15_
  127.7 39.3 %shard_map.213 = (bf16[512,768]{1,0:T(8,128)(2,1)}, bf16[512,768]{1,0:T(8,128)(2,1)}, f32[512,768]{1,0:T(8,128)}, bf16[512,768]{1,0:T(8,128)(2,1)}, f32[8,768]{1...) custom-call(s32[3]{0:T(128)} %pad_add_fusion.refs_3_.refs_0_, bf16[512,768]{1,0:T(8,128)(2,1)} %refs_16_, ...), custom_call_target="tpu_custom_call" | custom-call | flops 46000001024 | tf_op jit(solution)/shard_map/pallas_call | solution.py:39
  167.1 1.0 copy-done.3
  168.4 1.0 broadcast_select_fusion.refs_0_.refs_1_.refs_11_
  169.4 1.8 all-gather.8.cloned.1.call-done
  171.2 15.0 %shard_map.214 = (bf16[512,2304]{1,0:T(8,128)(2,1)}, bf16[512,768]{1,0:T(8,128)(2,1)}, f32[12,1,512]{2,1,0:T(1,128)}, bf16[2304,768]{1,0:T(8,128)(2,1)}, bf16[76...) custom-call(bf16[512,768]{1,0:T(8,128)(2,1)} %broadcast_select_fusion.refs_0_.refs_1_.refs_11_, ...), custom_call_target="tpu_custom_call" | custom-call | flops 17250000896 | tf_op jit(solution)/shard_map/pallas_call | solution.py:39
  186.2 39.8 %shard_map.215 = (bf16[512,768]{1,0:T(8,128)(2,1)}, bf16[512,768]{1,0:T(8,128)(2,1)}, f32[512,768]{1,0:T(8,128)}, bf16[512,768]{1,0:T(8,128)(2,1)}, f32[8,768]{1...) custom-call(s32[3]{0:T(128)} %pad_add_fusion.refs_3_.refs_0_, ...), custom_call_target="tpu_custom_call" | custom-call | flops 46000001024 | tf_op jit(solution)/shard_map/pallas_call | solution.py:39
  226.3 23.3 %shard_map.216 = (f32[512,768]{1,0:T(8,128)}, f32[16,768]{1,0:T(8,128)}, bf16[4,4,112,768]{3,2,1,0:T(8,128)(2,1)}, bf16[4,4,112,768]{3,2,1,0:T(8,128)(2,1)}) custom-call(s32[3]{0:T(128)} %pad_add_fusion.refs_3_.refs_0_, bf16[512,2304]{1,0:T(8,128)(2,1)} %get-tuple-element.237.refs_1_, bf16[512,768]{1,0:T(8,128)(2,1)} %get-tuple-element.224.refs_2_, ...), custom_call_target="tpu_custom_call" | custom-call | flops 25300000768 | tf_op jit(solution)/shard_map/pallas_call | solution.py:39
  249.9 1.8 add_select_fusion.refs_5_
  251.8 6.3 %shard_map.217 = (bf16[4,192,768]{2,1,0:T(8,128)(2,1)}, bf16[4,192,768]{2,1,0:T(8,128)(2,1)}, bf16[4,192,768]{2,1,0:T(8,128)(2,1)}, bf16[2,192,768]{2,1,0:T(8,128)(2,1)}, bf16[2,192,768]{2,1,0:T(8,128)(2,1)}) custom-call(bf16[4,4,192,768]{3,2,1,0:T(8,128)(2,1)} %get-tuple-element.250.refs_0_, bf16[4,4,192,768]{3,2,1,0:T(8,128)(2,1)} %copy-done.27), custom_call_target="tpu_custom_call" | custom-call | flops 4600000000 | tf_op jit(solution)/shard_map/pallas_call | solution.py:39
  258.0 1.2 collective-permute-start.20
  259.5 1.5 copy-done.28
  261.0 4.3 %shard_map.218 = (bf16[4,112,768]{2,1,0:T(8,128)(2,1)}, bf16[4,112,768]{2,1,0:T(8,128)(2,1)}, bf16[4,112,768]{2,1,0:T(8,128)(2,1)}, bf16[2,112,768]{2,1,0:T(8,128)(2,1)}, bf16[2,112,768]{2,1,0:T(8,128)(2,1)}) custom-call(bf16[4,4,112,768]{3,2,1,0:T(8,128)(2,1)} %get-tuple-element.257.refs_0_, bf16[4,4,112,768]{3,2,1,0:T(8,128)(2,1)} %copy-done.28), custom_call_target="tpu_custom_call" | custom-call | flops 4600000000 | tf_op jit(solution)/shard_map/pallas_call | solution.py:39
  265.2 2.1 collective-permute-start.22
  267.9 13.0 %shard_map.219 = (bf16[16,768]{1,0:T(8,128)(2,1)}, bf16[16,768]{1,0:T(8,128)(2,1)}, f32[16,768]{1,0:T(8,128)}, bf16[16,768]{1,0:T(8,128)(2,1)}, f32[8,768]{1,0:T...) custom-call(bf16[512,768]{1,0:T(8,128)(2,1)} %refs_16_, ...), custom_call_target="tpu_custom_call" | custom-call | flops 13799999488 | tf_op jit(solution)/shard_map/pallas_call | solution.py:39
  281.0 4.4 %collective-permute-done.22 = bf16[2,112,768]{2,1,0:T(8,128)(2,1)S(1)} collective-permute-done((bf16[2,112,768]{2,1,0:T(8,128)(2,1)}, bf16[2,112,768]{2,1,0:T(8,128)(2,1)S(1)}, u32[]{:S(2)}, u32[]{:S(2)}) %collective-permute-start.22) | collective-permute-done | bytes 344096 | tf_op jit(solution)/shard_map/ppermute | solution.py:579
  285.3 4.3 %collective-permute-done.23 = bf16[2,112,768]{2,1,0:T(8,128)(2,1)S(1)} collective-permute-done((bf16[2,112,768]{2,1,0:T(8,128)(2,1)}, bf16[2,112,768]{2,1,0:T(8,128)(2,1)S(1)}, u32[]{:S(2)}, u32[]{:S(2)}) %collective-permute-start.23) | collective-permute-done | bytes 344096 | tf_op jit(solution)/shard_map/ppermute | solution.py:579
  291.1 2.3 collective-permute-start.24
  293.3 22.3 %shard_map.220 = (f32[512,768]{1,0:T(8,128)}, f32[16,768]{1,0:T(8,128)}, bf16[4,4,112,768]{3,2,1,0:T(8,128)(2,1)}, bf16[4,4,112,768]{3,2,1,0:T(8,128)(2,1)}) custom-call(s32[3]{0:T(128)} %pad_add_fusion.refs_3_.refs_0_, bf16[512,2304]{1,0:T(8,128)(2,1)} %get-tuple-element.229.refs_1_, bf16[512,768]{1,0:T(8,128)(2,1)} %get-tuple-element.215.refs_2_.refs_1_, ...), custom_call_target="tpu_custom_call" | custom-call | flops 25300000768 | tf_op jit(solution)/shard_map/pallas_call | solution.py:39
  315.6 4.0 reduce-scatter.4.cloned.1.call-done
  319.7 2.8 add_add_fusion
  322.6 0.9 copy-done.10
  323.9 1.4 collective-permute-start.32
  325.3 4.4 %shard_map.221 = (bf16[4,112,768]{2,1,0:T(8,128)(2,1)}, bf16[4,112,768]{2,1,0:T(8,128)(2,1)}, bf16[4,112,768]{2,1,0:T(8,128)(2,1)}, bf16[2,112,768]{2,1,0:T(8,128)(2,1)}, bf16[2,112,768]{2,1,0:T(8,128)(2,1)}) custom-call(bf16[4,4,112,768]{3,2,1,0:T(8,128)(2,1)} %get-tuple-element.292.refs_0_, bf16[4,4,112,768]{3,2,1,0:T(8,128)(2,1)} %collective-permute-done.26.refs_1_), custom_call_target="tpu_custom_call" | custom-call | flops 4600000000 | tf_op jit(solution)/shard_map/pallas_call | solution.py:39
  332.1 0.8 slice_reduce_fusion.1
  333.6 1.1 collective-permute-start.31
  334.7 1.0 collective-permute-start.29
  335.7 1.0 collective-permute-start.27
  336.9 1.1 collective-permute-start.34
  338.0 20.8 %collective-permute-done.29 = bf16[2,112,768]{2,1,0:T(8,128)(2,1)S(1)} collective-permute-done((bf16[2,112,768]{2,1,0:T(8,128)(2,1)}, bf16[2,112,768]{2,1,0:T(8,128)(2,1)S(1)}, u32[]{:S(2)}, u32[]{:S(2)}) %collective-permute-start.29) | collective-permute-done | bytes 344096 | tf_op jit(solution)/shard_map/ppermute | solution.py:579
  358.9 1.1 collective-permute-start.30
  360.1 1.0 collective-permute-start.28
  361.2 14.8 %collective-permute-done.30.refs_2_ = bf16[4,112,768]{2,1,0:T(8,128)(2,1)} collective-permute-done((bf16[4,112,768]{2,1,0:T(8,128)(2,1)S(1)}, bf16[4,112,768]{2,1,0:T(8,128)(2,1)}, u32[]{:S(2)}, u32[]{:S(2)}) %collective-permute-start.30) | collective-permute-done | bytes 688160 | tf_op jit(solution)/shard_map/ppermute | solution.py:579
  376.8 0.9 copy-done.31
  377.6 3.4 shard_map.222
  381.1 0.9 collective-permute-start.35
  382.1 2.9 collective-permute-done.35
  385.6 3.9 collective-permute-done.36
  389.6 1.1 collective-permute-start.37
  390.7 8.9 %collective-permute-done.37 = bf16[16,2304]{1,0:T(8,128)(2,1)S(1)} collective-permute-done((bf16[16,2304]{1,0:T(8,128)(2,1)S(1)}, bf16[16,2304]{1,0:T(8,128)(2,1)S(1)}, u32[]{:S(2)}, u32[]{:S(2)}) %collective-permute-start.37) | collective-permute-done | bytes 73760 | tf_op jit(solution)/shard_map/ppermute | solution.py:692
  400.3 0.9 pad_maximum_fusion.1
  401.2 0.9 pad_maximum_fusion
  402.0 11.2 %reduce-scatter.8.cloned.1.call-done = bf16[1,224,768]{2,1,0:T(8,128)(2,1)} async-done(((bf16[4,224,768]{2,1,0:T(8,128)(2,1)}), bf16[1,224,768]{2,1,0:T(8,128)(2,1)}) %reduce-scatter.8.cloned.1.call-update) | async-done | bytes 344080 | tf_op jit(solution)/shard_map/reduce_scatter | solution.py:753
  413.3 1.0 slice_convert_fusion.1
  (215 shorter events, 17.7 us)
Async XLA Ops:
  7.2 3.0 copy-start.26
  7.2 3.0 copy-start.25
  7.2 3.0 copy-start.16
  7.2 3.8 copy-start.22
  7.2 57.9 %all-gather.6.cloned.1.call-start = ((), (), s32[]{:S(2)}) async-start(), calls=%async_computation.6 | async-start | bytes 1474560 | tf_op jit(solution)/shard_map/all_gather | solution.py:620
  10.1 161.2 %all-gather.8.cloned.1.call-start = ((), (), s32[]{:S(2)}) async-start(), calls=%async_computation.7 | async-start | bytes 15409152 | tf_op jit(solution)/shard_map/all_gather | solution.py:711
  11.2 26.5 %copy-start.5 = (bf16[304,768]{1,0:T(8,128)(2,1)}, bf16[304,768]{1,0:T(8,128)(2,1)S(1)}, u32[]{:S(2)}) copy-start(bf16[304,768]{1,0:T(8,128)(2,1)S(1)} %bitcast_dynamic-update-slice_fusion.1) | copy-start | bytes 1400836
  11.2 53.9 %copy-start.24 = (s32[1,512]{1,0:T(1,128)S(1)}, s32[1,512]{1,0:T(1,128)}, u32[]{:S(2)}) copy-start(s32[1,512]{1,0:T(1,128)} %refs_4_.3) | copy-start | bytes 6148
  37.6 30.6 %copy-start.6 = (bf16[448,768]{1,0:T(8,128)(2,1)}, bf16[448,768]{1,0:T(8,128)(2,1)S(1)}, u32[]{:S(2)}) copy-start(bf16[448,768]{1,0:T(8,128)(2,1)S(1)} %all-gather) | copy-start | bytes 2064388
  37.7 282.0 %reduce-scatter.4.cloned.1.call-start = ((), (), s32[]{:S(2)}) async-start(), calls=%async_computation.3 | async-start | bytes 9732096 | tf_op jit(solution)/shard_map/reduce_scatter | solution.py:721
  37.7 13.8 %collective-permute-start = (bf16[4,112,768]{2,1,0:T(8,128)(2,1)S(1)}, bf16[4,112,768]{2,1,0:T(8,128)(2,1)S(1)}, u32[]{:S(2)}, u32[]{:S(2)}) collective-permute-start(bf16[4,112,768]{2,1,0:T(8,128)(2,1)S(1)} %bitcast.122), channel_id=1, source_target_pairs={{0,4},{4,0},{1,5},{5,1},{2,6},{6,2},{3,7},{7,3},{8,12},{12,8},{9,1... | collective-permute-start | bytes 2064392 | tf_op jit(solution)/shard_map/ppermute | solution.py:579
  39.4 15.9 %collective-permute-start.1 = (bf16[4,112,768]{2,1,0:T(8,128)(2,1)S(1)}, bf16[4,112,768]{2,1,0:T(8,128)(2,1)}, u32[]{:S(2)}, u32[]{:S(2)}) collective-permute-start(bf16[4,112,768]{2,1,0:T(8,128)(2,1)S(1)} %bitcast.123), channel_id=1, source_target_pairs={{0,2},{2,0},{1,3},{3,1},{4,6},{6,4},{5,7},{7,5},{8,10},{10,8},{9,1... | collective-permute-start | bytes 2064392 | tf_op jit(solution)/shard_map/ppermute | solution.py:579
  40.9 24.2 %collective-permute-start.4 = (bf16[4,112,768]{2,1,0:T(8,128)(2,1)S(1)}, bf16[4,112,768]{2,1,0:T(8,128)(2,1)S(1)}, u32[]{:S(2)}, u32[]{:S(2)}) collective-permute-start(bf16[4,112,768]{2,1,0:T(8,128)(2,1)S(1)} %bitcast.124), channel_id=1, source_target_pairs={{0,1},{1,0},{2,3},{3,2},{4,5},{5,4},{6,7},{7,6},{8,9},{9,8},{10,11... | collective-permute-start | bytes 2064392 | tf_op jit(solution)/shard_map/ppermute | solution.py:579
  51.5 16.8 %copy-start.19 = (bf16[4,112,768]{2,1,0:T(8,128)(2,1)}, bf16[4,112,768]{2,1,0:T(8,128)(2,1)S(1)}, u32[]{:S(2)}) copy-start(bf16[4,112,768]{2,1,0:T(8,128)(2,1)S(1)} %collective-permute-done.refs_5_) | copy-start | bytes 2064388
  51.5 8.0 %collective-permute-start.2 = (bf16[2,112,768]{2,1,0:T(8,128)(2,1)S(1)}, bf16[2,112,768]{2,1,0:T(8,128)(2,1)}, u32[]{:S(2)}, u32[]{:S(2)}) collective-permute-start(bf16[2,112,768]{2,1,0:T(8,128)(2,1)S(1)} %slice.402), channel_id=1, source_target_pairs={{0,2},{2,0},{1,3},{3,1},{4,6},{6,4},{5,7},{7,5},{8,10},{10,8},{9,1... | collective-permute-start | bytes 1032200 | tf_op jit(solution)/shard_map/ppermute | solution.py:579
  56.3 7.4 %collective-permute-start.3 = (bf16[2,112,768]{2,1,0:T(8,128)(2,1)S(1)}, bf16[2,112,768]{2,1,0:T(8,128)(2,1)}, u32[]{:S(2)}, u32[]{:S(2)}) collective-permute-start(bf16[2,112,768]{2,1,0:T(8,128)(2,1)S(1)} %slice.403), channel_id=1, source_target_pairs={{0,4},{4,0},{1,5},{5,1},{2,6},{6,2},{3,7},{7,3},{8,12},{12,8},{9,1... | collective-permute-start | bytes 1032200 | tf_op jit(solution)/shard_map/ppermute | solution.py:579
  56.9 10.5 %collective-permute-start.5 = (bf16[4,112,768]{2,1,0:T(8,128)(2,1)S(1)}, bf16[4,112,768]{2,1,0:T(8,128)(2,1)}, u32[]{:S(2)}, u32[]{:S(2)}) collective-permute-start(bf16[4,112,768]{2,1,0:T(8,128)(2,1)S(1)} %collective-permute-done.refs_5_), channel_id=1, source_target_pairs={{0,1},{1,0},{2,3},{3,2},{4,5},{5,4},{6,7},{7,6},{8,9},{9,8},{10,11... | collective-permute-start | bytes 2064392 | tf_op jit(solution)/shard_map/ppermute | solution.py:579
  56.9 10.5 %collective-permute-start.6 = (bf16[4,112,768]{2,1,0:T(8,128)(2,1)}, bf16[4,112,768]{2,1,0:T(8,128)(2,1)}, u32[]{:S(2)}, u32[]{:S(2)}) collective-permute-start(bf16[4,112,768]{2,1,0:T(8,128)(2,1)} %collective-permute-done.1.refs_6_), channel_id=1, source_target_pairs={{0,1},{1,0},{2,3},{3,2},{4,5},{5,4},{6,7},{7,6},{8,9},{9,8},{10,11... | collective-permute-start | bytes 2064392 | tf_op jit(solution)/shard_map/ppermute | solution.py:579
  59.5 7.8 %collective-permute-start.7 = (bf16[2,112,768]{2,1,0:T(8,128)(2,1)}, bf16[2,112,768]{2,1,0:T(8,128)(2,1)}, u32[]{:S(2)}, u32[]{:S(2)}) collective-permute-start(bf16[2,112,768]{2,1,0:T(8,128)(2,1)} %collective-permute-done.2.refs_7_), channel_id=1, source_target_pairs={{0,1},{1,0},{2,3},{3,2},{4,5},{5,4},{6,7},{7,6},{8,9},{9,8},{10,11... | collective-permute-start | bytes 1032200 | tf_op jit(solution)/shard_map/ppermute | solution.py:579
  63.8 3.6 collective-permute-start.8
  65.1 3.2 copy-start.30
  65.1 41.1 %collective-permute-start.10 = (bf16[4,192,768]{2,1,0:T(8,128)(2,1)}, bf16[4,192,768]{2,1,0:T(8,128)(2,1)S(1)}, u32[]{:S(2)}, u32[]{:S(2)}) collective-permute-start(bf16[4,192,768]{2,1,0:T(8,128)(2,1)} %bitcast.148), channel_id=1, source_target_pairs={{0,2},{2,0},{1,3},{3,1},{4,6},{6,4},{5,7},{7,5},{8,10},{10,8},{9,1... | collective-permute-start | bytes 3538952 | tf_op jit(solution)/shard_map/ppermute | solution.py:579
  67.4 38.9 %collective-permute-start.9 = (bf16[4,192,768]{2,1,0:T(8,128)(2,1)}, bf16[4,192,768]{2,1,0:T(8,128)(2,1)}, u32[]{:S(2)}, u32[]{:S(2)}) collective-permute-start(bf16[4,192,768]{2,1,0:T(8,128)(2,1)} %bitcast.149), channel_id=1, source_target_pairs={{0,4},{4,0},{1,5},{5,1},{2,6},{6,2},{3,7},{7,3},{8,12},{12,8},{9,1... | collective-permute-start | bytes 3538952 | tf_op jit(solution)/shard_map/ppermute | solution.py:579
  106.2 4.7 %copy-start.13 = (bf16[4,192,768]{2,1,0:T(8,128)(2,1)}, bf16[4,192,768]{2,1,0:T(8,128)(2,1)S(1)}, u32[]{:S(2)}) copy-start(bf16[4,192,768]{2,1,0:T(8,128)(2,1)S(1)} %collective-permute-done.10.refs_9_.refs_8_) | copy-start | bytes 3538948
  106.2 4.1 copy-start.29
  107.8 15.0 %collective-permute-start.11 = (bf16[2,192,768]{2,1,0:T(8,128)(2,1)S(1)}, bf16[2,192,768]{2,1,0:T(8,128)(2,1)S(1)}, u32[]{:S(2)}, u32[]{:S(2)}) collective-permute-start(bf16[2,192,768]{2,1,0:T(8,128)(2,1)S(1)} %slice.344), channel_id=1, source_target_pairs={{0,2},{2,0},{1,3},{3,1},{4,6},{6,4},{5,7},{7,5},{8,10},{10,8},{9,1... | collective-permute-start | bytes 1769480 | tf_op jit(solution)/shard_map/ppermute | solution.py:579
  110.3 14.2 %collective-permute-start.12 = (bf16[2,192,768]{2,1,0:T(8,128)(2,1)S(1)}, bf16[2,192,768]{2,1,0:T(8,128)(2,1)}, u32[]{:S(2)}, u32[]{:S(2)}) collective-permute-start(bf16[2,192,768]{2,1,0:T(8,128)(2,1)S(1)} %slice.345), channel_id=1, source_target_pairs={{0,4},{4,0},{1,5},{5,1},{2,6},{6,2},{3,7},{7,3},{8,12},{12,8},{9,1... | collective-permute-start | bytes 1769480 | tf_op jit(solution)/shard_map/ppermute | solution.py:579
  110.4 17.3 %collective-permute-start.13 = (bf16[4,192,768]{2,1,0:T(8,128)(2,1)S(1)}, bf16[4,192,768]{2,1,0:T(8,128)(2,1)}, u32[]{:S(2)}, u32[]{:S(2)}) collective-permute-start(bf16[4,192,768]{2,1,0:T(8,128)(2,1)S(1)} %bitcast.152), channel_id=1, source_target_pairs={{0,1},{1,0},{2,3},{3,2},{4,5},{5,4},{6,7},{7,6},{8,9},{9,8},{10,11... | collective-permute-start | bytes 3538952 | tf_op jit(solution)/shard_map/ppermute | solution.py:579
  110.5 17.2 %collective-permute-start.14 = (bf16[4,192,768]{2,1,0:T(8,128)(2,1)}, bf16[4,192,768]{2,1,0:T(8,128)(2,1)}, u32[]{:S(2)}, u32[]{:S(2)}) collective-permute-start(bf16[4,192,768]{2,1,0:T(8,128)(2,1)} %collective-permute-done.9.refs_8_.refs_7_), channel_id=1, source_target_pairs={{0,1},{1,0},{2,3},{3,2},{4,5},{5,4},{6,7},{7,6},{8,9},{9,8},{10,11... | collective-permute-start | bytes 3538952 | tf_op jit(solution)/shard_map/ppermute | solution.py:579
  111.0 16.7 %collective-permute-start.15 = (bf16[4,192,768]{2,1,0:T(8,128)(2,1)S(1)}, bf16[4,192,768]{2,1,0:T(8,128)(2,1)}, u32[]{:S(2)}, u32[]{:S(2)}) collective-permute-start(bf16[4,192,768]{2,1,0:T(8,128)(2,1)S(1)} %collective-permute-done.10.refs_9_.refs_8_), channel_id=1, source_target_pairs={{0,1},{1,0},{2,3},{3,2},{4,5},{5,4},{6,7},{7,6},{8,9},{9,8},{10,11... | collective-permute-start | bytes 3538952 | tf_op jit(solution)/shard_map/ppermute | solution.py:579
  122.8 4.9 %copy-start.32 = (bf16[2,192,768]{2,1,0:T(8,128)(2,1)}, bf16[2,192,768]{2,1,0:T(8,128)(2,1)S(1)}, u32[]{:S(2)}) copy-start(bf16[2,192,768]{2,1,0:T(8,128)(2,1)S(1)} %collective-permute-done.11.refs_10_.refs_9_) | copy-start | bytes 1769476
  122.8 3.0 collective-permute-start.16
  124.5 3.2 collective-permute-start.17
  167.0 194.1 %reduce-scatter.6.cloned.1.call-start = ((), (), s32[]{:S(2)}) async-start(), calls=%async_computation.4 | async-start | bytes 1474560 | tf_op jit(solution)/shard_map/reduce_scatter | solution.py:659
  226.0 23.6 %collective-permute-start.18 = (bf16[4,4,192,768]{3,2,1,0:T(8,128)(2,1)}, bf16[4,4,192,768]{3,2,1,0:T(8,128)(2,1)S(1)}, u32[]{:S(2)}, u32[]{:S(2)}) collective-permute-start(bf16[4,4,192,768]{3,2,1,0:T(8,128)(2,1)} %get-tuple-element.247), channel_id=1, source_target_pairs={{0,1},{1,0},{2,3},{3,2},{4,5},{5,4},{6,7},{7,6},{8,9},{9,8},{10,11... | collective-permute-start | bytes 14155784 | tf_op jit(solution)/shard_map/ppermute | solution.py:579
  249.6 9.9 %collective-permute-start.19 = (bf16[4,4,112,768]{3,2,1,0:T(8,128)(2,1)}, bf16[4,4,112,768]{3,2,1,0:T(8,128)(2,1)S(1)}, u32[]{:S(2)}, u32[]{:S(2)}) collective-permute-start(bf16[4,4,112,768]{3,2,1,0:T(8,128)(2,1)} %get-tuple-element.258), channel_id=1, source_target_pairs={{0,1},{1,0},{2,3},{3,2},{4,5},{5,4},{6,7},{7,6},{8,9},{9,8},{10,11... | collective-permute-start | bytes 8257544 | tf_op jit(solution)/shard_map/ppermute | solution.py:579
  258.0 22.9 %collective-permute-start.20 = (bf16[2,192,768]{2,1,0:T(8,128)(2,1)}, bf16[2,192,768]{2,1,0:T(8,128)(2,1)S(1)}, u32[]{:S(2)}, u32[]{:S(2)}) collective-permute-start(bf16[2,192,768]{2,1,0:T(8,128)(2,1)} %get-tuple-element.255), channel_id=1, source_target_pairs={{0,2},{2,0},{1,3},{3,1},{4,6},{6,4},{5,7},{7,5},{8,10},{10,8},{9,1... | collective-permute-start | bytes 1769480 | tf_op jit(solution)/shard_map/ppermute | solution.py:579
  259.3 21.7 %collective-permute-start.21 = (bf16[2,192,768]{2,1,0:T(8,128)(2,1)}, bf16[2,192,768]{2,1,0:T(8,128)(2,1)S(1)}, u32[]{:S(2)}, u32[]{:S(2)}) collective-permute-start(bf16[2,192,768]{2,1,0:T(8,128)(2,1)} %get-tuple-element.256), channel_id=1, source_target_pairs={{0,4},{4,0},{1,5},{5,1},{2,6},{6,2},{3,7},{7,3},{8,12},{12,8},{9,1... | collective-permute-start | bytes 1769480 | tf_op jit(solution)/shard_map/ppermute | solution.py:579
  265.2 20.1 %collective-permute-start.22 = (bf16[2,112,768]{2,1,0:T(8,128)(2,1)}, bf16[2,112,768]{2,1,0:T(8,128)(2,1)S(1)}, u32[]{:S(2)}, u32[]{:S(2)}) collective-permute-start(bf16[2,112,768]{2,1,0:T(8,128)(2,1)} %get-tuple-element.262), channel_id=1, source_target_pairs={{0,2},{2,0},{1,3},{3,1},{4,6},{6,4},{5,7},{7,5},{8,10},{10,8},{9,1... | collective-permute-start | bytes 1032200 | tf_op jit(solution)/shard_map/ppermute | solution.py:579
  267.3 22.4 %collective-permute-start.23 = (bf16[2,112,768]{2,1,0:T(8,128)(2,1)}, bf16[2,112,768]{2,1,0:T(8,128)(2,1)S(1)}, u32[]{:S(2)}, u32[]{:S(2)}) collective-permute-start(bf16[2,112,768]{2,1,0:T(8,128)(2,1)} %get-tuple-element.263), channel_id=1, source_target_pairs={{0,4},{4,0},{1,5},{5,1},{2,6},{6,2},{3,7},{7,3},{8,12},{12,8},{9,1... | collective-permute-start | bytes 1032200 | tf_op jit(solution)/shard_map/ppermute | solution.py:579
  267.9 21.7 %copy-start.1 = (bf16[4,192,768]{2,1,0:T(8,128)(2,1)S(1)}, bf16[4,192,768]{2,1,0:T(8,128)(2,1)}, u32[]{:S(2)}) copy-start(bf16[4,192,768]{2,1,0:T(8,128)(2,1)} %get-tuple-element.277) | copy-start | bytes 3538948
  280.9 8.8 %copy-start = (bf16[4,192,768]{2,1,0:T(8,128)(2,1)S(1)}, bf16[4,192,768]{2,1,0:T(8,128)(2,1)}, u32[]{:S(2)}) copy-start(bf16[4,192,768]{2,1,0:T(8,128)(2,1)} %get-tuple-element.275) | copy-start | bytes 3538948
  285.3 4.5 %copy-start.7 = (bf16[2,112,768]{2,1,0:T(8,128)(2,1)}, bf16[2,112,768]{2,1,0:T(8,128)(2,1)S(1)}, u32[]{:S(2)}) copy-start(bf16[2,112,768]{2,1,0:T(8,128)(2,1)S(1)} %collective-permute-done.22) | copy-start | bytes 1032196
  290.7 29.0 %collective-permute-start.25 = (bf16[4,192,768]{2,1,0:T(8,128)(2,1)S(1)}, bf16[4,192,768]{2,1,0:T(8,128)(2,1)}, u32[]{:S(2)}, u32[]{:S(2)}) collective-permute-start(bf16[4,192,768]{2,1,0:T(8,128)(2,1)S(1)} %add_dynamic-update-slice_fusion), channel_id=1, source_target_pairs={{0,2},{2,0},{1,3},{3,1},{4,6},{6,4},{5,7},{7,5},{8,10},{10,8},{9,1... | collective-permute-start | bytes 3538952 | tf_op jit(solution)/shard_map/ppermute | solution.py:579
  291.1 28.6 %collective-permute-start.24 = (bf16[4,192,768]{2,1,0:T(8,128)(2,1)S(1)}, bf16[4,192,768]{2,1,0:T(8,128)(2,1)}, u32[]{:S(2)}, u32[]{:S(2)}) collective-permute-start(bf16[4,192,768]{2,1,0:T(8,128)(2,1)S(1)} %add_dynamic-update-slice_fusion.1), channel_id=1, source_target_pairs={{0,4},{4,0},{1,5},{5,1},{2,6},{6,2},{3,7},{7,3},{8,12},{12,8},{9,1... | collective-permute-start | bytes 3538952 | tf_op jit(solution)/shard_map/ppermute | solution.py:579
  293.3 26.3 %copy-start.2 = (bf16[4,192,768]{2,1,0:T(8,128)(2,1)S(1)}, bf16[4,192,768]{2,1,0:T(8,128)(2,1)}, u32[]{:S(2)}) copy-start(bf16[4,192,768]{2,1,0:T(8,128)(2,1)} %get-tuple-element.311) | copy-start | bytes 3538948
  319.7 5.6 %collective-permute-start.26 = (bf16[4,4,112,768]{3,2,1,0:T(8,128)(2,1)}, bf16[4,4,112,768]{3,2,1,0:T(8,128)(2,1)}, u32[]{:S(2)}, u32[]{:S(2)}) collective-permute-start(bf16[4,4,112,768]{3,2,1,0:T(8,128)(2,1)} %get-tuple-element.300), channel_id=1, source_target_pairs={{0,1},{1,0},{2,3},{3,2},{4,5},{5,4},{6,7},{7,6},{8,9},{9,8},{10,11... | collective-permute-start | bytes 8257544 | tf_op jit(solution)/shard_map/ppermute | solution.py:579
  322.5 90.7 %reduce-scatter.8.cloned.1.call-start = ((), (), s32[]{:S(2)}) async-start(), calls=%async_computation.5 | async-start | bytes 1720320 | tf_op jit(solution)/shard_map/reduce_scatter | solution.py:753
  323.8 9.7 %copy-start.8 = (bf16[2,112,768]{2,1,0:T(8,128)(2,1)S(1)}, bf16[2,112,768]{2,1,0:T(8,128)(2,1)}, u32[]{:S(2)}) copy-start(bf16[2,112,768]{2,1,0:T(8,128)(2,1)} %copy-done.7) | copy-start | bytes 1032196
  323.8 9.7 %copy-start.17 = (bf16[4,112,768]{2,1,0:T(8,128)(2,1)S(1)}, bf16[4,112,768]{2,1,0:T(8,128)(2,1)}, u32[]{:S(2)}) copy-start(bf16[4,112,768]{2,1,0:T(8,128)(2,1)} %get-tuple-element.307) | copy-start | bytes 2064388
  323.9 37.3 %collective-permute-start.32 = (bf16[4,112,768]{2,1,0:T(8,128)(2,1)S(1)}, bf16[4,112,768]{2,1,0:T(8,128)(2,1)}, u32[]{:S(2)}, u32[]{:S(2)}) collective-permute-start(bf16[4,112,768]{2,1,0:T(8,128)(2,1)S(1)} %add_dynamic-update-slice_fusion.2), channel_id=1, source_target_pairs={{0,2},{2,0},{1,3},{3,1},{4,6},{6,4},{5,7},{7,5},{8,10},{10,8},{9,1... | collective-permute-start | bytes 2064392 | tf_op jit(solution)/shard_map/ppermute | solution.py:579
  329.7 29.1 %copy-start.21 = (bf16[4,112,768]{2,1,0:T(8,128)(2,1)S(1)}, bf16[4,112,768]{2,1,0:T(8,128)(2,1)}, u32[]{:S(2)}) copy-start(bf16[4,112,768]{2,1,0:T(8,128)(2,1)} %get-tuple-element.304) | copy-start | bytes 2064388
  333.0 27.0 %copy-start.20 = (bf16[4,112,768]{2,1,0:T(8,128)(2,1)S(1)}, bf16[4,112,768]{2,1,0:T(8,128)(2,1)}, u32[]{:S(2)}) copy-start(bf16[4,112,768]{2,1,0:T(8,128)(2,1)} %get-tuple-element.302) | copy-start | bytes 2064388
  333.3 3.4 collective-permute-start.33
  333.6 27.5 %collective-permute-start.31 = (bf16[4,112,768]{2,1,0:T(8,128)(2,1)S(1)}, bf16[4,112,768]{2,1,0:T(8,128)(2,1)}, u32[]{:S(2)}, u32[]{:S(2)}) collective-permute-start(bf16[4,112,768]{2,1,0:T(8,128)(2,1)S(1)} %add_dynamic-update-slice_fusion.3), channel_id=1, source_target_pairs={{0,4},{4,0},{1,5},{5,1},{2,6},{6,2},{3,7},{7,3},{8,12},{12,8},{9,1... | collective-permute-start | bytes 2064392 | tf_op jit(solution)/shard_map/ppermute | solution.py:579
  334.7 24.0 %collective-permute-start.29 = (bf16[2,112,768]{2,1,0:T(8,128)(2,1)}, bf16[2,112,768]{2,1,0:T(8,128)(2,1)S(1)}, u32[]{:S(2)}, u32[]{:S(2)}) collective-permute-start(bf16[2,112,768]{2,1,0:T(8,128)(2,1)} %get-tuple-element.305), channel_id=1, source_target_pairs={{0,4},{4,0},{1,5},{5,1},{2,6},{6,2},{3,7},{7,3},{8,12},{12,8},{9,1... | collective-permute-start | bytes 1032200 | tf_op jit(solution)/shard_map/ppermute | solution.py:579
  335.7 24.2 %collective-permute-start.27 = (bf16[2,112,768]{2,1,0:T(8,128)(2,1)}, bf16[2,112,768]{2,1,0:T(8,128)(2,1)S(1)}, u32[]{:S(2)}, u32[]{:S(2)}) collective-permute-start(bf16[2,112,768]{2,1,0:T(8,128)(2,1)} %get-tuple-element.303), channel_id=1, source_target_pairs={{0,2},{2,0},{1,3},{3,1},{4,6},{6,4},{5,7},{7,5},{8,10},{10,8},{9,1... | collective-permute-start | bytes 1032200 | tf_op jit(solution)/shard_map/ppermute | solution.py:579
  336.9 24.2 %collective-permute-start.34 = (bf16[2,3072]{1,0:T(2,128)(2,1)S(1)}, bf16[2,3072]{1,0:T(2,128)(2,1)S(1)}, u32[]{:S(2)}, u32[]{:S(2)}) collective-permute-start(bf16[2,3072]{1,0:T(2,128)(2,1)S(1)} %pad_maximum_fusion.14), channel_id=1, source_target_pairs={{0,2},{2,0},{1,3},{3,1},{4,6},{6,4},{5,7},{7,5},{8,10},{10,8},{9,1... | collective-permute-start | bytes 36872 | tf_op jit(solution)/shard_map/ppermute | solution.py:579
  358.9 17.1 %collective-permute-start.30 = (bf16[4,112,768]{2,1,0:T(8,128)(2,1)S(1)}, bf16[4,112,768]{2,1,0:T(8,128)(2,1)}, u32[]{:S(2)}, u32[]{:S(2)}) collective-permute-start(bf16[4,112,768]{2,1,0:T(8,128)(2,1)S(1)} %add_dynamic-update-slice_fusion.4), channel_id=1, source_target_pairs={{0,2},{2,0},{1,3},{3,1},{4,6},{6,4},{5,7},{7,5},{8,10},{10,8},{9,1... | collective-permute-start | bytes 2064392 | tf_op jit(solution)/shard_map/ppermute | solution.py:579
  360.1 16.7 %collective-permute-start.28 = (bf16[4,112,768]{2,1,0:T(8,128)(2,1)S(1)}, bf16[4,112,768]{2,1,0:T(8,128)(2,1)S(1)}, u32[]{:S(2)}, u32[]{:S(2)}) collective-permute-start(bf16[4,112,768]{2,1,0:T(8,128)(2,1)S(1)} %add_dynamic-update-slice_fusion.5), channel_id=1, source_target_pairs={{0,4},{4,0},{1,5},{5,1},{2,6},{6,2},{3,7},{7,3},{8,12},{12,8},{9,1... | collective-permute-start | bytes 2064392 | tf_op jit(solution)/shard_map/ppermute | solution.py:579
  381.1 4.6 %copy-start.12 = (bf16[1,192,768]{2,1,0:T(8,128)(2,1)S(1)}, bf16[1,192,768]{2,1,0:T(8,128)(2,1)}, u32[]{:S(2)}) copy-start(bf16[1,192,768]{2,1,0:T(8,128)(2,1)} %reduce-scatter.6.cloned.1.call-done) | copy-start | bytes 884740
  381.1 3.8 collective-permute-start.35
  385.1 4.5 %collective-permute-start.36 = (bf16[8,2304]{1,0:T(8,128)(2,1)S(1)}, bf16[8,2304]{1,0:T(8,128)(2,1)S(1)}, u32[]{:S(2)}, u32[]{:S(2)}) collective-permute-start(bf16[8,2304]{1,0:T(8,128)(2,1)S(1)} %pad_maximum_fusion.8), channel_id=1, source_target_pairs={{0,8},{8,0},{16,24},{24,16},{1,9},{9,1},{17,25},{25,17},{2,10},{10... | collective-permute-start | bytes 110600 | tf_op jit(solution)/shard_map/ppermute | solution.py:692
  389.6 10.0 %collective-permute-start.37 = (bf16[16,2304]{1,0:T(8,128)(2,1)S(1)}, bf16[16,2304]{1,0:T(8,128)(2,1)S(1)}, u32[]{:S(2)}, u32[]{:S(2)}) collective-permute-start(bf16[16,2304]{1,0:T(8,128)(2,1)S(1)} %pad_maximum_fusion.7), channel_id=1, source_target_pairs={{0,16},{8,24},{16,0},{24,8},{1,17},{9,25},{17,1},{25,9},{2,18},{10... | collective-permute-start | bytes 221192 | tf_op jit(solution)/shard_map/ppermute | solution.py:692
  (12 other events, 18.5 us)
Sparse Core Ops, SparseCore 0:
  10.2 38.6 all-gather.5
  52.4 118.7 all-gather.7
  177.2 142.4 reduce-scatter.3
  322.7 28.0 reduce-scatter.5
  381.2 32.0 reduce-scatter.7

commit v4 on v3

--- a/solution.py
+++ b/solution.py
@@ -713,8 +713,7 @@
     a1 += link.diagonal(a1)
     m1 = link.near(after(m1, a1[:3]))
     a1 += swaps(a1, "core")
-    one = link.attend(*after((tokens, marks, a1), m1[0]))
-    m1 = after(m1, one["mix"])
+    one = link.attend(*after((tokens, marks, a1), m1))
     m1 += link.diagonal(m1)
     m1 += swaps(m1, "core")
     back_one = link.feed("order", one, m1, cot_first, None, True)
@@ -744,8 +743,9 @@
     )
     received_a1 = swap(sent_a1, "core")
     sum_m2 = link.reduce_z(kept_m2[0], got_m2)
-    got_a2 = link.reduce_near(link.add_diagonal(*kept_a2[1:3], got_a2))
-    kept_a1 = add_parts(kept_a1, received_a1)
+    added_a2 = link.add_diagonal(*kept_a2[1:3], got_a2)
+    got_a2 = link.reduce_near(added_a2)
+    kept_a1 = add_parts(*after((kept_a1, received_a1), added_a2))
     got_a1 = link.reduce_diagonal(kept_a1[3:])
     got_a1 = link.reduce_near(link.add_diagonal(*kept_a1[1:3], got_a1))
     fix = after(fix, kept_a1)

time: 430 us -> 436 us (1.014)
  transfers between devices with their start and end apart: 43 -> 43, of which waited for: 20 -> 17; matrix products, arithmetic and copies ran while one was open for 4% -> 5% of each run, Pallas kernels for 43% -> 42%
where the time goes in v4:
time: 436 us; the launch traced here: 430 us
  Pallas kernels  186 us (43%)
  waiting for transfers between devices  136 us (31%)
  starting transfers between devices  31.7 us (7%)
  blocking collectives  26.4 us (6%)
  local copies, waits for them, and re-layouts  19.2 us (4%)
  between operations  15.6 us (4%)
  other arithmetic  15.5 us (4%)
    pallas_call x11, Pallas kernels, call(): pl.pallas_call(kernel, out_shape=out_shapes, in_specs=[SMEM if a.ndim ==...  186 us
    ppermute x36, waiting for transfers between devices, swap(): return lax.ppermute(array, axis, [(0, 1), (1, 0)])  110 us
    ppermute x36, starting transfers between devices, swap(): return lax.ppermute(array, axis, [(0, 1), (1, 0)])  27.9 us
    all_gather x1, blocking collectives, along_z(): return lax.all_gather(slab, 'z', axis=0, tiled=False)  26.4 us
    reduce_scatter x1, waiting for transfers between devices, near_body(): both = lax.psum_scatter(both, 'z', scatter_dimension=0, tiled=False)  13 us
    ppermute x2, waiting for transfers between devices, first_row_terms(): flat = jnp.concatenate([flat, lax.ppermute(flat, 'z', pairs)], 0)  10.9 us
  transfers between devices with their start and end apart: 43, of which 17 were waited for; matrix products, arithmetic and copies ran while one was open for 5% of the time, Pallas kernels for 42%

profile of v4, /device:TPU:0, one launch (start us, length us, event | category | flops | bytes accessed | tf_op | source)
XLA Modules:
  0.0 430.2 jit_solution(14224591003619310965)
XLA Ops:
  7.3 1.0 slice_bitcast_fusion.4
  8.3 1.0 slice_bitcast_fusion.5
  11.2 26.4 %all-gather = bf16[448,768]{1,0:T(8,128)(2,1)S(1)} all-gather(bf16[112,768]{1,0:T(8,128)(2,1)S(1)} %pad_maximum_fusion.4), channel_id=2, replica_groups=mesh['z'=4,'y'=2,'x'=2,'core'=2] {'z'}, dimensions={0}, use_global_device_ids=true | all-gather | bytes 860160 | tf_op jit(solution)/shard_map/all_gather | solution.py:620
  37.6 1.6 collective-permute-start
  39.2 1.5 collective-permute-start.1
  40.7 10.2 %collective-permute-done.refs_5_ = bf16[4,112,768]{2,1,0:T(8,128)(2,1)} collective-permute-done((bf16[4,112,768]{2,1,0:T(8,128)(2,1)S(1)}, bf16[4,112,768]{2,1,0:T(8,128)(2,1)}, u32[]{:S(2)}, u32[]{:S(2)}) %collective-permute-start) | collective-permute-done | bytes 688160 | tf_op jit(solution)/shard_map/ppermute | solution.py:579
  50.9 1.1 collective-permute-done.1.refs_6_
  52.0 1.6 collective-permute-start.10
  53.8 1.0 slice.402
  54.8 0.9 collective-permute-start.2
  55.7 1.0 slice.403
  56.7 1.4 collective-permute-start.3
  58.2 34.8 %collective-permute-done.2.refs_7_ = bf16[2,112,768]{2,1,0:T(8,128)(2,1)S(1)} collective-permute-done((bf16[2,112,768]{2,1,0:T(8,128)(2,1)S(1)}, bf16[2,112,768]{2,1,0:T(8,128)(2,1)S(1)}, u32[]{:S(2)}, u32[]{:S(2)}) %collective-permute-start.2) | collective-permute-done | bytes 344096 | tf_op jit(solution)/shard_map/ppermute | solution.py:579
  93.6 0.8 copy-done.14
  94.5 2.5 collective-permute-start.11
  99.0 0.9 copy.52.refs_2_.refs_5_
  100.6 0.9 copy.50.refs_2_
  101.9 11.9 %collective-permute-done.11.refs_10_.refs_9_ = bf16[2,192,768]{2,1,0:T(8,128)(2,1)} collective-permute-done((bf16[2,192,768]{2,1,0:T(8,128)(2,1)S(1)}, bf16[2,192,768]{2,1,0:T(8,128)(2,1)}, u32[]{:S(2)}, u32[]{:S(2)}) %collective-permute-start.11) | collective-permute-done | bytes 589856 | tf_op jit(solution)/shard_map/ppermute | solution.py:579
  114.4 15.3 %shard_map.212 = (bf16[512,2304]{1,0:T(8,128)(2,1)}, bf16[512,768]{1,0:T(8,128)(2,1)}, f32[12,1,512]{2,1,0:T(1,128)}, bf16[2304,768]{1,0:T(8,128)(2,1)}, bf16[76...) custom-call(bf16[512,768]{1,0:T(8,128)(2,1)} %refs_16_, s32[1,512]{1,0:T(1,128)} %refs_4_.3, ...), custom_call_target="tpu_custom_call" | custom-call | flops 17250000896 | tf_op jit(solution)/shard_map/pallas_call | solution.py:39
  131.5 39.1 %shard_map.213 = (bf16[512,768]{1,0:T(8,128)(2,1)}, bf16[512,768]{1,0:T(8,128)(2,1)}, f32[512,768]{1,0:T(8,128)}, bf16[512,768]{1,0:T(8,128)(2,1)}, f32[8,768]{1...) custom-call(s32[3]{0:T(128)} %pad_add_fusion.refs_3_.refs_0_, bf16[512,768]{1,0:T(8,128)(2,1)} %refs_16_, ...), custom_call_target="tpu_custom_call" | custom-call | flops 46000001024 | tf_op jit(solution)/shard_map/pallas_call | solution.py:39
  170.7 1.0 copy-done.3
  172.0 1.0 broadcast_select_fusion.refs_0_.refs_1_.refs_11_
  173.0 15.0 %shard_map.214 = (bf16[512,2304]{1,0:T(8,128)(2,1)}, bf16[512,768]{1,0:T(8,128)(2,1)}, f32[12,1,512]{2,1,0:T(1,128)}, bf16[2304,768]{1,0:T(8,128)(2,1)}, bf16[76...) custom-call(bf16[512,768]{1,0:T(8,128)(2,1)} %broadcast_select_fusion.refs_0_.refs_1_.refs_11_, ...), custom_call_target="tpu_custom_call" | custom-call | flops 17250000896 | tf_op jit(solution)/shard_map/pallas_call | solution.py:39
  188.0 39.8 %shard_map.215 = (bf16[512,768]{1,0:T(8,128)(2,1)}, bf16[512,768]{1,0:T(8,128)(2,1)}, f32[512,768]{1,0:T(8,128)}, bf16[512,768]{1,0:T(8,128)(2,1)}, f32[8,768]{1...) custom-call(s32[3]{0:T(128)} %pad_add_fusion.refs_3_.refs_0_, ...), custom_call_target="tpu_custom_call" | custom-call | flops 46000001024 | tf_op jit(solution)/shard_map/pallas_call | solution.py:39
  227.8 22.5 %shard_map.216 = (f32[512,768]{1,0:T(8,128)}, f32[16,768]{1,0:T(8,128)}, bf16[4,4,112,768]{3,2,1,0:T(8,128)(2,1)}, bf16[4,4,112,768]{3,2,1,0:T(8,128)(2,1)}) custom-call(s32[3]{0:T(128)} %pad_add_fusion.refs_3_.refs_0_, bf16[512,2304]{1,0:T(8,128)(2,1)} %get-tuple-element.233.refs_1_, bf16[512,768]{1,0:T(8,128)(2,1)} %get-tuple-element.220.refs_2_, ...), custom_call_target="tpu_custom_call" | custom-call | flops 25300000768 | tf_op jit(solution)/shard_map/pallas_call | solution.py:39
  250.9 1.6 add_select_fusion.refs_5_
  252.5 6.3 %shard_map.217 = (bf16[4,192,768]{2,1,0:T(8,128)(2,1)}, bf16[4,192,768]{2,1,0:T(8,128)(2,1)}, bf16[4,192,768]{2,1,0:T(8,128)(2,1)}, bf16[2,192,768]{2,1,0:T(8,128)(2,1)}, bf16[2,192,768]{2,1,0:T(8,128)(2,1)}) custom-call(bf16[4,4,192,768]{3,2,1,0:T(8,128)(2,1)} %get-tuple-element.246.refs_0_, bf16[4,4,192,768]{3,2,1,0:T(8,128)(2,1)} %copy-done.26), custom_call_target="tpu_custom_call" | custom-call | flops 4600000000 | tf_op jit(solution)/shard_map/pallas_call | solution.py:39
  258.8 1.5 collective-permute-start.20
  260.3 1.4 collective-permute-start.21
  261.8 1.5 copy-done.27
  263.3 4.2 shard_map.218
  268.6 13.5 %shard_map.219 = (bf16[16,768]{1,0:T(8,128)(2,1)}, bf16[16,768]{1,0:T(8,128)(2,1)}, f32[16,768]{1,0:T(8,128)}, bf16[16,768]{1,0:T(8,128)(2,1)}, f32[8,768]{1,0:T...) custom-call(bf16[512,768]{1,0:T(8,128)(2,1)} %refs_16_, ...), custom_call_target="tpu_custom_call" | custom-call | flops 13799999488 | tf_op jit(solution)/shard_map/pallas_call | solution.py:39
  282.2 4.1 collective-permute-done.22
  286.2 5.4 %collective-permute-done.23 = bf16[2,112,768]{2,1,0:T(8,128)(2,1)S(1)} collective-permute-done((bf16[2,112,768]{2,1,0:T(8,128)(2,1)}, bf16[2,112,768]{2,1,0:T(8,128)(2,1)S(1)}, u32[]{:S(2)}, u32[]{:S(2)}) %collective-permute-start.23) | collective-permute-done | bytes 344096 | tf_op jit(solution)/shard_map/ppermute | solution.py:579
  293.5 1.4 collective-permute-start.24
  294.9 22.2 %shard_map.220 = (f32[512,768]{1,0:T(8,128)}, f32[16,768]{1,0:T(8,128)}, bf16[4,4,112,768]{3,2,1,0:T(8,128)(2,1)}, bf16[4,4,112,768]{3,2,1,0:T(8,128)(2,1)}) custom-call(s32[3]{0:T(128)} %pad_add_fusion.refs_3_.refs_0_, bf16[512,2304]{1,0:T(8,128)(2,1)} %get-tuple-element.225.refs_1_, bf16[512,768]{1,0:T(8,128)(2,1)} %get-tuple-element.214.refs_2_.refs_1_, ...), custom_call_target="tpu_custom_call" | custom-call | flops 25300000768 | tf_op jit(solution)/shard_map/pallas_call | solution.py:39
  317.2 1.8 reduce-scatter.4.cloned.1.call-done
  319.0 3.1 collective-permute-done.25
  322.6 2.9 add_add_fusion
  325.6 0.9 copy-done.10
  327.0 1.1 collective-permute-done.26.refs_1_
  328.1 4.2 shard_map.221
  332.3 0.8 slice.372
  333.8 0.8 slice_reduce_fusion.2
  334.7 0.8 slice_reduce_fusion.1
  336.1 1.5 collective-permute-start.32
  337.6 1.4 collective-permute-start.31
  340.3 1.6 collective-permute-start.34
  341.9 20.5 %collective-permute-done.29 = bf16[2,112,768]{2,1,0:T(8,128)(2,1)S(1)} collective-permute-done((bf16[2,112,768]{2,1,0:T(8,128)(2,1)}, bf16[2,112,768]{2,1,0:T(8,128)(2,1)S(1)}, u32[]{:S(2)}, u32[]{:S(2)}) %collective-permute-start.29) | collective-permute-done | bytes 344096 | tf_op jit(solution)/shard_map/ppermute | solution.py:579
  362.4 1.8 add_dynamic-update-slice_fusion.2
  364.8 1.4 collective-permute-start.28
  366.4 14.7 %collective-permute-done.30.refs_2_ = bf16[4,112,768]{2,1,0:T(8,128)(2,1)} collective-permute-done((bf16[4,112,768]{2,1,0:T(8,128)(2,1)}, bf16[4,112,768]{2,1,0:T(8,128)(2,1)}, u32[]{:S(2)}, u32[]{:S(2)}) %collective-permute-start.30) | collective-permute-done | bytes 688160 | tf_op jit(solution)/shard_map/ppermute | solution.py:579
  381.3 3.5 shard_map.222
  384.8 1.4 collective-permute-start.35
  386.3 2.4 collective-permute-done.35
  388.8 1.4 collective-permute-start.36
  390.3 3.3 collective-permute-done.36
  393.6 2.1 collective-permute-start.37
  395.8 7.6 %collective-permute-done.37 = bf16[16,2304]{1,0:T(8,128)(2,1)S(1)} collective-permute-done((bf16[16,2304]{1,0:T(8,128)(2,1)S(1)}, bf16[16,2304]{1,0:T(8,128)(2,1)S(1)}, u32[]{:S(2)}, u32[]{:S(2)}) %collective-permute-start.37) | collective-permute-done | bytes 73760 | tf_op jit(solution)/shard_map/ppermute | solution.py:692
  404.1 0.9 pad_maximum_fusion.1
  404.9 0.9 pad_maximum_fusion
  405.8 13.0 %reduce-scatter.8.cloned.1.call-done = bf16[1,224,768]{2,1,0:T(8,128)(2,1)} async-done(((bf16[4,224,768]{2,1,0:T(8,128)(2,1)}), bf16[1,224,768]{2,1,0:T(8,128)(2,1)}) %reduce-scatter.8.cloned.1.call-update) | async-done | bytes 344080 | tf_op jit(solution)/shard_map/reduce_scatter | solution.py:753
  418.7 1.0 slice_convert_fusion.1
  422.6 0.8 pad_maximum_fusion.2
  (223 shorter events, 19.9 us)
Async XLA Ops:
  7.2 2.9 copy-start.22
  7.2 3.0 copy-start.25
  7.2 3.0 copy-start.24
  7.2 3.0 copy-start.17
  7.2 3.8 copy-start.21
  7.2 44.7 %all-gather.6.cloned.1.call-start = ((), (), s32[]{:S(2)}) async-start(), calls=%async_computation.6 | async-start | bytes 1474560 | tf_op jit(solution)/shard_map/all_gather | solution.py:620
  8.3 2.8 copy-start.15
  10.1 162.9 %all-gather.8.cloned.1.call-start = ((), (), s32[]{:S(2)}) async-start(), calls=%async_computation.7 | async-start | bytes 15409152 | tf_op jit(solution)/shard_map/all_gather | solution.py:711
  11.2 26.4 %copy-start.5 = (bf16[304,768]{1,0:T(8,128)(2,1)}, bf16[304,768]{1,0:T(8,128)(2,1)S(1)}, u32[]{:S(2)}) copy-start(bf16[304,768]{1,0:T(8,128)(2,1)S(1)} %bitcast_dynamic-update-slice_fusion.1) | copy-start | bytes 1400836
  37.5 56.1 %copy-start.6 = (bf16[448,768]{1,0:T(8,128)(2,1)}, bf16[448,768]{1,0:T(8,128)(2,1)S(1)}, u32[]{:S(2)}) copy-start(bf16[448,768]{1,0:T(8,128)(2,1)S(1)} %all-gather) | copy-start | bytes 2064388
  37.6 281.4 %reduce-scatter.4.cloned.1.call-start = ((), (), s32[]{:S(2)}) async-start(), calls=%async_computation.3 | async-start | bytes 9732096 | tf_op jit(solution)/shard_map/reduce_scatter | solution.py:720
  37.6 13.3 %collective-permute-start = (bf16[4,112,768]{2,1,0:T(8,128)(2,1)S(1)}, bf16[4,112,768]{2,1,0:T(8,128)(2,1)}, u32[]{:S(2)}, u32[]{:S(2)}) collective-permute-start(bf16[4,112,768]{2,1,0:T(8,128)(2,1)S(1)} %bitcast.122), channel_id=1, source_target_pairs={{0,4},{4,0},{1,5},{5,1},{2,6},{6,2},{3,7},{7,3},{8,12},{12,8},{9,1... | collective-permute-start | bytes 2064392 | tf_op jit(solution)/shard_map/ppermute | solution.py:579
  39.2 12.8 %collective-permute-start.1 = (bf16[4,112,768]{2,1,0:T(8,128)(2,1)S(1)}, bf16[4,112,768]{2,1,0:T(8,128)(2,1)}, u32[]{:S(2)}, u32[]{:S(2)}) collective-permute-start(bf16[4,112,768]{2,1,0:T(8,128)(2,1)S(1)} %bitcast.123), channel_id=1, source_target_pairs={{0,2},{2,0},{1,3},{3,1},{4,6},{6,4},{5,7},{7,5},{8,10},{10,8},{9,1... | collective-permute-start | bytes 2064392 | tf_op jit(solution)/shard_map/ppermute | solution.py:579
  52.0 41.0 %collective-permute-start.10 = (bf16[4,192,768]{2,1,0:T(8,128)(2,1)}, bf16[4,192,768]{2,1,0:T(8,128)(2,1)S(1)}, u32[]{:S(2)}, u32[]{:S(2)}) collective-permute-start(bf16[4,192,768]{2,1,0:T(8,128)(2,1)} %bitcast.148), channel_id=1, source_target_pairs={{0,2},{2,0},{1,3},{3,1},{4,6},{6,4},{5,7},{7,5},{8,10},{10,8},{9,1... | collective-permute-start | bytes 3538952 | tf_op jit(solution)/shard_map/ppermute | solution.py:579
  53.5 39.9 %collective-permute-start.9 = (bf16[4,192,768]{2,1,0:T(8,128)(2,1)}, bf16[4,192,768]{2,1,0:T(8,128)(2,1)S(1)}, u32[]{:S(2)}, u32[]{:S(2)}) collective-permute-start(bf16[4,192,768]{2,1,0:T(8,128)(2,1)} %bitcast.149), channel_id=1, source_target_pairs={{0,4},{4,0},{1,5},{5,1},{2,6},{6,2},{3,7},{7,3},{8,12},{12,8},{9,1... | collective-permute-start | bytes 3538952 | tf_op jit(solution)/shard_map/ppermute | solution.py:579
  53.8 40.7 %collective-permute-start.4 = (bf16[4,112,768]{2,1,0:T(8,128)(2,1)S(1)}, bf16[4,112,768]{2,1,0:T(8,128)(2,1)S(1)}, u32[]{:S(2)}, u32[]{:S(2)}) collective-permute-start(bf16[4,112,768]{2,1,0:T(8,128)(2,1)S(1)} %bitcast.124), channel_id=1, source_target_pairs={{0,1},{1,0},{2,3},{3,2},{4,5},{5,4},{6,7},{7,6},{8,9},{9,8},{10,11... | collective-permute-start | bytes 2064392 | tf_op jit(solution)/shard_map/ppermute | solution.py:579
  54.8 38.1 %collective-permute-start.2 = (bf16[2,112,768]{2,1,0:T(8,128)(2,1)S(1)}, bf16[2,112,768]{2,1,0:T(8,128)(2,1)S(1)}, u32[]{:S(2)}, u32[]{:S(2)}) collective-permute-start(bf16[2,112,768]{2,1,0:T(8,128)(2,1)S(1)} %slice.402), channel_id=1, source_target_pairs={{0,2},{2,0},{1,3},{3,1},{4,6},{6,4},{5,7},{7,5},{8,10},{10,8},{9,1... | collective-permute-start | bytes 1032200 | tf_op jit(solution)/shard_map/ppermute | solution.py:579
  56.7 42.3 %copy-start.23 = (s32[1,512]{1,0:T(1,128)S(1)}, s32[1,512]{1,0:T(1,128)}, u32[]{:S(2)}) copy-start(s32[1,512]{1,0:T(1,128)} %refs_4_.3) | copy-start | bytes 6148
  56.7 40.2 %collective-permute-start.3 = (bf16[2,112,768]{2,1,0:T(8,128)(2,1)S(1)}, bf16[2,112,768]{2,1,0:T(8,128)(2,1)}, u32[]{:S(2)}, u32[]{:S(2)}) collective-permute-start(bf16[2,112,768]{2,1,0:T(8,128)(2,1)S(1)} %slice.403), channel_id=1, source_target_pairs={{0,4},{4,0},{1,5},{5,1},{2,6},{6,2},{3,7},{7,3},{8,12},{12,8},{9,1... | collective-permute-start | bytes 1032200 | tf_op jit(solution)/shard_map/ppermute | solution.py:579
  92.9 9.0 %copy-start.34 = (bf16[2,112,768]{2,1,0:T(8,128)(2,1)}, bf16[2,112,768]{2,1,0:T(8,128)(2,1)S(1)}, u32[]{:S(2)}) copy-start(bf16[2,112,768]{2,1,0:T(8,128)(2,1)S(1)} %collective-permute-done.2.refs_7_) | copy-start | bytes 1032196
  92.9 5.3 %collective-permute-start.7 = (bf16[2,112,768]{2,1,0:T(8,128)(2,1)S(1)}, bf16[2,112,768]{2,1,0:T(8,128)(2,1)S(1)}, u32[]{:S(2)}, u32[]{:S(2)}) collective-permute-start(bf16[2,112,768]{2,1,0:T(8,128)(2,1)S(1)} %collective-permute-done.2.refs_7_), channel_id=1, source_target_pairs={{0,1},{1,0},{2,3},{3,2},{4,5},{5,4},{6,7},{7,6},{8,9},{9,8},{10,11... | collective-permute-start | bytes 1032200 | tf_op jit(solution)/shard_map/ppermute | solution.py:579
  92.9 9.0 %copy-start.13 = (bf16[4,192,768]{2,1,0:T(8,128)(2,1)}, bf16[4,192,768]{2,1,0:T(8,128)(2,1)S(1)}, u32[]{:S(2)}) copy-start(bf16[4,192,768]{2,1,0:T(8,128)(2,1)S(1)} %collective-permute-done.10.refs_9_.refs_8_) | copy-start | bytes 3538948
  93.0 7.6 %collective-permute-start.5 = (bf16[4,112,768]{2,1,0:T(8,128)(2,1)}, bf16[4,112,768]{2,1,0:T(8,128)(2,1)}, u32[]{:S(2)}, u32[]{:S(2)}) collective-permute-start(bf16[4,112,768]{2,1,0:T(8,128)(2,1)} %collective-permute-done.refs_5_), channel_id=1, source_target_pairs={{0,1},{1,0},{2,3},{3,2},{4,5},{5,4},{6,7},{7,6},{8,9},{9,8},{10,11... | collective-permute-start | bytes 2064392 | tf_op jit(solution)/shard_map/ppermute | solution.py:579
  93.5 7.1 %collective-permute-start.6 = (bf16[4,112,768]{2,1,0:T(8,128)(2,1)}, bf16[4,112,768]{2,1,0:T(8,128)(2,1)}, u32[]{:S(2)}, u32[]{:S(2)}) collective-permute-start(bf16[4,112,768]{2,1,0:T(8,128)(2,1)} %collective-permute-done.1.refs_6_), channel_id=1, source_target_pairs={{0,1},{1,0},{2,3},{3,2},{4,5},{5,4},{6,7},{7,6},{8,9},{9,8},{10,11... | collective-permute-start | bytes 2064392 | tf_op jit(solution)/shard_map/ppermute | solution.py:579
  94.5 3.9 copy-start.30
  94.5 19.4 %collective-permute-start.11 = (bf16[2,192,768]{2,1,0:T(8,128)(2,1)S(1)}, bf16[2,192,768]{2,1,0:T(8,128)(2,1)}, u32[]{:S(2)}, u32[]{:S(2)}) collective-permute-start(bf16[2,192,768]{2,1,0:T(8,128)(2,1)S(1)} %slice.404), channel_id=1, source_target_pairs={{0,2},{2,0},{1,3},{3,1},{4,6},{6,4},{5,7},{7,5},{8,10},{10,8},{9,1... | collective-permute-start | bytes 1769480 | tf_op jit(solution)/shard_map/ppermute | solution.py:579
  97.0 16.9 %collective-permute-start.12 = (bf16[2,192,768]{2,1,0:T(8,128)(2,1)S(1)}, bf16[2,192,768]{2,1,0:T(8,128)(2,1)}, u32[]{:S(2)}, u32[]{:S(2)}) collective-permute-start(bf16[2,192,768]{2,1,0:T(8,128)(2,1)S(1)} %slice.405), channel_id=1, source_target_pairs={{0,4},{4,0},{1,5},{5,1},{2,6},{6,2},{3,7},{7,3},{8,12},{12,8},{9,1... | collective-permute-start | bytes 1769480 | tf_op jit(solution)/shard_map/ppermute | solution.py:579
  98.3 2.3 collective-permute-start.8
  100.5 13.8 %copy-start.36 = (bf16[2,112,768]{2,1,0:T(8,128)(2,1)}, bf16[2,112,768]{2,1,0:T(8,128)(2,1)S(1)}, u32[]{:S(2)}) copy-start(bf16[2,112,768]{2,1,0:T(8,128)(2,1)S(1)} %collective-permute-done.8.refs_13_) | copy-start | bytes 1032196
  100.5 29.1 %collective-permute-start.13 = (bf16[4,192,768]{2,1,0:T(8,128)(2,1)}, bf16[4,192,768]{2,1,0:T(8,128)(2,1)}, u32[]{:S(2)}, u32[]{:S(2)}) collective-permute-start(bf16[4,192,768]{2,1,0:T(8,128)(2,1)} %bitcast.150), channel_id=1, source_target_pairs={{0,1},{1,0},{2,3},{3,2},{4,5},{5,4},{6,7},{7,6},{8,9},{9,8},{10,11... | collective-permute-start | bytes 3538952 | tf_op jit(solution)/shard_map/ppermute | solution.py:579
  101.4 28.3 %collective-permute-start.14 = (bf16[4,192,768]{2,1,0:T(8,128)(2,1)}, bf16[4,192,768]{2,1,0:T(8,128)(2,1)S(1)}, u32[]{:S(2)}, u32[]{:S(2)}) collective-permute-start(bf16[4,192,768]{2,1,0:T(8,128)(2,1)} %copy-done.14), channel_id=1, source_target_pairs={{0,1},{1,0},{2,3},{3,2},{4,5},{5,4},{6,7},{7,6},{8,9},{9,8},{10,11... | collective-permute-start | bytes 3538952 | tf_op jit(solution)/shard_map/ppermute | solution.py:579
  101.9 27.8 %collective-permute-start.15 = (bf16[4,192,768]{2,1,0:T(8,128)(2,1)S(1)}, bf16[4,192,768]{2,1,0:T(8,128)(2,1)S(1)}, u32[]{:S(2)}, u32[]{:S(2)}) collective-permute-start(bf16[4,192,768]{2,1,0:T(8,128)(2,1)S(1)} %collective-permute-done.10.refs_9_.refs_8_), channel_id=1, source_target_pairs={{0,1},{1,0},{2,3},{3,2},{4,5},{5,4},{6,7},{7,6},{8,9},{9,8},{10,11... | collective-permute-start | bytes 3538952 | tf_op jit(solution)/shard_map/ppermute | solution.py:579
  113.9 15.8 %collective-permute-start.16 = (bf16[2,192,768]{2,1,0:T(8,128)(2,1)}, bf16[2,192,768]{2,1,0:T(8,128)(2,1)S(1)}, u32[]{:S(2)}, u32[]{:S(2)}) collective-permute-start(bf16[2,192,768]{2,1,0:T(8,128)(2,1)} %collective-permute-done.11.refs_10_.refs_9_), channel_id=1, source_target_pairs={{0,1},{1,0},{2,3},{3,2},{4,5},{5,4},{6,7},{7,6},{8,9},{9,8},{10,11... | collective-permute-start | bytes 1769480 | tf_op jit(solution)/shard_map/ppermute | solution.py:579
  113.9 15.8 %collective-permute-start.17 = (bf16[2,192,768]{2,1,0:T(8,128)(2,1)}, bf16[2,192,768]{2,1,0:T(8,128)(2,1)S(1)}, u32[]{:S(2)}, u32[]{:S(2)}) collective-permute-start(bf16[2,192,768]{2,1,0:T(8,128)(2,1)} %collective-permute-done.12.refs_11_.refs_10_), channel_id=1, source_target_pairs={{0,1},{1,0},{2,3},{3,2},{4,5},{5,4},{6,7},{7,6},{8,9},{9,8},{10,11... | collective-permute-start | bytes 1769480 | tf_op jit(solution)/shard_map/ppermute | solution.py:579
  170.6 195.7 %reduce-scatter.6.cloned.1.call-start = ((), (), s32[]{:S(2)}) async-start(), calls=%async_computation.4 | async-start | bytes 1474560 | tf_op jit(solution)/shard_map/reduce_scatter | solution.py:659
  227.8 22.6 %collective-permute-start.18 = (bf16[4,4,192,768]{3,2,1,0:T(8,128)(2,1)}, bf16[4,4,192,768]{3,2,1,0:T(8,128)(2,1)S(1)}, u32[]{:S(2)}, u32[]{:S(2)}) collective-permute-start(bf16[4,4,192,768]{3,2,1,0:T(8,128)(2,1)} %get-tuple-element.243), channel_id=1, source_target_pairs={{0,1},{1,0},{2,3},{3,2},{4,5},{5,4},{6,7},{7,6},{8,9},{9,8},{10,11... | collective-permute-start | bytes 14155784 | tf_op jit(solution)/shard_map/ppermute | solution.py:579
  250.3 11.4 %collective-permute-start.19 = (bf16[4,4,112,768]{3,2,1,0:T(8,128)(2,1)}, bf16[4,4,112,768]{3,2,1,0:T(8,128)(2,1)S(1)}, u32[]{:S(2)}, u32[]{:S(2)}) collective-permute-start(bf16[4,4,112,768]{3,2,1,0:T(8,128)(2,1)} %get-tuple-element.254), channel_id=1, source_target_pairs={{0,1},{1,0},{2,3},{3,2},{4,5},{5,4},{6,7},{7,6},{8,9},{9,8},{10,11... | collective-permute-start | bytes 8257544 | tf_op jit(solution)/shard_map/ppermute | solution.py:579
  258.8 23.3 %collective-permute-start.20 = (bf16[2,192,768]{2,1,0:T(8,128)(2,1)}, bf16[2,192,768]{2,1,0:T(8,128)(2,1)S(1)}, u32[]{:S(2)}, u32[]{:S(2)}) collective-permute-start(bf16[2,192,768]{2,1,0:T(8,128)(2,1)} %get-tuple-element.251), channel_id=1, source_target_pairs={{0,2},{2,0},{1,3},{3,1},{4,6},{6,4},{5,7},{7,5},{8,10},{10,8},{9,1... | collective-permute-start | bytes 1769480 | tf_op jit(solution)/shard_map/ppermute | solution.py:579
  260.3 21.8 %collective-permute-start.21 = (bf16[2,192,768]{2,1,0:T(8,128)(2,1)}, bf16[2,192,768]{2,1,0:T(8,128)(2,1)S(1)}, u32[]{:S(2)}, u32[]{:S(2)}) collective-permute-start(bf16[2,192,768]{2,1,0:T(8,128)(2,1)} %get-tuple-element.252), channel_id=1, source_target_pairs={{0,4},{4,0},{1,5},{5,1},{2,6},{6,2},{3,7},{7,3},{8,12},{12,8},{9,1... | collective-permute-start | bytes 1769480 | tf_op jit(solution)/shard_map/ppermute | solution.py:579
  267.5 18.7 %collective-permute-start.22 = (bf16[2,112,768]{2,1,0:T(8,128)(2,1)}, bf16[2,112,768]{2,1,0:T(8,128)(2,1)S(1)}, u32[]{:S(2)}, u32[]{:S(2)}) collective-permute-start(bf16[2,112,768]{2,1,0:T(8,128)(2,1)} %get-tuple-element.258), channel_id=1, source_target_pairs={{0,2},{2,0},{1,3},{3,1},{4,6},{6,4},{5,7},{7,5},{8,10},{10,8},{9,1... | collective-permute-start | bytes 1032200 | tf_op jit(solution)/shard_map/ppermute | solution.py:579
  267.9 23.7 %collective-permute-start.23 = (bf16[2,112,768]{2,1,0:T(8,128)(2,1)}, bf16[2,112,768]{2,1,0:T(8,128)(2,1)S(1)}, u32[]{:S(2)}, u32[]{:S(2)}) collective-permute-start(bf16[2,112,768]{2,1,0:T(8,128)(2,1)} %get-tuple-element.259), channel_id=1, source_target_pairs={{0,4},{4,0},{1,5},{5,1},{2,6},{6,2},{3,7},{7,3},{8,12},{12,8},{9,1... | collective-permute-start | bytes 1032200 | tf_op jit(solution)/shard_map/ppermute | solution.py:579
  268.6 23.0 %copy-start.1 = (bf16[4,192,768]{2,1,0:T(8,128)(2,1)S(1)}, bf16[4,192,768]{2,1,0:T(8,128)(2,1)}, u32[]{:S(2)}) copy-start(bf16[4,192,768]{2,1,0:T(8,128)(2,1)} %get-tuple-element.273) | copy-start | bytes 3538948
  282.1 9.6 %copy-start = (bf16[4,192,768]{2,1,0:T(8,128)(2,1)S(1)}, bf16[4,192,768]{2,1,0:T(8,128)(2,1)}, u32[]{:S(2)}) copy-start(bf16[4,192,768]{2,1,0:T(8,128)(2,1)} %get-tuple-element.271) | copy-start | bytes 3538948
  286.2 5.6 %copy-start.7 = (bf16[2,112,768]{2,1,0:T(8,128)(2,1)}, bf16[2,112,768]{2,1,0:T(8,128)(2,1)S(1)}, u32[]{:S(2)}) copy-start(bf16[2,112,768]{2,1,0:T(8,128)(2,1)S(1)} %collective-permute-done.22) | copy-start | bytes 1032196
  292.7 29.4 %collective-permute-start.25 = (bf16[4,192,768]{2,1,0:T(8,128)(2,1)S(1)}, bf16[4,192,768]{2,1,0:T(8,128)(2,1)}, u32[]{:S(2)}, u32[]{:S(2)}) collective-permute-start(bf16[4,192,768]{2,1,0:T(8,128)(2,1)S(1)} %add_dynamic-update-slice_fusion), channel_id=1, source_target_pairs={{0,2},{2,0},{1,3},{3,1},{4,6},{6,4},{5,7},{7,5},{8,10},{10,8},{9,1... | collective-permute-start | bytes 3538952 | tf_op jit(solution)/shard_map/ppermute | solution.py:579
  293.5 29.1 %collective-permute-start.24 = (bf16[4,192,768]{2,1,0:T(8,128)(2,1)S(1)}, bf16[4,192,768]{2,1,0:T(8,128)(2,1)}, u32[]{:S(2)}, u32[]{:S(2)}) collective-permute-start(bf16[4,192,768]{2,1,0:T(8,128)(2,1)S(1)} %add_dynamic-update-slice_fusion.1), channel_id=1, source_target_pairs={{0,4},{4,0},{1,5},{5,1},{2,6},{6,2},{3,7},{7,3},{8,12},{12,8},{9,1... | collective-permute-start | bytes 3538952 | tf_op jit(solution)/shard_map/ppermute | solution.py:579
  294.9 27.7 %copy-start.2 = (bf16[4,192,768]{2,1,0:T(8,128)(2,1)S(1)}, bf16[4,192,768]{2,1,0:T(8,128)(2,1)}, u32[]{:S(2)}) copy-start(bf16[4,192,768]{2,1,0:T(8,128)(2,1)} %get-tuple-element.309) | copy-start | bytes 3538948
  322.6 5.4 %collective-permute-start.26 = (bf16[4,4,112,768]{3,2,1,0:T(8,128)(2,1)}, bf16[4,4,112,768]{3,2,1,0:T(8,128)(2,1)}, u32[]{:S(2)}, u32[]{:S(2)}) collective-permute-start(bf16[4,4,112,768]{3,2,1,0:T(8,128)(2,1)} %get-tuple-element.296), channel_id=1, source_target_pairs={{0,1},{1,0},{2,3},{3,2},{4,5},{5,4},{6,7},{7,6},{8,9},{9,8},{10,11... | collective-permute-start | bytes 8257544 | tf_op jit(solution)/shard_map/ppermute | solution.py:579
  322.6 3.0 copy-start.19
  325.6 93.2 %reduce-scatter.8.cloned.1.call-start = ((), (), s32[]{:S(2)}) async-start(), calls=%async_computation.5 | async-start | bytes 1720320 | tf_op jit(solution)/shard_map/reduce_scatter | solution.py:753
  332.3 32.4 %copy-start.20 = (bf16[4,112,768]{2,1,0:T(8,128)(2,1)S(1)}, bf16[4,112,768]{2,1,0:T(8,128)(2,1)}, u32[]{:S(2)}) copy-start(bf16[4,112,768]{2,1,0:T(8,128)(2,1)} %get-tuple-element.304) | copy-start | bytes 2064388
  335.9 4.3 collective-permute-start.33
  336.1 30.2 %collective-permute-start.32 = (bf16[4,112,768]{2,1,0:T(8,128)(2,1)S(1)}, bf16[4,112,768]{2,1,0:T(8,128)(2,1)S(1)}, u32[]{:S(2)}, u32[]{:S(2)}) collective-permute-start(bf16[4,112,768]{2,1,0:T(8,128)(2,1)S(1)} %add_dynamic-update-slice_fusion.4), channel_id=1, source_target_pairs={{0,2},{2,0},{1,3},{3,1},{4,6},{6,4},{5,7},{7,5},{8,10},{10,8},{9,1... | collective-permute-start | bytes 2064392 | tf_op jit(solution)/shard_map/ppermute | solution.py:579
  337.6 28.7 %collective-permute-start.31 = (bf16[4,112,768]{2,1,0:T(8,128)(2,1)S(1)}, bf16[4,112,768]{2,1,0:T(8,128)(2,1)}, u32[]{:S(2)}, u32[]{:S(2)}) collective-permute-start(bf16[4,112,768]{2,1,0:T(8,128)(2,1)S(1)} %add_dynamic-update-slice_fusion.5), channel_id=1, source_target_pairs={{0,4},{4,0},{1,5},{5,1},{2,6},{6,2},{3,7},{7,3},{8,12},{12,8},{9,1... | collective-permute-start | bytes 2064392 | tf_op jit(solution)/shard_map/ppermute | solution.py:579
  338.9 23.4 %collective-permute-start.29 = (bf16[2,112,768]{2,1,0:T(8,128)(2,1)}, bf16[2,112,768]{2,1,0:T(8,128)(2,1)S(1)}, u32[]{:S(2)}, u32[]{:S(2)}) collective-permute-start(bf16[2,112,768]{2,1,0:T(8,128)(2,1)} %get-tuple-element.307), channel_id=1, source_target_pairs={{0,4},{4,0},{1,5},{5,1},{2,6},{6,2},{3,7},{7,3},{8,12},{12,8},{9,1... | collective-permute-start | bytes 1032200 | tf_op jit(solution)/shard_map/ppermute | solution.py:579
  339.6 25.1 %collective-permute-start.27 = (bf16[2,112,768]{2,1,0:T(8,128)(2,1)}, bf16[2,112,768]{2,1,0:T(8,128)(2,1)S(1)}, u32[]{:S(2)}, u32[]{:S(2)}) collective-permute-start(bf16[2,112,768]{2,1,0:T(8,128)(2,1)} %get-tuple-element.305), channel_id=1, source_target_pairs={{0,2},{2,0},{1,3},{3,1},{4,6},{6,4},{5,7},{7,5},{8,10},{10,8},{9,1... | collective-permute-start | bytes 1032200 | tf_op jit(solution)/shard_map/ppermute | solution.py:579
  340.3 25.9 %collective-permute-start.34 = (bf16[2,3072]{1,0:T(2,128)(2,1)S(1)}, bf16[2,3072]{1,0:T(2,128)(2,1)S(1)}, u32[]{:S(2)}, u32[]{:S(2)}) collective-permute-start(bf16[2,3072]{1,0:T(2,128)(2,1)S(1)} %pad_maximum_fusion.14), channel_id=1, source_target_pairs={{0,2},{2,0},{1,3},{3,1},{4,6},{6,4},{5,7},{7,5},{8,10},{10,8},{9,1... | collective-permute-start | bytes 36872 | tf_op jit(solution)/shard_map/ppermute | solution.py:579
  364.2 16.9 %collective-permute-start.30 = (bf16[4,112,768]{2,1,0:T(8,128)(2,1)}, bf16[4,112,768]{2,1,0:T(8,128)(2,1)}, u32[]{:S(2)}, u32[]{:S(2)}) collective-permute-start(bf16[4,112,768]{2,1,0:T(8,128)(2,1)} %add_dynamic-update-slice_fusion.2), channel_id=1, source_target_pairs={{0,2},{2,0},{1,3},{3,1},{4,6},{6,4},{5,7},{7,5},{8,10},{10,8},{9,1... | collective-permute-start | bytes 2064392 | tf_op jit(solution)/shard_map/ppermute | solution.py:579
  364.8 16.5 %collective-permute-start.28 = (bf16[4,112,768]{2,1,0:T(8,128)(2,1)S(1)}, bf16[4,112,768]{2,1,0:T(8,128)(2,1)}, u32[]{:S(2)}, u32[]{:S(2)}) collective-permute-start(bf16[4,112,768]{2,1,0:T(8,128)(2,1)S(1)} %add_dynamic-update-slice_fusion.3), channel_id=1, source_target_pairs={{0,4},{4,0},{1,5},{5,1},{2,6},{6,2},{3,7},{7,3},{8,12},{12,8},{9,1... | collective-permute-start | bytes 2064392 | tf_op jit(solution)/shard_map/ppermute | solution.py:579
  366.3 14.9 %copy-start.31 = (bf16[4,112,768]{2,1,0:T(8,128)(2,1)}, bf16[4,112,768]{2,1,0:T(8,128)(2,1)S(1)}, u32[]{:S(2)}) copy-start(bf16[4,112,768]{2,1,0:T(8,128)(2,1)S(1)} %collective-permute-done.32.refs_5_) | copy-start | bytes 2064388
  384.7 5.5 %copy-start.12 = (bf16[1,192,768]{2,1,0:T(8,128)(2,1)S(1)}, bf16[1,192,768]{2,1,0:T(8,128)(2,1)}, u32[]{:S(2)}) copy-start(bf16[1,192,768]{2,1,0:T(8,128)(2,1)} %reduce-scatter.6.cloned.1.call-done) | copy-start | bytes 884740
  384.8 3.8 collective-permute-start.35
  388.8 4.8 %collective-permute-start.36 = (bf16[8,2304]{1,0:T(8,128)(2,1)S(1)}, bf16[8,2304]{1,0:T(8,128)(2,1)S(1)}, u32[]{:S(2)}, u32[]{:S(2)}) collective-permute-start(bf16[8,2304]{1,0:T(8,128)(2,1)S(1)} %pad_maximum_fusion.8), channel_id=1, source_target_pairs={{0,8},{8,0},{16,24},{24,16},{1,9},{9,1},{17,25},{25,17},{2,10},{10... | collective-permute-start | bytes 110600 | tf_op jit(solution)/shard_map/ppermute | solution.py:692
  393.6 9.7 %collective-permute-start.37 = (bf16[16,2304]{1,0:T(8,128)(2,1)S(1)}, bf16[16,2304]{1,0:T(8,128)(2,1)S(1)}, u32[]{:S(2)}, u32[]{:S(2)}) collective-permute-start(bf16[16,2304]{1,0:T(8,128)(2,1)S(1)} %pad_maximum_fusion.7), channel_id=1, source_target_pairs={{0,16},{8,24},{16,0},{24,8},{1,17},{9,25},{17,1},{25,9},{2,18},{10... | collective-permute-start | bytes 221192 | tf_op jit(solution)/shard_map/ppermute | solution.py:692
  (16 other events, 20.3 us)
Sparse Core Ops, SparseCore 0:
  10.2 38.5 all-gather.5
  52.3 116.4 all-gather.7
  174.7 144.2 reduce-scatter.3
  325.7 30.1 reduce-scatter.5
  384.9 33.8 reduce-scatter.7
